TPU v7x, 32 devices: a whole 2x2x4 slice. The times are simulated.
32 devices in a mesh: dp: 8 (over y, x, core), mp: 4 (over z).
Axes of the slice: x: 2, y: 2, z: 4, core: 2. Of those that a mesh axis runs over, the one named last changes fastest.
Arguments:
- byte_input: bfloat16 [4, 128, 8192], P(None, 'dp'), may hold values from -6 to 6
- seq_lengths: int32 [4, 3], replicated, may hold values from 9 to 80, as said below
- patch_weight: bfloat16 [8, 1024, 1024], P('mp'), may hold values from -0.0625 to 0.0625
- norm_in_gain: float32 [1024], replicated, may hold values from 0.5 to 1.5
- in_weight: bfloat16 [4, 1024, 1288], P('mp'), may hold values from -0.1875 to 0.1875
- conv_weight: float32 [4, 768, 4], P('mp'), may hold values from -3 to 3
- conv_bias: float32 [4, 768], P('mp'), may hold values from -3 to 3
- step_bias: float32 [4, 8], P('mp'), may hold values from -3 to 0.5
- log_decay: float32 [4, 8], P('mp'), may hold values from -4.5 to 0
- skip_gain: float32 [4, 8], P('mp'), may hold values from 0.5 to 1.5
- group_gain: float32 [4, 512], P('mp'), may hold values from 0.5 to 1.5
- out_weight: bfloat16 [4, 512, 1024], P('mp'), may hold values from -0.125 to 0.125
- attn_gain: float32 [1024], replicated, may hold values from 0.5 to 1.5
- qkv_weight: bfloat16 [3, 1024, 1024], P(None, None, 'mp'), may hold values from -0.1875 to 0.1875
- attn_out_weight: bfloat16 [1024, 1024], P('mp'), may hold values from -0.375 to 0.375
- ffn_gain: float32 [1024], replicated, may hold values from 0.5 to 1.5
- ffn_weight: bfloat16 [3, 1024, 4096], P(None, 'mp', 'dp'), may hold values from -0.1875 to 0.1875
- out_grad: bfloat16 [4, 1024, 1024], P(None, 'dp'), may hold values from -6 to 6
Outputs:
- block_out: bfloat16 [4, 1024, 1024], P(None, 'dp', 'mp')
- input_grad: float32 [4, 128, 8192], P(None, 'dp', 'mp')
- grad_patch_weight: float32 [8, 1024, 1024], P('mp', 'dp')
- grad_norm_in_gain: float32 [1024], P('dp')
- grad_in_weight: float32 [4, 1024, 1288], P('mp', 'dp')
- grad_conv_weight: float32 [4, 768, 4], P('mp', 'dp')
- grad_conv_bias: float32 [4, 768], P('mp', 'dp')
- grad_step_bias: float32 [4, 8], P('mp')
- grad_log_decay: float32 [4, 8], P('mp')
- grad_skip_gain: float32 [4, 8], P('mp')
- grad_group_gain: float32 [4, 512], P('mp', 'dp')
- grad_out_weight: float32 [4, 512, 1024], P('mp', 'dp')
- grad_attn_gain: float32 [1024], P('dp')
- grad_qkv_weight: float32 [3, 1024, 1024], P(None, 'dp', 'mp')
- grad_attn_out_weight: float32 [1024, 1024], P('mp', 'dp')
- grad_ffn_gain: float32 [1024], P('dp')
- grad_ffn_weight: float32 [3, 1024, 4096], P(None, 'mp', 'dp')
Inputs may be any that keep to these rules, and one draw needn't show every extreme that they name: `seq_lengths`: lengths count patches of 8 bytes; every length is at least 1. In each micro-batch the three sequences lie end to end from patch 0 in this order and are followed by 1 to 8 patches of padding; the first holds more than half of the 128 patches, the third 16 to 31. In some micro-batch the first holds exactly the maximum.
All inputs are finite; a program needn't handle non-finite values.
Results may differ from a plain program's by a relative error of at most 0.02.
Values may be sent and summed in bfloat16 or wider, within the bound.
A program may use at most 256 MiB of HBM per device.

v0:
```python
from functools import partial

import jax
import jax.numpy as jnp
from jax import lax
from jax.sharding import PartitionSpec as P

STATE = 128
CONV = 4
SEQS = 3
GROUP_WIDTH = 512
GROUP_HEADS = 8
HEAD_DIM = 64
ATT_DIM = 64
CONV_CH = 768


norm_eps = 1e-06
highest = lax.Precision.HIGHEST
large_negative = -1e30


def entering(array, axis, combine, identity, reverse):
    size, place = (lax.axis_size(axis), lax.axis_index(axis))
    everything = jax.tree.map(lambda part: lax.all_gather(part, axis), array)
    start = jax.tree.map(
        lambda part, zero: jnp.broadcast_to(jnp.asarray(zero, part.dtype), part.shape),
        array,
        identity,
    )

    def turn(k, before):
        at = size - 1 - k if reverse else k
        reached = at > place if reverse else at < place
        new = combine(before, jax.tree.map(lambda part: part[at], everything))
        return jax.tree.map(lambda a, b: jnp.where(reached, a, b), new, before)

    return lax.fori_loop(0, size, turn, start)


def passed_along(block, axis, distance):
    devices = range(lax.axis_size(axis))
    route = [(i - distance, i) for i in devices if i - distance in devices]
    return lax.ppermute(block, axis, route)


def rms_scale(values, scale_gain):
    return (
        values
        * lax.rsqrt(jnp.mean(values * values, axis=-1, keepdims=True) + norm_eps)
        * scale_gain
    )


def norm_grad(values, scale_gain, upstream):
    primal_out, pull_back = jax.vjp(rms_scale, values, scale_gain)
    return pull_back(upstream)


def segment_ids(seq_lengths, first_patch, patch_count):
    seq_ends = jnp.cumsum(seq_lengths)
    places = first_patch + jnp.arange(patch_count, dtype=jnp.int32)
    return jnp.sum((places[:, None] >= seq_ends[None, :]).astype(jnp.int32), axis=1)


def block_terms(values, inputs, outputs, step_sizes, log_decays, segment, previous):
    running = jnp.cumsum(log_decays, axis=0)
    block_len = segment.shape[0]
    ordinal = jnp.arange(block_len)
    same_seg = (segment[:, None] == segment[None, :]) & (ordinal[None, :] <= ordinal[:, None])
    log_gap = running[:, None] - running[None, :]
    pair_mask = same_seg[:, :, None, None]
    decays = jnp.where(pair_mask, jnp.exp(jnp.where(pair_mask, log_gap, 0.0)), 0.0)
    inner_prod = jnp.einsum("tgn,sgn->tsg", outputs, inputs, precision=highest)
    weights = decays * inner_prod[:, :, :, None] * step_sizes[None]
    within = jnp.einsum("tsgh,sghe->tghe", weights, values, precision=highest)
    carry_weight = jnp.exp(running) * (segment == previous).astype(jnp.float32)[:, None, None]
    last_seg = segment[block_len - 1]
    to_end = (
        jnp.exp(running[block_len - 1][None] - running)
        * (segment == last_seg).astype(jnp.float32)[:, None, None]
        * step_sizes
    )
    local_state = jnp.einsum("sgh,sghe,sgn->ghen", to_end, values, inputs, precision=highest)
    through = jnp.exp(running[block_len - 1]) * (last_seg == previous).astype(jnp.float32)
    return (within, carry_weight, local_state, through)


def join_carry(earlier, latter):
    return (earlier[0] * latter[0], latter[0][..., None, None] * earlier[1] + latter[1])


def carry_chain(decay_part, state_part, backward):
    identity_pair = (jnp.ones_like(decay_part), jnp.zeros_like(state_part))
    return entering((decay_part, state_part), "dp", join_carry, identity_pair, backward)


def rim_pass(tail_rows, offset):
    return passed_along(tail_rows, "dp", offset)


def head_sum(partial_sum):
    return lax.psum(partial_sum, "mp")


def gather_rows(features):
    return lax.all_gather(features, "dp", axis=0, tiled=True)


def spread_rows(terms):
    return lax.psum_scatter(terms, "dp", scatter_dimension=0, tiled=True)


def swiglu_grads(hidden_grad, gate_up):
    sigmoid_gate = jax.nn.sigmoid(gate_up[0])
    gate_grad = hidden_grad * gate_up[1] * sigmoid_gate * (1.0 + gate_up[0] * (1.0 - sigmoid_gate))
    up_grad = hidden_grad * gate_up[0] * sigmoid_gate
    return jnp.stack([gate_grad, up_grad]).astype(jnp.bfloat16)


def mixer_front(
    projected, tail_rows, conv_weight, conv_bias, step_bias, log_decay, segment, previous
):
    patches = projected.shape[0]
    groups_here = projected.shape[1]
    gate_part = projected[:, :, :GROUP_WIDTH]
    conv_in = jnp.concatenate(
        [tail_rows, projected[:, :, GROUP_WIDTH : GROUP_WIDTH + CONV_CH]], axis=0
    )
    seg_ext = jnp.concatenate([jnp.full((CONV - 1,), previous, jnp.int32), segment], axis=0)
    conv_out = conv_bias[None]
    for lag_index in range(CONV):
        keep_mask = (seg_ext[lag_index : lag_index + patches] == segment).astype(jnp.float32)[
            :, None, None
        ]
        conv_out = (
            conv_out
            + conv_in[lag_index : lag_index + patches]
            * keep_mask
            * conv_weight[:, :, lag_index][None]
        )
    activated = jax.nn.silu(conv_out)
    values = activated[:, :, :GROUP_WIDTH].reshape(patches, groups_here, GROUP_HEADS, HEAD_DIM)
    inputs = activated[:, :, GROUP_WIDTH : GROUP_WIDTH + STATE]
    outputs = activated[:, :, GROUP_WIDTH + STATE :]
    step_sizes = jax.nn.softplus(projected[:, :, GROUP_WIDTH + CONV_CH :] + step_bias[None])
    log_decays = -step_sizes * jnp.exp(log_decay)[None]
    within, carry_weight, local_state, through = block_terms(
        values, inputs, outputs, step_sizes, log_decays, segment, previous
    )
    return (gate_part, values, outputs, carry_weight, within, through, local_state)


def mixer_finish(gate_part, values, outputs, carry_weight, within, state_in, skip_gain, group_gain):
    carried = carry_weight[..., None] * jnp.einsum(
        "ghen,tgn->tghe", state_in, outputs, precision=highest
    )
    result = within + carried + skip_gain[None, :, :, None] * values
    patches = result.shape[0]
    gated_out = result.reshape(patches, result.shape[1], GROUP_WIDTH) * jax.nn.silu(gate_part)
    return rms_scale(gated_out, group_gain[None])


def body(
    byte_input,
    seq_lengths,
    patch_weight,
    norm_in_gain,
    in_weight,
    conv_weight,
    conv_bias,
    step_bias,
    log_decay,
    skip_gain,
    group_gain,
    out_weight,
    attn_gain,
    qkv_weight,
    attn_out_weight,
    ffn_gain,
    ffn_weight,
    out_grad,
):
    micro_count, patch_rows, input_cols = byte_input.shape
    model_dim = norm_in_gain.shape[0]
    patch_len = input_cols // model_dim
    byte_rows = patch_rows * patch_len
    part_cols = qkv_weight.shape[2]
    att_heads = part_cols // ATT_DIM
    my_bytes = patch_weight.shape[0]
    dp_size = lax.axis_size("dp")
    mp_index = lax.axis_index("mp")
    dp_index = lax.axis_index("dp")
    col_start = mp_index * part_cols
    input_start = mp_index * my_bytes * model_dim
    first_patch = dp_index * patch_rows
    patch_acc = jnp.zeros(patch_weight.shape, jnp.float32)
    in_acc = jnp.zeros(in_weight.shape, jnp.float32)
    conv_w_acc = jnp.zeros(conv_weight.shape, jnp.float32)
    conv_b_acc = jnp.zeros(conv_bias.shape, jnp.float32)
    step_acc = jnp.zeros(step_bias.shape, jnp.float32)
    decay_acc = jnp.zeros(log_decay.shape, jnp.float32)
    skip_acc = jnp.zeros(skip_gain.shape, jnp.float32)
    group_acc = jnp.zeros(group_gain.shape, jnp.float32)
    out_acc = jnp.zeros(out_weight.shape, jnp.float32)
    qkv_acc = jnp.zeros(qkv_weight.shape, jnp.float32)
    attn_acc = jnp.zeros(attn_out_weight.shape, jnp.float32)
    ffn_acc = jnp.zeros(ffn_weight.shape, jnp.float32)
    gain_in_acc = jnp.zeros((model_dim,), jnp.float32)
    gain_attn_acc = jnp.zeros((model_dim,), jnp.float32)
    gain_ffn_acc = jnp.zeros((model_dim,), jnp.float32)
    block_rows = []
    input_rows = []
    for micro_index in range(micro_count):
        stream_in = byte_input[micro_index]
        lengths_now = seq_lengths[micro_index]
        segment = segment_ids(lengths_now, first_patch, patch_rows)
        before = segment_ids(lengths_now, first_patch - 1, 1)[0]
        previous = jnp.where(first_patch > 0, before, -1)
        valid_rows = jnp.repeat((segment < SEQS).astype(jnp.float32), patch_len)[:, None]
        own_input = lax.dynamic_slice_in_dim(
            stream_in, input_start, my_bytes * model_dim, 1
        ).reshape(patch_rows, my_bytes, model_dim)
        global_in = head_sum(
            jnp.einsum("pkd,kde->pe", own_input, patch_weight, preferred_element_type=jnp.float32)
        )
        normed_in = rms_scale(global_in, norm_in_gain).astype(jnp.bfloat16)
        projected = jnp.einsum(
            "pd,gdc->pgc", normed_in, in_weight, preferred_element_type=jnp.float32
        )
        tail_keep = (segment[patch_rows - (CONV - 1) :] == segment[patch_rows - 1]).astype(
            jnp.float32
        )[:, None, None]
        tail_in = rim_pass(
            projected[patch_rows - (CONV - 1) :, :, GROUP_WIDTH : GROUP_WIDTH + CONV_CH]
            * tail_keep,
            1,
        )
        front_fn = partial(mixer_front, segment=segment, previous=previous)
        front_out, front_pull = jax.vjp(
            front_fn, projected, tail_in, conv_weight, conv_bias, step_bias, log_decay
        )
        state_in = carry_chain(front_out[5], front_out[6], False)[1]
        normed_mix, finish_pull = jax.vjp(
            mixer_finish,
            front_out[0],
            front_out[1],
            front_out[2],
            front_out[3],
            front_out[4],
            state_in,
            skip_gain,
            group_gain,
        )
        group_normed = normed_mix.astype(jnp.bfloat16)
        global_out = global_in + head_sum(
            jnp.einsum("pgc,gcd->pd", group_normed, out_weight, preferred_element_type=jnp.float32)
        )
        local_in = stream_in.astype(jnp.float32).reshape(byte_rows, model_dim) + jnp.repeat(
            global_out, patch_len, axis=0
        )
        attn_in = rms_scale(local_in, attn_gain).astype(jnp.bfloat16)
        qkv_all = jnp.einsum(
            "td,kde->kte", attn_in, qkv_weight, preferred_element_type=jnp.float32
        ).astype(jnp.bfloat16)
        shaped = qkv_all.reshape(3, patch_rows, patch_len, att_heads, ATT_DIM)
        scores = jnp.einsum(
            "pihe,pjhe->phij", shaped[0], shaped[1], preferred_element_type=jnp.float32
        ) * ATT_DIM ** (-0.5)
        causal = jnp.tril(jnp.ones((patch_len, patch_len), jnp.bool_))
        attn_probs = jax.nn.softmax(jnp.where(causal[None, None], scores, large_negative), axis=-1)
        probs_low = attn_probs.astype(jnp.bfloat16)
        heads_out = (
            jnp.einsum("phij,pjhe->pihe", probs_low, shaped[2], preferred_element_type=jnp.float32)
            .astype(jnp.bfloat16)
            .reshape(byte_rows, part_cols)
        )
        attn_branch = lax.psum(
            jnp.dot(heads_out, attn_out_weight, preferred_element_type=jnp.float32), "mp"
        )
        after_attn = local_in + attn_branch
        ffn_full = rms_scale(after_attn, ffn_gain).astype(jnp.bfloat16)
        own_cols = lax.dynamic_slice_in_dim(after_attn, col_start, part_cols, 1)
        ffn_in = lax.dynamic_slice_in_dim(ffn_full, col_start, part_cols, 1)
        ffn_rows_in = gather_rows(ffn_in)
        gate_up = lax.psum(
            jnp.einsum(
                "tc,kcf->ktf", ffn_rows_in, ffn_weight[:2], preferred_element_type=jnp.float32
            ),
            "mp",
        )
        hidden = (jax.nn.silu(gate_up[0]) * gate_up[1]).astype(jnp.bfloat16)
        down_part = jnp.einsum(
            "tf,cf->tc", hidden, ffn_weight[2], preferred_element_type=jnp.float32
        )
        ffn_out = spread_rows(down_part)
        block_rows.append(((own_cols + ffn_out) * valid_rows).astype(jnp.bfloat16))
        grad_full = out_grad[micro_index].astype(jnp.float32) * valid_rows
        own_grad = lax.dynamic_slice_in_dim(grad_full, col_start, part_cols, 1).astype(jnp.bfloat16)
        grad_rows = gather_rows(own_grad)
        down_grad = jnp.einsum("tc,tf->cf", grad_rows, hidden, preferred_element_type=jnp.float32)
        hidden_grad = lax.psum(
            jnp.einsum("tc,cf->tf", grad_rows, ffn_weight[2], preferred_element_type=jnp.float32),
            "mp",
        )
        gate_up_grad = swiglu_grads(hidden_grad, gate_up)
        in_grad_pair = jnp.einsum(
            "tc,ktf->kcf", ffn_rows_in, gate_up_grad, preferred_element_type=jnp.float32
        )
        ffn_acc = ffn_acc + jnp.concatenate([in_grad_pair, down_grad[None]], axis=0)
        ffn_in_grad = jnp.einsum(
            "ktf,kcf->tc", gate_up_grad, ffn_weight[:2], preferred_element_type=jnp.float32
        )
        ffn_in_grad = spread_rows(ffn_in_grad)
        ffn_in_full = lax.all_gather(ffn_in_grad, "mp", axis=1, tiled=True)
        after_norm_grad, ffn_gain_piece = norm_grad(after_attn, ffn_gain, ffn_in_full)
        gain_ffn_acc = gain_ffn_acc + ffn_gain_piece
        after_grad = grad_full + after_norm_grad
        branch_grad = after_grad.astype(jnp.bfloat16)
        attn_acc = attn_acc + jnp.einsum(
            "tc,td->cd", heads_out, branch_grad, preferred_element_type=jnp.float32
        )
        heads_grad = jnp.einsum(
            "td,cd->tc", branch_grad, attn_out_weight, preferred_element_type=jnp.float32
        ).reshape(patch_rows, patch_len, att_heads, ATT_DIM)
        probs_grad = jnp.einsum(
            "pihe,pjhe->phij", heads_grad, shaped[2].astype(jnp.float32), precision=highest
        )
        value_grad = jnp.einsum(
            "phij,pihe->pjhe", probs_low.astype(jnp.float32), heads_grad, precision=highest
        )
        score_grad = (
            attn_probs
            * (probs_grad - jnp.sum(attn_probs * probs_grad, axis=-1, keepdims=True))
            * ATT_DIM ** (-0.5)
        )
        query_grad = jnp.einsum(
            "phij,pjhe->pihe", score_grad, shaped[1].astype(jnp.float32), precision=highest
        )
        key_grad = jnp.einsum(
            "phij,pihe->pjhe", score_grad, shaped[0].astype(jnp.float32), precision=highest
        )
        qkv_grad = (
            jnp.stack([query_grad, key_grad, value_grad])
            .reshape(3, byte_rows, part_cols)
            .astype(jnp.bfloat16)
        )
        qkv_acc = qkv_acc + jnp.einsum(
            "td,kte->kde", attn_in, qkv_grad, preferred_element_type=jnp.float32
        )
        attn_in_grad = lax.psum(
            jnp.einsum("kte,kde->td", qkv_grad, qkv_weight, preferred_element_type=jnp.float32),
            "mp",
        )
        local_norm_grad, attn_gain_piece = norm_grad(local_in, attn_gain, attn_in_grad)
        gain_attn_acc = gain_attn_acc + attn_gain_piece
        local_grad = after_grad + local_norm_grad
        global_grad = jnp.sum(local_grad.reshape(patch_rows, patch_len, model_dim), axis=1)
        mixer_grad = global_grad.astype(jnp.bfloat16)
        out_acc = out_acc + jnp.einsum(
            "pgc,pd->gcd", group_normed, mixer_grad, preferred_element_type=jnp.float32
        )
        normed_grad = jnp.einsum(
            "pd,gcd->pgc", mixer_grad, out_weight, preferred_element_type=jnp.float32
        )
        finish_grads = finish_pull(normed_grad)
        later_grad = carry_chain(front_out[5], finish_grads[5], True)[1]
        through_grad = jnp.sum(later_grad * state_in, axis=(2, 3))
        front_grads = front_pull(
            (
                finish_grads[0],
                finish_grads[1],
                finish_grads[2],
                finish_grads[3],
                finish_grads[4],
                through_grad,
                later_grad,
            )
        )
        skip_acc = skip_acc + finish_grads[6]
        group_acc = group_acc + finish_grads[7]
        conv_w_acc = conv_w_acc + front_grads[2]
        conv_b_acc = conv_b_acc + front_grads[3]
        step_acc = step_acc + front_grads[4]
        decay_acc = decay_acc + front_grads[5]
        tail_back = rim_pass(front_grads[1], -1) * tail_keep
        projected_grad = (
            front_grads[0]
            .at[patch_rows - (CONV - 1) :, :, GROUP_WIDTH : GROUP_WIDTH + CONV_CH]
            .add(tail_back)
        )
        projected_low = projected_grad.astype(jnp.bfloat16)
        in_acc = in_acc + jnp.einsum(
            "pd,pgc->gdc", normed_in, projected_low, preferred_element_type=jnp.float32
        )
        normed_in_grad = head_sum(
            jnp.einsum("pgc,gdc->pd", projected_low, in_weight, preferred_element_type=jnp.float32)
        )
        global_norm_grad, in_gain_piece = norm_grad(global_in, norm_in_gain, normed_in_grad)
        gain_in_acc = gain_in_acc + in_gain_piece
        global_in_grad = (global_grad + global_norm_grad).astype(jnp.bfloat16)
        patch_acc = patch_acc + jnp.einsum(
            "pkd,pe->kde", own_input, global_in_grad, preferred_element_type=jnp.float32
        )
        patch_piece = jnp.einsum(
            "pe,kde->pkd", global_in_grad, patch_weight, preferred_element_type=jnp.float32
        ).reshape(patch_rows, my_bytes * model_dim)
        own_local = lax.dynamic_slice_in_dim(
            local_grad.reshape(patch_rows, input_cols), input_start, my_bytes * model_dim, 1
        )
        input_rows.append(own_local + patch_piece)
    reduced = (
        lax.psum_scatter(patch_acc, "dp", scatter_dimension=1, tiled=True),
        lax.psum_scatter(gain_in_acc[None], "dp", scatter_dimension=1, tiled=True),
        lax.psum_scatter(in_acc, "dp", scatter_dimension=1, tiled=True),
        lax.psum_scatter(conv_w_acc, "dp", scatter_dimension=1, tiled=True),
        lax.psum_scatter(conv_b_acc, "dp", scatter_dimension=1, tiled=True),
        lax.psum_scatter(jnp.tile(step_acc, (1, dp_size)), "dp", scatter_dimension=1, tiled=True),
        lax.psum_scatter(jnp.tile(decay_acc, (1, dp_size)), "dp", scatter_dimension=1, tiled=True),
        lax.psum_scatter(jnp.tile(skip_acc, (1, dp_size)), "dp", scatter_dimension=1, tiled=True),
        lax.psum_scatter(group_acc, "dp", scatter_dimension=1, tiled=True),
        lax.psum_scatter(out_acc, "dp", scatter_dimension=1, tiled=True),
        lax.psum_scatter(gain_attn_acc[None], "dp", scatter_dimension=1, tiled=True),
        lax.psum_scatter(qkv_acc, "dp", scatter_dimension=1, tiled=True),
        lax.psum_scatter(attn_acc, "dp", scatter_dimension=1, tiled=True),
        lax.psum_scatter(gain_ffn_acc[None], "dp", scatter_dimension=1, tiled=True),
    )
    return (
        jnp.stack(block_rows),
        jnp.stack(input_rows),
        reduced[0],
        reduced[1][0],
        reduced[2],
        reduced[3],
        reduced[4],
        reduced[5],
        reduced[6],
        reduced[7],
        reduced[8],
        reduced[9],
        reduced[10][0],
        reduced[11],
        reduced[12],
        reduced[13][0],
        ffn_acc,
    )


def solution(mesh):
    in_specs = (
        P(None, "dp", None),
        P(),
        P("mp", None, None),
        P(),
        P("mp", None, None),
        P("mp", None, None),
        P("mp", None),
        P("mp", None),
        P("mp", None),
        P("mp", None),
        P("mp", None),
        P("mp", None, None),
        P(),
        P(None, None, "mp"),
        P("mp", None),
        P(),
        P(None, "mp", "dp"),
        P(None, "dp", None),
    )
    out_specs = (
        P(None, "dp", "mp"),
        P(None, "dp", "mp"),
        P("mp", "dp", None),
        P("dp"),
        P("mp", "dp", None),
        P("mp", "dp", None),
        P("mp", "dp"),
        P("mp", None),
        P("mp", None),
        P("mp", None),
        P("mp", "dp"),
        P("mp", "dp", None),
        P("dp"),
        P(None, "dp", "mp"),
        P("mp", "dp"),
        P("dp"),
        P(None, "mp", "dp"),
    )
    return jax.shard_map(body, mesh=mesh, in_specs=in_specs, out_specs=out_specs, check_vma=False)
```

profile of v0, /device:TPU:2, one launch (start us, length us, event | category | flops | bytes accessed | tf_op | source)
XLA Modules:
  0.0 2714.1 jit_solution(16002499339858907598)
XLA Ops:
  12.5 3.6 convolution_bitcast_fusion.49
  42.2 19.7 all-reduce.95.cloned.1.call-done
  90.7 8.9 collective-permute-done.1
  109.6 6.7 collective-permute-done.2
  144.1 10.8 all_gather.108
  154.9 9.3 all_gather.112
  164.2 9.4 all_gather.116
  173.6 9.0 all_gather.120
  187.7 3.8 fusion.206
  203.3 24.0 while.124
  233.6 13.6 while.125
  253.5 13.7 while.126
  279.5 13.6 while.127
  327.3 14.7 all-reduce.93.cloned.1.call-done
  425.2 9.8 all_gather.136
  435.0 8.9 all_gather.132
  443.9 9.8 all_gather.128
  453.7 9.1 all_gather.124
  469.7 39.9 %all-reduce.91.cloned.1.call-done = (f32[128,1024]{1,0:T(8,128)}, f32[128,1024]{1,0:T(8,128)}, f32[128,1024]{1,0:T(8,128)}, f32[128,1024]{1,0:T(8,128)}) async-done(((f32[128,1024]{1,0:T(8,128)}, f32[128,1024]{1,0:T(8,128)}, f32[128,1024]{1,0:T(8,128)}, f32[128,1024]{1,0:T(8,128)}), (f32[128,1024]{1,0:T(8,128)}, f32[128,1024]{1,0:T(8,128)}, f32[128,1024]{1,0:T(8,128)}, ...) | async-done | bytes 2097168 | tf_op jit(solution)/shard_map/psum | solution.py:278
  514.2 9.8 all_gather.123
  526.7 8.9 all_gather.119
  538.4 9.8 all_gather.115
  551.0 8.9 all_gather.111
  563.5 841.4 %all-reduce.89.cloned.1.call-done = (f32[2,1024,512]{2,1,0:T(8,128)}, f32[2,1024,512]{2,1,0:T(8,128)}, f32[2,1024,512]{2,1,0:T(8,128)}, f32[2,1024,512]{2,1,0:T(...) async-done(((f32[2,1024,512]{2,1,0:T(8,128)}, f32[2,1024,512]{2,1,0:T(8,128)}, f32[2,1024,512]{2,1,0:T(8,128)}, ...) | async-done | bytes 25165840 | tf_op jit(solution)/shard_map/psum | solution.py:286
  1404.9 4.1 fusion.170
  1412.1 4.1 fusion.172
  1419.4 4.3 fusion.171
  1426.8 4.1 fusion.173
  1434.0 13.2 reduce-scatter.43.cloned.1.call-done
  1447.2 17.4 all_gather.125
  1464.6 21.7 reduce-scatter.47.cloned.1.call-done
  1486.3 17.5 all_gather.133
  1503.8 22.3 reduce-scatter.45.cloned.1.call-done
  1526.1 17.4 all_gather.129
  1543.5 22.2 reduce-scatter.49.cloned.1.call-done
  1565.7 16.2 all_gather.137
  1653.0 88.9 %all-reduce.87.cloned.1.call-done = (f32[128,1024]{1,0:T(8,128)}, f32[128,1024]{1,0:T(8,128)}, f32[128,1024]{1,0:T(8,128)}, f32[128,1024]{1,0:T(8,128)}) async-done(((f32[128,1024]{1,0:T(8,128)}, f32[128,1024]{1,0:T(8,128)}, f32[128,1024]{1,0:T(8,128)}, f32[128,1024]{1,0:T(8,128)}), (f32[128,1024]{1,0:T(8,128)}, f32[128,1024]{1,0:T(8,128)}, f32[128,1024]{1,0:T(8,128)}, ...) | async-done | bytes 2097168 | tf_op jit(solution)/shard_map/psum | solution.py:351
  1816.0 19.6 while.130
  1837.3 19.5 while.129
  1858.6 19.9 while.128
  1887.1 14.0 while.131
  1961.7 3.8 multiply_reduce_fusion.34
  2017.0 4.0 fusion.144
  2021.1 3.9 fusion.142
  2025.1 3.9 fusion.140
  2029.2 4.0 fusion.138
  2044.1 6.1 add_bitcast_fusion.1
  2075.1 4.7 fusion.436
  2079.8 8.5 add_add_fusion
  2110.0 22.0 reduce-scatter.37.cloned.1.call-done
  2133.0 38.2 %reduce-scatter.39.cloned.1.call-done = f32[128,256]{1,0:T(8,128)} async-done(((f32[1024,256]{1,0:T(8,128)}), f32[128,256]{1,0:T(8,128)}) %reduce-scatter.39.cloned.1.call-update) | async-done | bytes 131088 | tf_op jit(solution)/shard_map/reduce_scatter | solution.py:111
  2172.2 38.2 %reduce-scatter.41.cloned.1.call-done = f32[128,256]{1,0:T(8,128)} async-done(((f32[1024,256]{1,0:T(8,128)}), f32[128,256]{1,0:T(8,128)}) %reduce-scatter.41.cloned.1.call-update) | async-done | bytes 131088 | tf_op jit(solution)/shard_map/reduce_scatter | solution.py:111
  2212.2 35.3 %reduce-scatter.71.cloned.1.call-done = f32[128,1]{1,0:T(8,128)} async-done(((f32[1024,1]{1,0:T(8,128)}), f32[128,1]{1,0:T(8,128)}) %reduce-scatter.71.cloned.1.call-update) | async-done | bytes 528
  2252.7 32.2 %reduce-scatter.67.cloned.1.call-done = f32[64,1]{1,0:T(8,128)} async-done(((f32[512,1]{1,0:T(8,128)}), f32[64,1]{1,0:T(8,128)}) %reduce-scatter.67.cloned.1.call-update) | async-done | bytes 272
  2286.3 35.8 %reduce-scatter.69.cloned.1.call-done = f32[128,1]{1,0:T(8,128)} async-done(((f32[1024,1]{1,0:T(8,128)}), f32[128,1]{1,0:T(8,128)}) %reduce-scatter.69.cloned.1.call-update) | async-done | bytes 528
  2323.5 48.5 %reduce-scatter.57.cloned.1.call-done = f32[3,128,256]{1,2,0:T(8,128)} async-done(((f32[3,1024,256]{1,2,0:T(8,128)}), f32[3,128,256]{1,2,0:T(8,128)}) %reduce-scatter.57.cloned.1.call-update) | async-done | bytes 393232 | tf_op jit(solution)/shard_map/reduce_scatter | solution.py:424
  2374.2 10.1 all-reduce.71
  2386.1 22.8 reduce-scatter.65.cloned.1.call-done
  2410.2 35.5 %reduce-scatter.63.cloned.1.call-done = f32[96,4]{1,0:T(8,128)} async-done(((f32[768,4]{1,0:T(8,128)}), f32[96,4]{1,0:T(8,128)}) %reduce-scatter.63.cloned.1.call-update) | async-done | bytes 1552
  2458.1 24.9 reduce-scatter.61.cloned.1.call-done
  2484.4 38.6 %reduce-scatter.59.cloned.1.call-done = f32[256,128]{1,0:T(8,128)} async-done(((f32[256,1024]{1,0:T(8,128)}), f32[256,128]{1,0:T(8,128)}) %reduce-scatter.59.cloned.1.call-update) | async-done | bytes 131088 | tf_op jit(solution)/shard_map/reduce_scatter | solution.py:425
  2523.0 45.4 %reduce-scatter.55.cloned.1.call-done = f32[1,64,1024]{2,1,0:T(8,128)} async-done(((f32[1,512,1024]{2,1,0:T(8,128)}), f32[1,64,1024]{2,1,0:T(8,128)}) %reduce-scatter.55.cloned.1.call-update) | async-done | bytes 262160 | tf_op jit(solution)/shard_map/reduce_scatter | solution.py:422
  2568.4 63.1 %reduce-scatter.53.cloned.1.call-done = f32[1,128,1288]{1,2,0:T(8,128)} async-done(((f32[1,1024,1288]{1,2,0:T(8,128)}), f32[1,128,1288]{1,2,0:T(8,128)}) %reduce-scatter.53.cloned.1.call-update) | async-done | bytes 659472 | tf_op jit(solution)/shard_map/reduce_scatter | solution.py:415
  2631.5 75.6 %reduce-scatter.51.cloned.1.call-done = f32[2,128,1024]{2,1,0:T(8,128)} async-done(((f32[2,1024,1024]{2,1,0:T(8,128)}), f32[2,128,1024]{2,1,0:T(8,128)}) %reduce-scatter.51.cloned.1.call-update) | async-done | bytes 1048592 | tf_op jit(solution)/shard_map/reduce_scatter | solution.py:413
  (1886 shorter events, 774.7 us)
Async XLA Ops:
  7.2 54.7 %all-reduce.95.cloned.1.call-start = ((), (), s32[]{:S(2)}) async-start(), calls=%async_computation.51 | async-start | bytes 524288 | tf_op jit(solution)/shard_map/psum | solution.py:103
  24.6 178.7 %all-gather.17.cloned.1.call-start = ((), (), s32[]{:S(2)}) async-start(), calls=%async_computation.32 | async-start | bytes 2359296 | tf_op jit(solution)/shard_map/all_gather | solution.py:25
  37.0 150.7 %copy-start.272 = (f32[768]{0:T(1024)}, f32[768]{0:T(1024)S(1)}, u32[]{:S(2)}) copy-start(f32[768]{0:T(1024)S(1)} %get-tuple-element.1661) | copy-start | bytes 9220
  37.0 150.7 %copy-start.274 = (f32[768]{0:T(1024)}, f32[768]{0:T(1024)S(1)}, u32[]{:S(2)}) copy-start(f32[768]{0:T(1024)S(1)} %get-tuple-element.1662) | copy-start | bytes 9220
  37.1 150.7 %copy-start.276 = (f32[768]{0:T(1024)}, f32[768]{0:T(1024)S(1)}, u32[]{:S(2)}) copy-start(f32[768]{0:T(1024)S(1)} %get-tuple-element.1663) | copy-start | bytes 9220
  37.1 150.7 %copy-start.278 = (f32[768]{0:T(1024)}, f32[768]{0:T(1024)S(1)}, u32[]{:S(2)}) copy-start(f32[768]{0:T(1024)S(1)} %get-tuple-element.1664) | copy-start | bytes 9220
  70.7 158.4 %copy-start.303 = (f32[16,8]{0,1:T(8,128)}, f32[16,8]{0,1:T(8,128)S(1)}, u32[]{:S(2)}) copy-start(f32[16,8]{0,1:T(8,128)S(1)} %get-tuple-element.1960) | copy-start | bytes 1540
  70.7 178.2 %copy-start.305 = (f32[16,8]{0,1:T(8,128)}, f32[16,8]{0,1:T(8,128)S(1)}, u32[]{:S(2)}) copy-start(f32[16,8]{0,1:T(8,128)S(1)} %get-tuple-element.1962) | copy-start | bytes 1540
  70.7 224.2 %copy-start.301 = (f32[16,8]{0,1:T(8,128)}, f32[16,8]{0,1:T(8,128)S(1)}, u32[]{:S(2)}) copy-start(f32[16,8]{0,1:T(8,128)S(1)} %get-tuple-element.1874) | copy-start | bytes 1540
  70.8 158.2 %copy-start.223 = (f32[16,1,8]{0,2,1:T(8,128)}, f32[16,1,8]{0,2,1:T(8,128)S(1)}, u32[]{:S(2)}) copy-start(f32[16,1,8]{0,2,1:T(8,128)S(1)} %copy.1641) | copy-start | bytes 1540
  71.0 177.9 %copy-start.217 = (f32[16,1,8]{0,2,1:T(8,128)}, f32[16,1,8]{0,2,1:T(8,128)S(1)}, u32[]{:S(2)}) copy-start(f32[16,1,8]{0,2,1:T(8,128)S(1)} %copy.1662) | copy-start | bytes 1540
  71.2 197.7 %copy-start.226 = (f32[16,1,8]{0,2,1:T(8,128)}, f32[16,1,8]{0,2,1:T(8,128)S(1)}, u32[]{:S(2)}) copy-start(f32[16,1,8]{0,2,1:T(8,128)S(1)} %copy.1683) | copy-start | bytes 1540
  71.3 223.5 %copy-start.220 = (f32[16,1,8]{0,2,1:T(8,128)}, f32[16,1,8]{0,2,1:T(8,128)S(1)}, u32[]{:S(2)}) copy-start(f32[16,1,8]{0,2,1:T(8,128)S(1)} %copy.1704) | copy-start | bytes 1540
  72.5 9.1 collective-permute-start
  85.8 147.8 %all-gather.19.cloned.1.call-start = ((), (), s32[]{:S(2)}) async-start(), calls=%async_computation.33 | async-start | bytes 2359296 | tf_op jit(solution)/shard_map/all_gather | solution.py:25
  87.7 11.9 collective-permute-start.1
  103.8 149.7 %all-gather.21.cloned.1.call-start = ((), (), s32[]{:S(2)}) async-start(), calls=%async_computation.34 | async-start | bytes 2359296 | tf_op jit(solution)/shard_map/all_gather | solution.py:25
  106.5 9.9 collective-permute-start.2
  122.1 156.9 %all-gather.23.cloned.1.call-start = ((), (), s32[]{:S(2)}) async-start(), calls=%async_computation.35 | async-start | bytes 2359296 | tf_op jit(solution)/shard_map/all_gather | solution.py:25
  130.2 57.5 %collective-permute-start.3 = (f32[3,1,768]{0,2,1:T(8,128)}, f32[3,1,768]{0,2,1:T(8,128)}, u32[]{:S(2)}, u32[]{:S(2)}) collective-permute-start(f32[3,1,768]{0,2,1:T(8,128)} %slice_multiply_fusion), channel_id=1, source_target_pairs={{0,4},{4,8},{8,12},{12,16},{16,20},{20,24},{24,28},{1,5},{5,9},{9,... | collective-permute-start | bytes 27656 | tf_op jit(solution)/shard_map/ppermute | solution.py:44
  203.2 138.8 %all-reduce.93.cloned.1.call-start = ((), (), s32[]{:S(2)}) async-start(), calls=%async_computation.50 | async-start | bytes 524288 | tf_op jit(solution)/shard_map/psum | solution.py:103
  306.1 203.5 %all-reduce.91.cloned.1.call-start = ((), (), s32[]{:S(2)}) async-start(), calls=%async_computation.49 | async-start | bytes 4194304 | tf_op jit(solution)/shard_map/psum | solution.py:278
  342.9 1403.9 %copy-start.111 = (f32[16,1024]{1,0:T(8,128)}, f32[16,1024]{1,0:T(8,128)S(1)}, u32[]{:S(2)}) copy-start(f32[16,1024]{1,0:T(8,128)S(1)} %add.1424) | copy-start | bytes 196612
  354.7 1392.1 %copy-start.113 = (f32[16,1024]{1,0:T(8,128)}, f32[16,1024]{1,0:T(8,128)S(1)}, u32[]{:S(2)}) copy-start(f32[16,1024]{1,0:T(8,128)S(1)} %add.1445) | copy-start | bytes 196612
  421.7 983.2 %all-reduce.89.cloned.1.call-start = ((), (), s32[]{:S(2)}) async-start(), calls=%async_computation.48 | async-start | bytes 50331648 | tf_op jit(solution)/shard_map/psum | solution.py:286
  563.4 883.8 %reduce-scatter.43.cloned.1.call-start = ((), (), s32[]{:S(2)}) async-start(), calls=%async_computation.23 | async-start | bytes 1179648 | tf_op jit(solution)/shard_map/reduce_scatter | solution.py:111
  1412.1 74.2 %reduce-scatter.47.cloned.1.call-start = ((), (), s32[]{:S(2)}) async-start(), calls=%async_computation.25 | async-start | bytes 1179648 | tf_op jit(solution)/shard_map/reduce_scatter | solution.py:111
  1419.3 106.8 %reduce-scatter.45.cloned.1.call-start = ((), (), s32[]{:S(2)}) async-start(), calls=%async_computation.24 | async-start | bytes 1179648 | tf_op jit(solution)/shard_map/reduce_scatter | solution.py:111
  1426.7 139.0 %reduce-scatter.49.cloned.1.call-start = ((), (), s32[]{:S(2)}) async-start(), calls=%async_computation.26 | async-start | bytes 1179648 | tf_op jit(solution)/shard_map/reduce_scatter | solution.py:111
  1433.9 308.0 %all-reduce.87.cloned.1.call-start = ((), (), s32[]{:S(2)}) async-start(), calls=%async_computation.47 | async-start | bytes 4194304 | tf_op jit(solution)/shard_map/psum | solution.py:351
  1652.9 163.0 %all-gather.29.cloned.1.call-start = ((), (), s32[]{:S(2)}) async-start(), calls=%async_computation.38 | async-start | bytes 2359296 | tf_op jit(solution)/shard_map/all_gather | solution.py:25
  1760.0 77.3 %all-gather.27.cloned.1.call-start = ((), (), s32[]{:S(2)}) async-start(), calls=%async_computation.37 | async-start | bytes 2359296 | tf_op jit(solution)/shard_map/all_gather | solution.py:25
  1763.8 94.8 %all-gather.25.cloned.1.call-start = ((), (), s32[]{:S(2)}) async-start(), calls=%async_computation.36 | async-start | bytes 2359296 | tf_op jit(solution)/shard_map/all_gather | solution.py:25
  1769.9 117.2 %all-gather.31.cloned.1.call-start = ((), (), s32[]{:S(2)}) async-start(), calls=%async_computation.39 | async-start | bytes 2359296 | tf_op jit(solution)/shard_map/all_gather | solution.py:25
  1815.9 239.3 %all-reduce.85.cloned.1.call-start = ((), (), s32[]{:S(2)}) async-start(), calls=%async_computation.46 | async-start | bytes 524288 | tf_op jit(solution)/shard_map/psum | solution.py:103
  1973.0 21.5 collective-permute-start.4
  1975.7 19.0 collective-permute-start.5
  1982.9 12.7 collective-permute-start.6
  1987.1 19.3 collective-permute-start.7
  2016.9 91.7 %reduce-scatter.35.cloned.1.call-start = ((), (), s32[]{:S(2)}) async-start(), calls=%async_computation.19 | async-start | bytes 1179648 | tf_op jit(solution)/shard_map/reduce_scatter | solution.py:111
  2021.0 111.0 %reduce-scatter.37.cloned.1.call-start = ((), (), s32[]{:S(2)}) async-start(), calls=%async_computation.20 | async-start | bytes 1179648 | tf_op jit(solution)/shard_map/reduce_scatter | solution.py:111
  2025.0 146.1 %reduce-scatter.39.cloned.1.call-start = ((), (), s32[]{:S(2)}) async-start(), calls=%async_computation.21 | async-start | bytes 1179648 | tf_op jit(solution)/shard_map/reduce_scatter | solution.py:111
  2029.1 181.3 %reduce-scatter.41.cloned.1.call-start = ((), (), s32[]{:S(2)}) async-start(), calls=%async_computation.22 | async-start | bytes 1179648 | tf_op jit(solution)/shard_map/reduce_scatter | solution.py:111
  2033.2 214.3 %reduce-scatter.71.cloned.1.call-start = ((), (), s32[]{:S(2)}) async-start(), calls=%async_computation.45 | async-start | bytes 589824
  2041.9 243.1 %reduce-scatter.67.cloned.1.call-start = ((), (), s32[]{:S(2)}) async-start(), calls=%async_computation.43 | async-start | bytes 294912
  2042.9 279.3 %reduce-scatter.69.cloned.1.call-start = ((), (), s32[]{:S(2)}) async-start(), calls=%async_computation.44 | async-start | bytes 589824
  2044.0 328.0 %reduce-scatter.57.cloned.1.call-start = ((), (), s32[]{:S(2)}) async-start(), calls=%async_computation.30 | async-start | bytes 3538944 | tf_op jit(solution)/shard_map/reduce_scatter | solution.py:424
  2050.2 358.6 %reduce-scatter.65.cloned.1.call-start = ((), (), s32[]{:S(2)}) async-start(), calls=%async_computation.42 | async-start | bytes 442368
  2053.9 391.8 %reduce-scatter.63.cloned.1.call-start = ((), (), s32[]{:S(2)}) async-start(), calls=%async_computation.41 | async-start | bytes 442368
  2055.1 427.9 %reduce-scatter.61.cloned.1.call-start = ((), (), s32[]{:S(2)}) async-start(), calls=%async_computation.40 | async-start | bytes 589824
  2058.8 464.2 %reduce-scatter.59.cloned.1.call-start = ((), (), s32[]{:S(2)}) async-start(), calls=%async_computation.31 | async-start | bytes 1179648 | tf_op jit(solution)/shard_map/reduce_scatter | solution.py:425
  2060.2 508.2 %reduce-scatter.55.cloned.1.call-start = ((), (), s32[]{:S(2)}) async-start(), calls=%async_computation.29 | async-start | bytes 2359296 | tf_op jit(solution)/shard_map/reduce_scatter | solution.py:422
  2064.1 567.3 %reduce-scatter.53.cloned.1.call-start = ((), (), s32[]{:S(2)}) async-start(), calls=%async_computation.28 | async-start | bytes 5935104 | tf_op jit(solution)/shard_map/reduce_scatter | solution.py:415
  2071.6 635.5 %reduce-scatter.51.cloned.1.call-start = ((), (), s32[]{:S(2)}) async-start(), calls=%async_computation.27 | async-start | bytes 9437184 | tf_op jit(solution)/shard_map/reduce_scatter | solution.py:413
  2107.0 142.0 %copy-start.403 = (f32[512]{0:T(512)S(1)}, f32[512]{0:T(512)}, u32[]{:S(2)}) copy-start(f32[512]{0:T(512)} %get-tuple-element.1787) | copy-start | bytes 6148
  2107.0 142.1 %copy-start.402 = (f32[512]{0:T(512)S(1)}, f32[512]{0:T(512)}, u32[]{:S(2)}) copy-start(f32[512]{0:T(512)} %get-tuple-element.1946) | copy-start | bytes 6148
  2107.0 142.4 %copy-start.426 = (f32[512]{0:T(512)S(1)}, f32[512]{0:T(512)}, u32[]{:S(2)}) copy-start(f32[512]{0:T(512)} %get-tuple-element.1789) | copy-start | bytes 6148
  2107.0 142.6 %copy-start.425 = (f32[512]{0:T(512)S(1)}, f32[512]{0:T(512)}, u32[]{:S(2)}) copy-start(f32[512]{0:T(512)} %get-tuple-element.1949) | copy-start | bytes 6148
  2107.0 142.9 %copy-start.153 = (f32[128,1024]{1,0:T(8,128)S(1)}, f32[128,1024]{1,0:T(8,128)}, u32[]{:S(2)}) copy-start(f32[128,1024]{1,0:T(8,128)} %get-tuple-element.1922) | copy-start | bytes 1572868
  2108.6 142.2 %copy-start.152 = (f32[128,1024]{1,0:T(8,128)S(1)}, f32[128,1024]{1,0:T(8,128)}, u32[]{:S(2)}) copy-start(f32[128,1024]{1,0:T(8,128)} %get-tuple-element.1808) | copy-start | bytes 1572868
  2108.6 143.1 %copy-start.151 = (f32[128,1024]{1,0:T(8,128)S(1)}, f32[128,1024]{1,0:T(8,128)}, u32[]{:S(2)}) copy-start(f32[128,1024]{1,0:T(8,128)} %get-tuple-element.1924) | copy-start | bytes 1572868
  2250.8 123.3 %copy-start.476 = (f32[8]{0:T(128)S(1)}, f32[8]{0:T(128)}, u32[]{:S(2)}) copy-start(f32[8]{0:T(128)} %get-tuple-element.1866) | copy-start | bytes 100
  2250.8 123.3 %copy-start.481 = (f32[8]{0:T(128)S(1)}, f32[8]{0:T(128)}, u32[]{:S(2)}) copy-start(f32[8]{0:T(128)} %get-tuple-element.1801) | copy-start | bytes 100
  2453.2 253.9 %copy-start.1 = (bf16[1,1024,1288]{1,2,0:T(8,128)(2,1)S(1)}, bf16[1,1024,1288]{1,2,0:T(8,128)(2,1)}, u32[]{:S(2)}) copy-start(bf16[1,1024,1288]{1,2,0:T(8,128)(2,1)} %param.47) | copy-start | bytes 7913476
  (516 other events, 5394.7 us)
Sparse Core Ops, SparseCore 0:
  24.7 37.1 all-reduce.94
  85.9 28.9 all-gather.16
  117.0 29.7 all-gather.18
  148.6 29.9 all-gather.20
  203.4 27.5 all-gather.22
  306.3 35.7 all-reduce.92
  421.8 87.7 all-reduce.90
  563.6 841.2 all-reduce.88
  1412.2 34.9 reduce-scatter.42
  1450.2 36.0 reduce-scatter.46
  1490.0 36.0 reduce-scatter.44
  1529.7 35.9 reduce-scatter.48
  1653.1 88.8 all-reduce.86
  1760.1 26.8 all-gather.28
  1788.9 28.0 all-gather.26
  1818.9 27.8 all-gather.24
  1849.3 27.9 all-gather.30
  2017.0 36.8 all-reduce.84
  2057.1 35.7 reduce-scatter.34
  2095.9 35.9 reduce-scatter.36
  2135.1 35.9 reduce-scatter.38
  2174.3 36.0 reduce-scatter.40
  2213.5 34.0 reduce-scatter.70
  2251.3 33.6 reduce-scatter.66
  2288.0 34.0 reduce-scatter.68
  2325.7 46.2 reduce-scatter.56
  2374.9 33.8 reduce-scatter.64
  2411.9 33.8 reduce-scatter.62
  2448.8 34.0 reduce-scatter.60
  2486.9 36.0 reduce-scatter.58
  2527.2 41.1 reduce-scatter.54
  2572.4 59.0 reduce-scatter.52
  2635.8 71.3 reduce-scatter.50
where the time goes:
time: 2730 us; the launch traced here: 2710 us
  waiting for transfers between devices  1660 us (61%)
  matrix products  282 us (10%)
  local copies, waits for them, and re-layouts  277 us (10%)
  other arithmetic  257 us (9%)
  blocking collectives  192 us (7%)
  between operations  27.4 us (1%)
    psum x1, waiting for transfers between devices, body(): lax.psum(jnp.einsum('tc,kcf->ktf', ffn_rows_in, ffn_weight[:2], preferred...  841 us
    unnamed x39, waiting for transfers between devices  187 us
    reduce_scatter x8, waiting for transfers between devices, spread_rows(): return lax.psum_scatter(terms, 'dp', scatter_dimension=0, tiled=True)  178 us
    select_n x64, other arithmetic, turn(): return jax.tree.map(lambda a, b: jnp.where(reached, a, b), new, before)  92 us
    psum x1, waiting for transfers between devices, body(): lax.psum(jnp.einsum('kte,kde->td', qkv_grad, qkv_weight, preferred_elemen...  88.9 us
    reduce_scatter x1, waiting for transfers between devices, body(): lax.psum_scatter(patch_acc, 'dp', scatter_dimension=1, tiled=True)  75.6 us
    all_gather x8, blocking collectives, gather_rows(): return lax.all_gather(features, 'dp', axis=0, tiled=True)  75 us
    unnamed x1112, local copies, waits for them, and re-layouts  72.3 us
  transfers between devices with their start and end apart: 41, of which 26 were waited for; matrix products, arithmetic and copies ran while one was open for 17% of the time, Pallas kernels for 0%

commit v1 on v0

v1 whole, which is shorter than its diff:
```python
from functools import partial

import jax
import jax.numpy as jnp
from jax import lax
from jax.experimental import pallas as pl
from jax.experimental.pallas import tpu as pltpu
from jax.sharding import PartitionSpec as P

STATE = 128
CONV = 4
SEQS = 3
GROUP_WIDTH = 512
GROUP_HEADS = 8
HEAD_DIM = 64
ATT_DIM = 64
CONV_CH = 768

norm_eps = 1e-06
highest = lax.Precision.HIGHEST
large_negative = -1e30
f32 = jnp.float32
bf16 = jnp.bfloat16
MESH = pl.DeviceIdType.MESH
VMEM = pl.BlockSpec(memory_space=pltpu.VMEM)
SMEM = pl.BlockSpec(memory_space=pltpu.SMEM)
DMA = pltpu.SemaphoreType.DMA


def dot(a, b, dims=((1,), (0,)), precision=None):
    return lax.dot_general(
        a, b, (dims, ((), ())), preferred_element_type=f32, precision=precision
    )


def inv_rms(values):
    return lax.rsqrt(jnp.mean(values * values, axis=-1, keepdims=True) + norm_eps)


def rms_back(values, gain, upstream):
    scale = inv_rms(values)
    weighted = upstream * gain
    inner = jnp.mean(weighted * values, axis=-1, keepdims=True)
    back = scale * weighted - values * (inner * scale * scale * scale)
    return back, upstream * (values * scale)


def silu_pair(values):
    sig = jax.nn.sigmoid(values)
    return values * sig, sig * (1.0 + values * (1.0 - sig))


def rcopy(src, dst, send_sem, recv_sem, dp, mp):
    return pltpu.make_async_remote_copy(
        src_ref=src,
        dst_ref=dst,
        send_sem=send_sem,
        recv_sem=recv_sem,
        device_id={"dp": dp, "mp": mp},
        device_id_type=MESH,
    )


def greet(barrier, dp, mp):
    pl.semaphore_signal(barrier, inc=1, device_id={"dp": dp, "mp": mp}, device_id_type=MESH)


def plain_params(mib=56):
    return pltpu.CompilerParams(vmem_limit_bytes=mib * 2**20)


def remote_params(cid, mib=40):
    return pltpu.CompilerParams(
        collective_id=cid, has_side_effects=True, vmem_limit_bytes=mib * 2**20
    )


def embed_kernel(n, mpn, own, weight, gain, total_out, normed_out, part, recv, low, normed, ss1, rs1, ss2, rs2):
    i, j = lax.axis_index("dp"), lax.axis_index("mp")
    reps = n // mpn
    m = i // reps
    inside = m == j
    barrier = pltpu.get_barrier_semaphore()
    for d in range(1, mpn):
        greet(barrier, i, (j + d) % mpn)
    for s in range(n):
        @pl.when(jnp.logical_not((s == i) & inside))
        def _():
            greet(barrier, s, m)
    rows = part.shape[1]
    sums = dot(own[...], weight[...])
    for t in range(mpn):
        part[t] = sums[t * rows : (t + 1) * rows]
    pl.semaphore_wait(barrier, mpn - 1 + reps * mpn - inside.astype(jnp.int32))
    first = []
    for d in range(1, mpn):
        t = (j + d) % mpn
        copy = rcopy(part.at[t], recv.at[j], ss1.at[t], rs1.at[j], i, t)
        copy.start()
        first.append(copy)
    total = part[j]
    for d in range(1, mpn):
        s = (j + d) % mpn
        rcopy(part.at[s], recv.at[s], ss1.at[s], rs1.at[s], i, s).wait_recv()
        total = total + recv[s]
    total_out[...] = total
    low[...] = (total * inv_rms(total) * gain[...]).astype(bf16)
    for h in range(reps):
        for t in range(mpn):
            q = h * mpn + t
            here = (j * reps + h == i) & (t == j)

            @pl.when(jnp.logical_not(here))
            def _():
                rcopy(low, normed.at[i], ss2.at[q], rs2.at[i], j * reps + h, t).start()

            @pl.when(here)
            def _():
                normed[i] = low[...]
    for s in range(n):
        @pl.when(jnp.logical_not((s == i) & inside))
        def _():
            rcopy(low, normed.at[s], ss2.at[0], rs2.at[s], s, m).wait_recv()
    normed_out[...] = normed[...]
    for copy in first:
        copy.wait_send()
    for h in range(reps):
        for t in range(mpn):
            q = h * mpn + t

            @pl.when(jnp.logical_not((j * reps + h == i) & (t == j)))
            def _():
                rcopy(low, normed.at[i], ss2.at[q], rs2.at[i], j * reps + h, t).wait_send()


def embed(n, mpn, own, weight, gain):
    rows, dim = own.shape[0] // mpn, weight.shape[1]
    reps = n // mpn
    return pl.pallas_call(
        partial(embed_kernel, n, mpn),
        out_shape=(
            jax.ShapeDtypeStruct((rows, dim), f32),
            jax.ShapeDtypeStruct((n, rows, dim), bf16),
        ),
        in_specs=[VMEM] * 3,
        out_specs=(VMEM, VMEM),
        scratch_shapes=[
            pltpu.VMEM((mpn, rows, dim), f32),
            pltpu.VMEM((mpn, rows, dim), f32),
            pltpu.VMEM((rows, dim), bf16),
            pltpu.VMEM((n, rows, dim), bf16),
            DMA((mpn,)),
            DMA((mpn,)),
            DMA((reps * mpn,)),
            DMA((n,)),
        ],
        compiler_params=remote_params(0),
        name="embed",
    )(own, weight, gain)


def seg_starts(lengths, places):
    end0 = lengths[0]
    end1 = end0 + lengths[1]
    end2 = end1 + lengths[2]
    return jnp.where(
        places >= end2, end2, jnp.where(places >= end1, end1, jnp.where(places >= end0, end0, 0))
    )


def conv_taps(conv_in, pos, lag):
    moved = conv_in if lag == 0 else pltpu.roll(conv_in, lag, 0)
    return jnp.where(pos >= lag, moved, 0.0)


def mixer_state(lengths, projected, conv_weight, conv_bias, step_bias, log_decay):
    patches = projected.shape[0]
    places = lax.broadcasted_iota(jnp.int32, (patches, 1), 0)
    start = seg_starts(lengths, places)
    pos = places - start
    conv_in = projected[:, GROUP_WIDTH : GROUP_WIDTH + CONV_CH]
    conv_out = conv_bias
    for lag in range(CONV):
        conv_out = conv_out + conv_taps(conv_in, pos, lag) * conv_weight[CONV - 1 - lag][None]
    step_raw = projected[:, GROUP_WIDTH + CONV_CH :] + step_bias
    step = jnp.maximum(step_raw, 0.0) + jnp.log1p(jnp.exp(-jnp.abs(step_raw)))
    logd = -step * jnp.exp(log_decay)
    across = lax.broadcasted_iota(jnp.int32, (patches, patches), 1)
    down = lax.broadcasted_iota(jnp.int32, (patches, patches), 0)
    mask = (across >= start) & (across <= down)
    running = dot(mask.astype(f32), logd, precision=highest)
    return pos, conv_in, conv_out, step_raw, step, logd, mask, running


def head_decay(mask, running, running_t, h):
    return jnp.exp(
        jnp.where(mask, running[:, h : h + 1] - running_t[h : h + 1, :], large_negative)
    )


def mixer_fwd_kernel(
    lengths, normed, in_weight, conv_weight, conv_bias, step_bias, log_decay, skip, group_gain, out_weight,
    proj_out, y_out, low_out, part_out,
):
    projected = dot(normed[...], in_weight[...])
    proj_out[...] = projected
    _, _, conv_out, _, step, _, mask, running = mixer_state(
        lengths, projected, conv_weight[...], conv_bias[...], step_bias[...], log_decay[...]
    )
    act = conv_out * jax.nn.sigmoid(conv_out)
    inputs = act[:, GROUP_WIDTH : GROUP_WIDTH + STATE]
    outputs = act[:, GROUP_WIDTH + STATE :]
    inner = dot(outputs, inputs, ((1,), (1,)))
    running_t, step_t = running.T, step.T
    pair = 2 * HEAD_DIM
    lane = lax.broadcasted_iota(jnp.int32, (1, pair), 1)
    pieces = []
    for c in range(GROUP_WIDTH // pair):
        values = act[:, c * pair : (c + 1) * pair]
        got = []
        for h in (2 * c, 2 * c + 1):
            weights = head_decay(mask, running, running_t, h) * inner * step_t[h : h + 1, :]
            got.append(dot(weights, values))
        pieces.append(jnp.where(lane < HEAD_DIM, got[0], got[1]))
    y = jnp.concatenate(pieces, axis=1) + skip[...] * act[:, :GROUP_WIDTH]
    y_out[...] = y
    gate = projected[:, :GROUP_WIDTH]
    gated = y * (gate * jax.nn.sigmoid(gate))
    low = (gated * inv_rms(gated) * group_gain[...]).astype(bf16)
    low_out[...] = low
    part_out[...] = dot(low, out_weight[...])


def mixer_fwd(lengths, normed, in_weight, conv_weight, conv_bias, step_bias, log_decay, skip, group_gain, out_weight):
    patches, dim = normed.shape
    return pl.pallas_call(
        mixer_fwd_kernel,
        out_shape=(
            jax.ShapeDtypeStruct((patches, in_weight.shape[1]), f32),
            jax.ShapeDtypeStruct((patches, GROUP_WIDTH), f32),
            jax.ShapeDtypeStruct((patches, GROUP_WIDTH), bf16),
            jax.ShapeDtypeStruct((patches, dim), f32),
        ),
        in_specs=[SMEM] + [VMEM] * 9,
        out_specs=(VMEM,) * 4,
        compiler_params=plain_params(),
        name="mixer_fwd",
    )(lengths, normed, in_weight, conv_weight, conv_bias, step_bias, log_decay, skip, group_gain, out_weight)


def mixer_bwd_kernel(
    half, lengths, g_mixer, normed_half, projected_ref, y_ref, low_half, in_weight, conv_weight, conv_bias,
    step_bias, log_decay, skip, group_gain, out_weight,
    part_out, in_grad, out_grad, small,
):
    projected = projected_ref[...]
    pos, conv_in, conv_out, step_raw, step, logd, mask, running = mixer_state(
        lengths, projected, conv_weight[...], conv_bias[...], step_bias[...], log_decay[...]
    )
    act, act_slope = silu_pair(conv_out)
    inputs = act[:, GROUP_WIDTH : GROUP_WIDTH + STATE]
    outputs = act[:, GROUP_WIDTH + STATE :]
    inner = dot(outputs, inputs, ((1,), (1,)))
    running_t, step_t = running.T, step.T
    upstream = g_mixer[...]
    out_grad[...] = dot(low_half[...], upstream, ((0,), (0,))).astype(bf16)
    normed_grad = dot(upstream, out_weight[...], ((1,), (1,)))
    y = y_ref[...]
    gate = projected[:, :GROUP_WIDTH]
    gate_act, gate_slope = silu_pair(gate)
    gated_grad, gain_rows = rms_back(y * gate_act, group_gain[...], normed_grad)
    y_grad = gated_grad * gate_act
    gate_grad = gated_grad * y * gate_slope
    values = act[:, :GROUP_WIDTH]
    skip_cols = jnp.sum(y_grad * values, axis=0, keepdims=True)
    pair = 2 * HEAD_DIM
    lane = lax.broadcasted_iota(jnp.int32, (1, pair), 1)
    inner_grad = jnp.zeros_like(inner)
    value_pieces, row_sums, col_sums = [], [], []
    for c in range(GROUP_WIDTH // pair):
        at = slice(c * pair, (c + 1) * pair)
        got = []
        for h in (2 * c, 2 * c + 1):
            own = (lane < HEAD_DIM) if h % 2 == 0 else (lane >= HEAD_DIM)
            mine = jnp.where(own, y_grad[:, at], 0.0)
            decay = head_decay(mask, running, running_t, h)
            step_row = step_t[h : h + 1, :]
            weight_grad = dot(mine, values[:, at], ((1,), (1,))) * decay
            scaled = weight_grad * step_row
            inner_grad = inner_grad + scaled
            col_sums.append(jnp.sum(weight_grad * inner, axis=0, keepdims=True))
            row_sums.append(jnp.sum(scaled * inner, axis=1, keepdims=True))
            weights = decay * inner * step_row
            got.append(dot(weights, mine, ((0,), (0,))))
        value_pieces.append(got[0] + got[1])
    values_grad = jnp.concatenate(value_pieces, axis=1) + skip[...] * y_grad
    inputs_grad = dot(inner_grad, outputs, ((0,), (0,)))
    outputs_grad = dot(inner_grad, inputs)
    col_grad = jnp.concatenate(col_sums, axis=0).T
    running_grad = jnp.concatenate(row_sums, axis=1) - col_grad * step
    logd_grad = dot(mask.astype(f32), running_grad, ((0,), (0,)), precision=highest)
    step_grad = (col_grad - logd_grad * jnp.exp(log_decay[...])) * jax.nn.sigmoid(step_raw)
    conv_grad = jnp.concatenate([values_grad, inputs_grad, outputs_grad], axis=1) * act_slope
    patches = projected.shape[0]
    conv_in_grad = jnp.zeros_like(conv_grad)
    small[...] = jnp.zeros_like(small)
    for lag in range(CONV):
        small[CONV - 1 - lag : CONV - lag, :] = jnp.sum(
            conv_grad * conv_taps(conv_in, pos, lag), axis=0, keepdims=True
        )
        kept = jnp.where(pos >= lag, conv_grad, 0.0) * conv_weight[CONV - 1 - lag][None]
        conv_in_grad = conv_in_grad + (kept if lag == 0 else pltpu.roll(kept, patches - lag, 0))
    small[CONV : CONV + 1, :] = jnp.sum(conv_grad, axis=0, keepdims=True)
    small[CONV + 1 : CONV + 2, :GROUP_WIDTH] = jnp.sum(gain_rows, axis=0, keepdims=True)
    small[CONV + 2 : CONV + 3, :GROUP_WIDTH] = skip_cols
    small[CONV + 3 : CONV + 4, :GROUP_HEADS] = jnp.sum(step_grad, axis=0, keepdims=True)
    small[CONV + 4 : CONV + 5, :GROUP_HEADS] = jnp.sum(logd_grad * logd, axis=0, keepdims=True)
    proj_grad = jnp.concatenate([gate_grad, conv_in_grad, step_grad], axis=1).astype(bf16)
    in_grad[...] = dot(normed_half[...], proj_grad, ((0,), (0,))).astype(bf16)
    part_out[...] = dot(proj_grad, in_weight[...], ((1,), (1,)))


def mixer_bwd(
    lengths, g_mixer, normed_half, projected, y, low_half, in_weight, conv_weight, conv_bias,
    step_bias, log_decay, skip, group_gain, out_weight,
):
    patches, dim = g_mixer.shape
    return pl.pallas_call(
        partial(mixer_bwd_kernel, None),
        out_shape=(
            jax.ShapeDtypeStruct((patches, dim), f32),
            jax.ShapeDtypeStruct((normed_half.shape[1], in_weight.shape[1]), bf16),
            jax.ShapeDtypeStruct((low_half.shape[1], dim), bf16),
            jax.ShapeDtypeStruct((16, CONV_CH), f32),
        ),
        in_specs=[SMEM] + [VMEM] * 13,
        out_specs=(VMEM,) * 4,
        compiler_params=plain_params(),
        name="mixer_bwd",
    )(
        lengths, g_mixer, normed_half, projected, y, low_half, in_weight, conv_weight, conv_bias,
        step_bias, log_decay, skip, group_gain, out_weight,
    )


def to_owner_greet(barrier, n, mpn, i, j):
    reps = n // mpn
    inside = i // reps == j
    for s in range(mpn):
        @pl.when(jnp.logical_not(inside & (s == j)))
        def _():
            greet(barrier, j * reps + i % reps, s)
    return n // reps - inside.astype(jnp.int32)


def to_owner_copy(n, mpn, i, j, q, part, recv, ss, rs):
    reps = n // mpn
    block = q * reps + i % reps
    return rcopy(part.at[block], recv.at[j], ss.at[q], rs.at[j], block, i // reps)


def to_owner_start(n, mpn, i, j, part, recv, ss, rs):
    reps = n // mpn
    m = i // reps
    for q in range(n // reps):
        block = q * reps + i % reps

        @pl.when(jnp.logical_not((block == i) & (m == j)))
        def _():
            to_owner_copy(n, mpn, i, j, q, part, recv, ss, rs).start()

    @pl.when(m == j)
    def _():
        recv[j] = part[i]


def to_owner_recv(n, mpn, i, j, part, recv, ss, rs):
    reps = n // mpn
    for s in range(mpn):
        @pl.when(jnp.logical_not((i // reps == j) & (s == j)))
        def _():
            rcopy(part.at[0], recv.at[s], ss.at[0], rs.at[s], j * reps + i % reps, s).wait_recv()


def to_owner_sent(n, mpn, i, j, part, recv, ss, rs):
    reps = n // mpn
    for q in range(n // reps):
        @pl.when(jnp.logical_not((q * reps + i % reps == i) & (i // reps == j)))
        def _():
            to_owner_copy(n, mpn, i, j, q, part, recv, ss, rs).wait_send()


def mix_out_kernel(n, mpn, part, global_in, all_out, recv, own, everyone, ss1, rs1, ss2, rs2):
    i, j = lax.axis_index("dp"), lax.axis_index("mp")
    barrier = pltpu.get_barrier_semaphore()
    count = to_owner_greet(barrier, n, mpn, i, j)
    for d in range(1, mpn):
        greet(barrier, i, (j + d) % mpn)
    pl.semaphore_wait(barrier, mpn - 1 + count)
    to_owner_start(n, mpn, i, j, part, recv, ss1, rs1)
    to_owner_recv(n, mpn, i, j, part, recv, ss1, rs1)
    total = global_in[...]
    for s in range(mpn):
        total = total + recv[s]
    own[...] = total
    everyone[j] = total
    copies = []
    for d in range(1, mpn):
        t = (j + d) % mpn
        copy = rcopy(own, everyone.at[j], ss2.at[t], rs2.at[j], i, t)
        copy.start()
        copies.append(copy)
    for d in range(1, mpn):
        s = (j + d) % mpn
        rcopy(own, everyone.at[s], ss2.at[s], rs2.at[s], i, s).wait_recv()
    all_out[...] = everyone[...]
    to_owner_sent(n, mpn, i, j, part, recv, ss1, rs1)
    for copy in copies:
        copy.wait_send()


def mix_out(n, mpn, part, global_in):
    rows, dim = global_in.shape
    return pl.pallas_call(
        partial(mix_out_kernel, n, mpn),
        out_shape=jax.ShapeDtypeStruct((mpn, rows, dim), f32),
        in_specs=[VMEM] * 2,
        out_specs=VMEM,
        scratch_shapes=[
            pltpu.VMEM((mpn, rows, dim), f32),
            pltpu.VMEM((rows, dim), f32),
            pltpu.VMEM((mpn, rows, dim), f32),
            DMA((mpn,)),
            DMA((mpn,)),
            DMA((mpn,)),
            DMA((mpn,)),
        ],
        compiler_params=remote_params(1),
        name="mix_out",
    )(part, global_in)


def slab_rows(bytes_ref, m, patch_out, k, dim):
    return bytes_ref[m, :, k * dim : (k + 1) * dim].astype(f32) + patch_out


def att_mask(rows, patches):
    across = lax.broadcasted_iota(jnp.int32, (rows, rows), 1)
    down = lax.broadcasted_iota(jnp.int32, (rows, rows), 0)
    return (across % patches == down % patches) & (across <= down)


def att_fwd_kernel(bytes_in, patch_out, gain, qkv_weight, out_weight, attn_in, qkv_out, heads_out, part):
    micro, patches, cols = bytes_in.shape
    dim = gain.shape[1]
    slabs = cols // dim
    rows = slabs * patches
    width = qkv_weight.shape[2]
    mask = att_mask(rows, patches)
    pair = 2 * ATT_DIM
    lane = lax.broadcasted_iota(jnp.int32, (1, pair), 1)

    def step(m, _):
        for k in range(slabs):
            here = slab_rows(bytes_in, m, patch_out[m], k, dim)
            attn_in[m, k * patches : (k + 1) * patches, :] = (
                here * inv_rms(here) * gain[...]
            ).astype(bf16)
        got = attn_in[m]
        for w in range(3):
            qkv_out[w, m] = dot(got, qkv_weight[w]).astype(bf16)
        for c in range(width // pair):
            at = slice(c * pair, (c + 1) * pair)
            query, key, value = qkv_out[0, m, :, at], qkv_out[1, m, :, at], qkv_out[2, m, :, at]
            res = []
            for own in (lane < ATT_DIM, lane >= ATT_DIM):
                mine = jnp.where(own, query, jnp.zeros_like(query))
                scores = dot(mine, key, ((1,), (1,))) * ATT_DIM ** (-0.5)
                scores = jnp.where(mask, scores, large_negative)
                probs = jnp.exp(scores - jnp.max(scores, axis=1, keepdims=True))
                probs = probs / jnp.sum(probs, axis=1, keepdims=True)
                res.append(dot(probs.astype(bf16), value))
            heads_out[m, :, at] = jnp.where(lane < ATT_DIM, res[0], res[1]).astype(bf16)
        part[m] = dot(heads_out[m], out_weight[...]).astype(bf16)
        return 0

    lax.fori_loop(0, micro, step, 0)


def att_fwd(bytes_in, patch_out, gain, qkv_weight, out_weight):
    micro, patches, cols = bytes_in.shape
    dim, width = qkv_weight.shape[1:]
    rows = patches * (cols // dim)
    return pl.pallas_call(
        att_fwd_kernel,
        out_shape=(
            jax.ShapeDtypeStruct((micro, rows, dim), bf16),
            jax.ShapeDtypeStruct((3, micro, rows, width), bf16),
            jax.ShapeDtypeStruct((micro, rows, width), bf16),
            jax.ShapeDtypeStruct((micro, rows, dim), bf16),
        ),
        in_specs=[VMEM] * 5,
        out_specs=(VMEM,) * 4,
        compiler_params=plain_params(),
        name="att_fwd",
    )(bytes_in, patch_out, gain, qkv_weight, out_weight)


def att_bwd_kernel(branch, attn_in, qkv, heads, qkv_weight, out_weight, part, qkv_grad, out_grad, low):
    micro, rows, dim = branch.shape
    width = out_weight.shape[0]
    patches = rows // 8
    mask = att_mask(rows, patches)
    pair = 2 * ATT_DIM
    lane = lax.broadcasted_iota(jnp.int32, (1, pair), 1)

    def step(m, _):
        heads_grad = dot(branch[m], out_weight[...], ((1,), (1,)))
        for c in range(width // pair):
            at = slice(c * pair, (c + 1) * pair)
            query, key, value = qkv[0, m, :, at], qkv[1, m, :, at], qkv[2, m, :, at]
            up = heads_grad[:, at].astype(bf16)
            got = [[], [], []]
            for own in (lane < ATT_DIM, lane >= ATT_DIM):
                mine = jnp.where(own, query, jnp.zeros_like(query))
                scores = dot(mine, key, ((1,), (1,))) * ATT_DIM ** (-0.5)
                scores = jnp.where(mask, scores, large_negative)
                probs = jnp.exp(scores - jnp.max(scores, axis=1, keepdims=True))
                probs = probs / jnp.sum(probs, axis=1, keepdims=True)
                my_up = jnp.where(own, up, jnp.zeros_like(up))
                probs_grad = dot(my_up, value, ((1,), (1,)))
                inner = jnp.sum(probs * probs_grad, axis=1, keepdims=True)
                score_grad = (probs * (probs_grad - inner) * ATT_DIM ** (-0.5)).astype(bf16)
                got[0].append(dot(score_grad, key))
                got[1].append(dot(score_grad, mine, ((0,), (0,))))
                got[2].append(dot(probs.astype(bf16), my_up, ((0,), (0,))))
            low[0, m, :, at] = jnp.where(lane < ATT_DIM, got[0][0], got[0][1]).astype(bf16)
            low[1, m, :, at] = (got[1][0] + got[1][1]).astype(bf16)
            low[2, m, :, at] = (got[2][0] + got[2][1]).astype(bf16)
        total = dot(low[0, m], qkv_weight[0], ((1,), (1,)))
        total = total + dot(low[1, m], qkv_weight[1], ((1,), (1,)))
        total = total + dot(low[2, m], qkv_weight[2], ((1,), (1,)))
        part[m] = total.astype(bf16)
        return 0

    lax.fori_loop(0, micro, step, 0)
    everything = attn_in[...].reshape(micro * rows, dim)
    for w in range(3):
        qkv_grad[w] = dot(everything, low[w].reshape(micro * rows, width), ((0,), (0,))).astype(bf16)
    out_grad[...] = dot(
        heads[...].reshape(micro * rows, width), branch[...].reshape(micro * rows, dim), ((0,), (0,))
    ).astype(bf16)


def att_bwd(branch, attn_in, qkv, heads, qkv_weight, out_weight):
    micro, rows, dim = branch.shape
    width = out_weight.shape[0]
    return pl.pallas_call(
        att_bwd_kernel,
        out_shape=(
            jax.ShapeDtypeStruct((micro, rows, dim), bf16),
            jax.ShapeDtypeStruct((3, dim, width), bf16),
            jax.ShapeDtypeStruct((width, dim), bf16),
        ),
        in_specs=[VMEM] * 6,
        out_specs=(VMEM,) * 3,
        scratch_shapes=[pltpu.VMEM((3, micro, rows, width), bf16)],
        compiler_params=plain_params(),
        name="att_bwd",
    )(branch, attn_in, qkv, heads, qkv_weight, out_weight)


def after_att_kernel(
    n, mpn, part, own_bytes, patch_out, gain, after_out, all_out, recv, low, everyone, ss1, rs1, ss2, rs2, ss3,
):
    i, j = lax.axis_index("dp"), lax.axis_index("mp")
    c, mine = i % 2, i // 2
    other = i + 1 - 2 * c
    barrier = pltpu.get_barrier_semaphore()
    for d in range(1, mpn):
        greet(barrier, i, (j + d) % mpn)
    greet(barrier, other, j)
    for d in range(1, n // 2):
        greet(barrier, (mine + d) % (n // 2) * 2 + c, j)
    pl.semaphore_wait(barrier, mpn - 1 + n // 2)
    copies = []
    for d in range(1, mpn):
        t = (j + d) % mpn
        copy = rcopy(part.at[t], recv.at[j], ss1.at[t], rs1.at[j], i, t)
        copy.start()
        copies.append(copy)
    patches, dim = patch_out.shape
    for k in range(part.shape[1] // patches):
        rows = slice(k * patches, (k + 1) * patches)
        after_out[rows, :] = (
            own_bytes[:, k * dim : (k + 1) * dim].astype(f32) + patch_out[...] + part[j, rows, :].astype(f32)
        )
    for d in range(1, mpn):
        s = (j + d) % mpn
        rcopy(part.at[s], recv.at[s], ss1.at[s], rs1.at[s], i, s).wait_recv()
        after_out[...] += recv[s].astype(f32)
    after = after_out[...]
    low[...] = (after * inv_rms(after) * gain[...]).astype(bf16)
    for d in range(1, n // 2):
        q = (mine + d) % (n // 2)
        copy = rcopy(low, everyone.at[i], ss2.at[q], rs2.at[i], q * 2 + c, j)
        copy.start()
        copies.append(copy)
    copy = rcopy(low, everyone.at[i], ss3.at[mine], rs2.at[i], other, j)
    copy.start()
    copies.append(copy)
    everyone[i] = low[...]
    for d in range(1, n // 2):
        q = (mine + n // 2 - d) % (n // 2)
        s = q * 2 + c
        rcopy(low, everyone.at[s], ss2.at[q], rs2.at[s], s, j).wait_recv()
        copy = rcopy(everyone.at[s], everyone.at[s], ss3.at[q], rs2.at[s], other, j)
        copy.start()
        copies.append(copy)
    for q in range(n // 2):
        s = q * 2 + 1 - c
        rcopy(low, everyone.at[s], ss3.at[q], rs2.at[s], other, j).wait_recv()
    all_out[...] = everyone[...]
    for copy in copies:
        copy.wait_send()


def after_att(n, mpn, part, own_bytes, patch_out, gain):
    _, rows, dim = part.shape
    return pl.pallas_call(
        partial(after_att_kernel, n, mpn),
        out_shape=(
            jax.ShapeDtypeStruct((rows, dim), f32),
            jax.ShapeDtypeStruct((n, rows, dim), bf16),
        ),
        in_specs=[VMEM] * 4,
        out_specs=(VMEM, VMEM),
        scratch_shapes=[
            pltpu.VMEM((mpn, rows, dim), bf16),
            pltpu.VMEM((rows, dim), bf16),
            pltpu.VMEM((n, rows, dim), bf16),
            DMA((mpn,)),
            DMA((mpn,)),
            DMA((n // 2,)),
            DMA((n,)),
            DMA((n // 2,)),
        ],
        compiler_params=remote_params(2),
        name="after_att",
    )(part, own_bytes, patch_out, gain)


def ffn_kernel(rows_in, grads_in, weight, down_out, in_grad, weight_grad, gate_low, up_low, hidden_low):
    blocks, rows, dim = rows_in.shape

    def step(b, _):
        here, up = rows_in[b], grads_in[b]
        gate = dot(here, weight[0])
        other = dot(here, weight[1])
        act, slope = silu_pair(gate)
        hidden = (act * other).astype(bf16)
        hidden_low[b] = hidden
        down_out[b] = dot(hidden, weight[2], ((1,), (1,))).astype(bf16)
        hidden_grad = dot(up, weight[2])
        gate_grad = (hidden_grad * other * slope).astype(bf16)
        up_grad = (hidden_grad * act).astype(bf16)
        gate_low[b] = gate_grad
        up_low[b] = up_grad
        back = dot(gate_grad, weight[0], ((1,), (1,))) + dot(up_grad, weight[1], ((1,), (1,)))
        in_grad[b] = back.astype(bf16)
        return 0

    lax.fori_loop(0, blocks, step, 0)
    hidden = weight.shape[2]
    everything = rows_in[...].reshape(blocks * rows, dim)
    weight_grad[0] = dot(everything, gate_low[...].reshape(blocks * rows, hidden), ((0,), (0,))).astype(bf16)
    weight_grad[1] = dot(everything, up_low[...].reshape(blocks * rows, hidden), ((0,), (0,))).astype(bf16)
    weight_grad[2] = dot(
        grads_in[...].reshape(blocks * rows, dim), hidden_low[...].reshape(blocks * rows, hidden), ((0,), (0,))
    ).astype(bf16)


def ffn(rows_in, grads_in, weight):
    blocks, rows, dim = rows_in.shape
    hidden = weight.shape[2]
    return pl.pallas_call(
        ffn_kernel,
        out_shape=(
            jax.ShapeDtypeStruct((blocks, rows, dim), bf16),
            jax.ShapeDtypeStruct((blocks, rows, dim), bf16),
            jax.ShapeDtypeStruct((3, dim, hidden), bf16),
        ),
        in_specs=[VMEM] * 3,
        out_specs=(VMEM,) * 3,
        scratch_shapes=[pltpu.VMEM((blocks, rows, hidden), bf16)] * 3,
        compiler_params=plain_params(60),
        name="ffn",
    )(rows_in, grads_in, weight)


def ffn_back_kernel(
    n, mpn, in_part, down_part, after_ref, own_grad, valid, gain,
    after_grad_out, branch_out, block_out, gain_out,
    pre, held, recv, branch, ssa, rsa, ssb, rsb, ss2, rs2,
):
    i, j = lax.axis_index("dp"), lax.axis_index("mp")
    c, mine = i % 2, i // 2
    other = i + 1 - 2 * c
    half = n // 2
    barrier = pltpu.get_barrier_semaphore()
    for d in range(1, mpn):
        greet(barrier, i, (j + d) % mpn)
    greet(barrier, other, j)
    for d in range(1, half):
        greet(barrier, (mine + d) % half * 2 + c, j)
    pl.semaphore_wait(barrier, mpn - 1 + half)
    copies = []
    for w, part in enumerate((in_part, down_part)):
        for d in range(1, half + 1):
            q = (mine + d) % half
            copy = rcopy(part.at[q * 2 + 1 - c], pre.at[w, q], ssa.at[w, q], rsa.at[w, q], other, j)
            copy.start()
            copies.append(copy)

    def spread(w, part):
        for d in range(1, half):
            q = (mine + d) % half
            rcopy(part.at[0], pre.at[w, q], ssa.at[w, q], rsa.at[w, q], other, j).wait_recv()
            held[w, q] = (part[q * 2 + c].astype(f32) + pre[w, q].astype(f32)).astype(bf16)
            copy = rcopy(held.at[w, q], recv.at[w, mine], ssb.at[w, q], rsb.at[w, mine], q * 2 + c, j)
            copy.start()
            copies.append(copy)

    def gathered(w, part):
        rcopy(part.at[0], pre.at[w, mine], ssa.at[w, mine], rsa.at[w, mine], other, j).wait_recv()
        total = part[i].astype(f32) + pre[w, mine].astype(f32)
        for d in range(1, half):
            q = (mine + d) % half
            rcopy(held.at[w, q], recv.at[w, q], ssb.at[w, q], rsb.at[w, q], q * 2 + c, j).wait_recv()
            total = total + recv[w, q].astype(f32)
        return total

    spread(0, in_part)
    after = after_ref[...]
    back, gain_rows = rms_back(after, gain[...], gathered(0, in_part))
    after_grad = own_grad[...].astype(f32) + back
    after_grad_out[...] = after_grad
    branch[j] = after_grad.astype(bf16)
    for d in range(1, mpn):
        t = (j + d) % mpn
        copy = rcopy(branch.at[j], branch.at[j], ss2.at[t], rs2.at[j], i, t)
        copy.start()
        copies.append(copy)
    spread(1, down_part)
    gain_out[...] = jnp.sum(gain_rows, axis=0, keepdims=True)
    block_out[...] = ((after_ref[...] + gathered(1, down_part)) * valid[...]).astype(bf16)
    for d in range(1, mpn):
        s = (j + d) % mpn
        rcopy(branch.at[s], branch.at[s], ss2.at[s], rs2.at[s], i, s).wait_recv()
    branch_out[...] = branch[...]
    for copy in copies:
        copy.wait_send()


def ffn_back(n, mpn, in_part, down_part, after, own_grad, valid, gain):
    _, rows, dim = in_part.shape
    half = n // 2
    return pl.pallas_call(
        partial(ffn_back_kernel, n, mpn),
        out_shape=(
            jax.ShapeDtypeStruct((rows, dim), f32),
            jax.ShapeDtypeStruct((mpn, rows, dim), bf16),
            jax.ShapeDtypeStruct((rows, dim), bf16),
            jax.ShapeDtypeStruct((1, dim), f32),
        ),
        in_specs=[VMEM] * 6,
        out_specs=(VMEM,) * 4,
        scratch_shapes=[
            pltpu.VMEM((2, half, rows, dim), bf16),
            pltpu.VMEM((2, half, rows, dim), bf16),
            pltpu.VMEM((2, half, rows, dim), bf16),
            pltpu.VMEM((mpn, rows, dim), bf16),
            DMA((2, half)),
            DMA((2, half)),
            DMA((2, half)),
            DMA((2, half)),
            DMA((mpn,)),
            DMA((mpn,)),
        ],
        compiler_params=remote_params(3, 58),
        name="ffn_back",
    )(in_part, down_part, after, own_grad, valid, gain)


def att_back_kernel(
    n, mpn, part, own_bytes, patch_out, after_grad, block_low, gain,
    local_out, block_out, global_out, mixer_out, gain_out,
    recv, local, local_in, local_all, block_all, low, mixer, ss1, rs1, ss2, rs2, ss3, rs3, ss4, rs4,
):
    i, j = lax.axis_index("dp"), lax.axis_index("mp")
    reps = n // mpn
    m = i // reps
    inside = m == j
    barrier = pltpu.get_barrier_semaphore()
    for d in range(1, mpn):
        greet(barrier, i, (j + d) % mpn)
    for s in range(n):
        @pl.when(jnp.logical_not((s == i) & inside))
        def _():
            greet(barrier, s, m)
    pl.semaphore_wait(barrier, mpn - 1 + reps * mpn - inside.astype(jnp.int32))
    copies = []
    for d in range(1, mpn):
        t = (j + d) % mpn
        copy = rcopy(part.at[t], recv.at[j], ss1.at[t], rs1.at[j], i, t)
        copy.start()
        copies.append(copy)
    for d in range(1, mpn):
        t = (j + d) % mpn
        copy = rcopy(block_low.at[t], block_all.at[j], ss3.at[t], rs3.at[j], i, t)
        copy.start()
        copies.append(copy)
    block_all[j] = block_low[j]
    patches, dim = patch_out.shape
    rows_all = part.shape[1]
    slabs = rows_all // patches
    for k in range(slabs):
        rows = slice(k * patches, (k + 1) * patches)
        local_in[rows, :] = own_bytes[:, k * dim : (k + 1) * dim].astype(f32) + patch_out[...]
    total = part[j].astype(f32)
    for d in range(1, mpn):
        s = (j + d) % mpn
        rcopy(part.at[s], recv.at[s], ss1.at[s], rs1.at[s], i, s).wait_recv()
        total = total + recv[s].astype(f32)
    back, gain_rows = rms_back(local_in[...], gain[...], total)
    local_grad = after_grad[...] + back
    global_grad = local_grad[:patches]
    for k in range(1, slabs):
        global_grad = global_grad + local_grad[k * patches : (k + 1) * patches]
    global_out[...] = global_grad
    low[...] = global_grad.astype(bf16)
    for h in range(reps):
        for t in range(mpn):
            q = h * mpn + t
            here = (j * reps + h == i) & (t == j)

            @pl.when(jnp.logical_not(here))
            def _():
                rcopy(low, mixer.at[i], ss2.at[q], rs2.at[i], j * reps + h, t).start()

            @pl.when(here)
            def _():
                mixer[i] = low[...]
    per = rows_all // mpn
    for t in range(mpn):
        local[t] = local_grad[t * per : (t + 1) * per].astype(bf16)
    for d in range(1, mpn):
        t = (j + d) % mpn
        copy = rcopy(local.at[t], local_all.at[j], ss4.at[t], rs4.at[j], i, t)
        copy.start()
        copies.append(copy)
    local_all[j] = local[j]
    gain_out[...] = jnp.sum(gain_rows, axis=0, keepdims=True)
    for s in range(n):
        @pl.when(jnp.logical_not((s == i) & inside))
        def _():
            rcopy(low, mixer.at[s], ss2.at[0], rs2.at[s], s, m).wait_recv()
    mixer_out[...] = mixer[...]
    for d in range(1, mpn):
        s = (j + d) % mpn
        rcopy(block_low.at[s], block_all.at[s], ss3.at[s], rs3.at[s], i, s).wait_recv()
        rcopy(local.at[s], local_all.at[s], ss4.at[s], rs4.at[s], i, s).wait_recv()
    block_out[...] = block_all[...]
    local_out[...] = local_all[...]
    for copy in copies:
        copy.wait_send()
    for h in range(reps):
        for t in range(mpn):
            q = h * mpn + t

            @pl.when(jnp.logical_not((j * reps + h == i) & (t == j)))
            def _():
                rcopy(low, mixer.at[i], ss2.at[q], rs2.at[i], j * reps + h, t).wait_send()


def att_back(n, mpn, part, own_bytes, patch_out, after_grad, block_low, gain):
    _, rows, dim = part.shape
    patches = patch_out.shape[0]
    reps = n // mpn
    cols = block_low.shape[2]
    return pl.pallas_call(
        partial(att_back_kernel, n, mpn),
        out_shape=(
            jax.ShapeDtypeStruct((mpn, rows // mpn, dim), bf16),
            jax.ShapeDtypeStruct((mpn, rows, cols), bf16),
            jax.ShapeDtypeStruct((patches, dim), f32),
            jax.ShapeDtypeStruct((n, patches, dim), bf16),
            jax.ShapeDtypeStruct((1, dim), f32),
        ),
        in_specs=[VMEM] * 6,
        out_specs=(VMEM,) * 5,
        scratch_shapes=[
            pltpu.VMEM((mpn, rows, dim), bf16),
            pltpu.VMEM((mpn, rows // mpn, dim), bf16),
            pltpu.VMEM((rows, dim), f32),
            pltpu.VMEM((mpn, rows // mpn, dim), bf16),
            pltpu.VMEM((mpn, rows, cols), bf16),
            pltpu.VMEM((patches, dim), bf16),
            pltpu.VMEM((n, patches, dim), bf16),
            DMA((mpn,)),
            DMA((mpn,)),
            DMA((reps * mpn,)),
            DMA((n,)),
            DMA((mpn,)),
            DMA((mpn,)),
            DMA((mpn,)),
            DMA((mpn,)),
        ],
        compiler_params=remote_params(4),
        name="att_back",
    )(part, own_bytes, patch_out, after_grad, block_low, gain)


def mix_back_kernel(
    n, mpn, part, global_in, global_grad, gain, in_part, out_part, small_part, gains_part,
    all_out, in_out, out_out, small_out, gains_out,
    recv, line, plane, in_recv, out_recv, small_recv, gains_held, gains_line, gains_plane, gains_pair,
    ss1, rs1, ss2, rs2, ss3, rs3, ss4, ssi, rsi, sso, rso, sss, rss, ssg, rsg, ssh, rsh, ssp, rsp,
):
    i, j = lax.axis_index("dp"), lax.axis_index("mp")
    reps = n // mpn
    m, h = i // reps, i % reps
    share = n // reps
    c, mine = i % 2, i // 2
    other = i + 1 - 2 * c
    half = n // 2
    group = i // share
    barrier = pltpu.get_barrier_semaphore()
    count = to_owner_greet(barrier, n, mpn, i, j)
    for d in range(1, mpn):
        greet(barrier, i, (j + d) % mpn)
    greet(barrier, other, j)
    for d in range(1, half):
        greet(barrier, (mine + d) % half * 2 + c, j)
    for t in range(mpn):
        @pl.when(t * reps + group != i)
        def _():
            greet(barrier, t * reps + group, j)
    self_share = (group == h).astype(jnp.int32)
    pl.semaphore_wait(barrier, count + mpn - 1 + half + share - self_share)
    to_owner_start(n, mpn, i, j, part, recv, ss1, rs1)

    bundles = (
        (in_part, in_recv, ssi, rsi),
        (out_part, out_recv, sso, rso),
        (small_part, small_recv, sss, rss),
    )

    def bundle_copy(src, dst, ss, rs, e):
        source = src if src is small_part else src.at[e]
        return rcopy(source, dst.at[m], ss.at[e], rs.at[m], h * share + e, j)

    for e in range(share):
        @pl.when(h * share + e != i)
        def _():
            for src, dst, ss, rs in bundles:
                bundle_copy(src, dst, ss, rs, e).start()

        @pl.when(h * share + e == i)
        def _():
            for src, dst, ss, rs in bundles:
                dst[m] = src[...] if src is small_part else src[e]

    to_owner_recv(n, mpn, i, j, part, recv, ss1, rs1)
    total = recv[0]
    for s in range(1, mpn):
        total = total + recv[s]
    back, gain_rows = rms_back(global_in[...], gain[...], total)
    line[j] = (global_grad[...] + back).astype(bf16)
    copies = []
    for d in range(1, mpn):
        t = (j + d) % mpn
        copy = rcopy(line.at[j], line.at[j], ss2.at[t], rs2.at[j], i, t)
        copy.start()
        copies.append(copy)
    gains_held[...] = gains_part[...]
    gains_held[0:1, :] = jnp.sum(gain_rows, axis=0, keepdims=True)
    gains_line[j] = gains_held[...]
    for d in range(1, mpn):
        t = (j + d) % mpn
        copy = rcopy(gains_held, gains_line.at[j], ssg.at[t], rsg.at[j], i, t)
        copy.start()
        copies.append(copy)
    for d in range(1, mpn):
        s = (j + d) % mpn
        rcopy(line.at[s], line.at[s], ss2.at[s], rs2.at[s], i, s).wait_recv()
    for d in range(1, half):
        q = (mine + d) % half
        copy = rcopy(line, plane.at[i], ss3.at[q], rs3.at[i], q * 2 + c, j)
        copy.start()
        copies.append(copy)
    copy = rcopy(line, plane.at[i], ss4.at[mine], rs3.at[i], other, j)
    copy.start()
    copies.append(copy)
    plane[i] = line[...]
    for d in range(1, mpn):
        s = (j + d) % mpn
        rcopy(gains_held, gains_line.at[s], ssg.at[s], rsg.at[s], i, s).wait_recv()
    gains_plane[mine] = sum(gains_line[s] for s in range(mpn))
    for d in range(1, half):
        q = (mine + d) % half
        copy = rcopy(gains_plane.at[mine], gains_plane.at[mine], ssh.at[q], rsh.at[mine], q * 2 + c, j)
        copy.start()
        copies.append(copy)
    for d in range(1, half):
        q = (mine + half - d) % half
        s = q * 2 + c
        rcopy(line, plane.at[s], ss3.at[q], rs3.at[s], s, j).wait_recv()
        copy = rcopy(plane.at[s], plane.at[s], ss4.at[q], rs3.at[s], other, j)
        copy.start()
        copies.append(copy)
    for d in range(1, half):
        q = (mine + d) % half
        rcopy(gains_plane.at[q], gains_plane.at[q], ssh.at[q], rsh.at[q], q * 2 + c, j).wait_recv()
    gains_pair[0] = sum(gains_plane[s] for s in range(half))
    copy = rcopy(gains_pair.at[0], gains_pair.at[1], ssp.at[0], rsp.at[0], other, j)
    copy.start()
    copies.append(copy)
    for q in range(half):
        s = q * 2 + 1 - c
        rcopy(line, plane.at[s], ss4.at[q], rs3.at[s], other, j).wait_recv()
    all_out[...] = plane[...]
    for t in range(mpn):
        @pl.when(t * reps + group != i)
        def _():
            for src, dst, ss, rs in bundles:
                source = src if src is small_part else src.at[0]
                rcopy(source, dst.at[t], ss.at[0], rs.at[t], t * reps + group, j).wait_recv()
    in_out[...] = sum(in_recv[t].astype(f32) for t in range(mpn))
    out_out[...] = sum(out_recv[t].astype(f32) for t in range(mpn))
    small_out[...] = sum(small_recv[t] for t in range(mpn))
    rcopy(gains_pair.at[0], gains_pair.at[1], ssp.at[0], rsp.at[0], other, j).wait_recv()
    gains_out[...] = gains_pair[0] + gains_pair[1]
    to_owner_sent(n, mpn, i, j, part, recv, ss1, rs1)
    for copy in copies:
        copy.wait_send()
    for e in range(share):
        @pl.when(h * share + e != i)
        def _():
            for src, dst, ss, rs in bundles:
                bundle_copy(src, dst, ss, rs, e).wait_send()


def mix_back(n, mpn, part, global_in, global_grad, gain, in_part, out_part, small_part, gains_part):
    rows, dim = global_in.shape
    half, share = n // 2, mpn
    return pl.pallas_call(
        partial(mix_back_kernel, n, mpn),
        out_shape=(
            jax.ShapeDtypeStruct((n, mpn, rows, dim), bf16),
            jax.ShapeDtypeStruct(in_part.shape[1:], f32),
            jax.ShapeDtypeStruct(out_part.shape[1:], f32),
            jax.ShapeDtypeStruct(small_part.shape, f32),
            jax.ShapeDtypeStruct(gains_part.shape, f32),
        ),
        in_specs=[VMEM] * 8,
        out_specs=(VMEM,) * 5,
        scratch_shapes=[
            pltpu.VMEM((mpn, rows, dim), f32),
            pltpu.VMEM((mpn, rows, dim), bf16),
            pltpu.VMEM((n, mpn, rows, dim), bf16),
            pltpu.VMEM((mpn,) + in_part.shape[1:], bf16),
            pltpu.VMEM((mpn,) + out_part.shape[1:], bf16),
            pltpu.VMEM((mpn,) + small_part.shape, f32),
            pltpu.VMEM(gains_part.shape, f32),
            pltpu.VMEM((mpn,) + gains_part.shape, f32),
            pltpu.VMEM((half,) + gains_part.shape, f32),
            pltpu.VMEM((2,) + gains_part.shape, f32),
            DMA((mpn,)), DMA((mpn,)),
            DMA((mpn,)), DMA((mpn,)),
            DMA((half,)), DMA((n,)),
            DMA((half,)),
            DMA((share,)), DMA((mpn,)),
            DMA((share,)), DMA((mpn,)),
            DMA((share,)), DMA((mpn,)),
            DMA((mpn,)), DMA((mpn,)),
            DMA((half,)), DMA((half,)),
            DMA((1,)), DMA((1,)),
        ],
        compiler_params=remote_params(5),
        name="mix_back",
    )(part, global_in, global_grad, gain, in_part, out_part, small_part, gains_part)


def patch_back_kernel(everyone, own, bytes_part, weight, local, weight_grad, input_grad):
    weight_grad[...] = dot(bytes_part[...], everyone[...], ((0,), (0,)))
    piece = dot(own[...], weight[...], ((1,), (1,)))
    micro, positions, patches, dim = local.shape
    for m in range(micro):
        for k in range(positions):
            input_grad[m, :, k * dim : (k + 1) * dim] = (
                piece[m * patches : (m + 1) * patches, k * dim : (k + 1) * dim]
                + local[m, k].astype(f32)
            )


def patch_back(everyone, own, bytes_part, weight, local):
    micro, positions, patches, dim = local.shape
    return pl.pallas_call(
        patch_back_kernel,
        out_shape=(
            jax.ShapeDtypeStruct((bytes_part.shape[1], dim), f32),
            jax.ShapeDtypeStruct((micro, patches, positions * dim), f32),
        ),
        in_specs=[VMEM] * 5,
        out_specs=(VMEM,) * 2,
        compiler_params=plain_params(),
        name="patch_back",
    )(everyone, own, bytes_part, weight, local)


def body(
    byte_input,
    seq_lengths,
    patch_weight,
    norm_in_gain,
    in_weight,
    conv_weight,
    conv_bias,
    step_bias,
    log_decay,
    skip_gain,
    group_gain,
    out_weight,
    attn_gain,
    qkv_weight,
    attn_out_weight,
    ffn_gain,
    ffn_weight,
    out_grad,
):
    micro, patches, cols = byte_input.shape
    dim = norm_in_gain.shape[0]
    patch_len = cols // dim
    positions = patch_weight.shape[0]
    own_cols = positions * dim
    n, mpn = lax.axis_size("dp"), lax.axis_size("mp")
    i, j = lax.axis_index("dp"), lax.axis_index("mp")
    reps = n // mpn
    share = n // reps
    part_cols = qkv_weight.shape[2]

    weight_cols = lax.all_gather(ffn_weight, "mp", axis=1, tiled=True)
    own_input = lax.dynamic_slice_in_dim(byte_input, j * own_cols, own_cols, 2)
    own_input = own_input.reshape(micro * patches, own_cols)
    lengths_own = lax.dynamic_index_in_dim(seq_lengths, j, 0, keepdims=False)
    ends = jnp.sum(lengths_own)
    places = i * patches + jnp.arange(patches, dtype=jnp.int32)
    valid = jnp.tile((places < ends).astype(f32), patch_len)[:, None]
    own_grad = lax.dynamic_index_in_dim(out_grad, j, 0, keepdims=False)
    own_grad = own_grad.reshape(patches, patch_len, dim).swapaxes(0, 1).reshape(patch_len * patches, dim)
    own_grad = jnp.where(valid > 0, own_grad, jnp.zeros_like(own_grad))
    grad_rows = lax.all_gather(own_grad, "dp")
    input_all = lax.all_gather(own_input, "dp")
    feature = dim // n
    bytes_part = lax.dynamic_slice_in_dim(
        input_all.reshape(n * micro * patches, positions, dim), i * feature, feature, 2
    ).reshape(n * micro * patches, positions * feature)

    pw = patch_weight.reshape(own_cols, dim)
    row = lambda v: v.reshape(1, -1)
    global_in, normed = embed(n, mpn, own_input, pw, row(norm_in_gain))
    normed = normed.reshape(n * patches, dim)
    lengths_mix = lax.dynamic_index_in_dim(seq_lengths, i // reps, 0, keepdims=False)
    in_w, out_w = in_weight[0], out_weight[0]
    taps = conv_weight[0].T
    skip_cols = row(jnp.repeat(skip_gain[0], HEAD_DIM))
    mixer_params = (taps, conv_bias, step_bias, log_decay, skip_cols, group_gain)
    projected, mixer_y, mixer_low, mixer_part = mixer_fwd(lengths_mix, normed, in_w, *mixer_params, out_w)
    global_out = mix_out(n, mpn, mixer_part.reshape(n, patches, dim), global_in)
    attn_in, qkv, heads, branch_part = att_fwd(
        byte_input, global_out, row(attn_gain), qkv_weight, attn_out_weight
    )
    own_bytes = lax.dynamic_index_in_dim(byte_input, j, 0, keepdims=False)
    own_global = lax.dynamic_index_in_dim(global_out, j, 0, keepdims=False)
    after, ffn_rows = after_att(n, mpn, branch_part, own_bytes, own_global, row(ffn_gain))
    down_part, ffn_in_part, ffn_grad_part = ffn(ffn_rows, grad_rows, weight_cols)
    ffn_grad = lax.psum_scatter(ffn_grad_part, "mp", scatter_dimension=1, tiled=True)
    after_grad, branch, block_low, ffn_gain_part = ffn_back(
        n, mpn, ffn_in_part, down_part, after, own_grad, valid, row(ffn_gain)
    )
    att_part, qkv_grad_part, out_grad_part = att_bwd(branch, attn_in, qkv, heads, qkv_weight, attn_out_weight)
    qkv_grad = lax.psum_scatter(qkv_grad_part, "dp", scatter_dimension=1, tiled=True)
    attn_out_grad = lax.psum_scatter(out_grad_part, "dp", scatter_dimension=1, tiled=True)
    block_cols = block_low.reshape(patch_len * patches, mpn, part_cols).swapaxes(0, 1)
    local, block_all, global_grad, g_mixer, attn_gain_part = att_back(
        n, mpn, att_part, own_bytes, own_global, after_grad, block_cols, row(attn_gain)
    )
    rank = i % reps
    normed_half = lax.dynamic_slice_in_dim(normed, rank * (dim // reps), dim // reps, 1)
    low_half = lax.dynamic_slice_in_dim(mixer_low, rank * (GROUP_WIDTH // reps), GROUP_WIDTH // reps, 1)
    normed_part, in_part, out_part, small_part = mixer_bwd(
        lengths_mix, g_mixer.reshape(n * patches, dim), normed_half, projected, mixer_y, low_half,
        in_w, *mixer_params, out_w,
    )
    gains_part = jnp.concatenate(
        [jnp.zeros((1, dim), f32), attn_gain_part, ffn_gain_part, jnp.zeros((5, dim), f32)], axis=0
    )
    everyone, in_grad, out_w_grad, small, gains = mix_back(
        n, mpn, normed_part.reshape(n, patches, dim), global_in, global_grad, row(norm_in_gain),
        in_part.reshape(share, dim // n, in_w.shape[1]), out_part.reshape(share, GROUP_WIDTH // n, dim),
        small_part, gains_part,
    )
    own_all = lax.dynamic_index_in_dim(everyone, i, 0, keepdims=False)
    patch_grad, input_grad = patch_back(
        everyone.reshape(n * micro * patches, dim), own_all.reshape(micro * patches, dim), bytes_part, pw,
        local.reshape(micro, positions, patches, dim),
    )

    block = block_all.reshape(micro, patch_len, patches, part_cols).swapaxes(1, 2)
    block = block.reshape(micro, patches * patch_len, part_cols)

    def mine(array, axis):
        size = array.shape[axis] // n
        return lax.dynamic_slice_in_dim(array, i * size, size, axis)

    conv_w_grad = mine(small[:CONV].T[None], 1)
    return (
        block,
        input_grad,
        patch_grad.reshape(positions, feature, dim),
        mine(gains[0], 0),
        in_grad[None],
        conv_w_grad,
        mine(small[CONV : CONV + 1], 1),
        small[CONV + 3 : CONV + 4, :GROUP_HEADS],
        small[CONV + 4 : CONV + 5, :GROUP_HEADS],
        jnp.sum(small[CONV + 2, :GROUP_WIDTH].reshape(1, GROUP_HEADS, HEAD_DIM), axis=2),
        mine(small[CONV + 1 : CONV + 2, :GROUP_WIDTH], 1),
        out_w_grad[None],
        mine(gains[1], 0),
        qkv_grad.astype(f32),
        attn_out_grad.astype(f32),
        mine(gains[2], 0),
        ffn_grad.astype(f32),
    )


def solution(mesh):
    in_specs = (
        P(None, "dp", None),
        P(),
        P("mp", None, None),
        P(),
        P("mp", None, None),
        P("mp", None, None),
        P("mp", None),
        P("mp", None),
        P("mp", None),
        P("mp", None),
        P("mp", None),
        P("mp", None, None),
        P(),
        P(None, None, "mp"),
        P("mp", None),
        P(),
        P(None, "mp", "dp"),
        P(None, "dp", None),
    )
    out_specs = (
        P(None, "dp", "mp"),
        P(None, "dp", "mp"),
        P("mp", "dp", None),
        P("dp"),
        P("mp", "dp", None),
        P("mp", "dp", None),
        P("mp", "dp"),
        P("mp", None),
        P("mp", None),
        P("mp", None),
        P("mp", "dp"),
        P("mp", "dp", None),
        P("dp"),
        P(None, "dp", "mp"),
        P("mp", "dp"),
        P("dp"),
        P(None, "mp", "dp"),
    )
    return jax.shard_map(body, mesh=mesh, in_specs=in_specs, out_specs=out_specs, check_vma=False)
```

time: 2730 us -> 409 us (0.15)
  waiting for transfers between devices: 1660 us -> 18.9 us
  Pallas kernels: 0 us -> 322 us
  matrix products: 282 us -> 0 us
  other arithmetic: 257 us -> 9.72 us
  local copies, waits for them, and re-layouts: 277 us -> 41.6 us
  blocking collectives: 192 us -> 0 us
    psum x6 -> x0, waiting for transfers between devices: 1000 us -> none  [the longest x1 841 us: body(): lax.psum(jnp.einsum('tc,kcf->ktf', ffn_rows_in, ffn_weight[:2], preferred...]
    reduce_scatter x13 -> x2, waiting for transfers between devices: 449 us -> 17.2 us  [the longest x1 17.2 us: body(): lax.psum_scatter(ffn_grad_part, 'mp', scatter_dimension=1, tiled=True)]
    pallas_call x0 -> x12, Pallas kernels: none -> 322 us  [the longest x1 52.5 us: ffn_back(): pl.pallas_call(partial(ffn_back_kernel, n, mpn), out_shape=(jax.ShapeDtyp...]
    dot_general x152 -> x0, matrix products: 273 us -> none  [the longest x12 27 us: block_terms(): jnp.einsum('sgh,sghe,sgn->ghen', to_end, values, inputs, precision=highest)]
    unnamed x39 -> x7, waiting for transfers between devices: 187 us -> 1.78 us
    all_gather x16 -> x0, blocking collectives: 182 us -> none  [the longest x8 75 us: gather_rows(): return lax.all_gather(features, 'dp', axis=0, tiled=True)]
    select_n x64 -> x2, other arithmetic: 92 us -> 1.58 us  [body(): own_grad = jnp.where(valid > 0, own_grad, jnp.zeros_like(own_grad))]
    reduce_sum x46 -> x2, other arithmetic: 58.9 us -> 2.55 us  [the longest x1 1.92 us: body(): ends = jnp.sum(lengths_own)]
  transfers between devices with their start and end apart: 41 -> 6, of which waited for: 26 -> 1; matrix products, arithmetic and copies ran while one was open for 17% -> 8% of each run, Pallas kernels for 0% -> 79%
where the time goes in v1:
time: 409 us; the launch traced here: 407 us
  Pallas kernels  322 us (79%)
  local copies, waits for them, and re-layouts  41.6 us (10%)
  waiting for transfers between devices  18.9 us (5%)
  between operations  14.5 us (4%)
  other arithmetic  9.72 us (2%)
    pallas_call x1, Pallas kernels, ffn_back(): pl.pallas_call(partial(ffn_back_kernel, n, mpn), out_shape=(jax.ShapeDtyp...  52.5 us
    pallas_call x1, Pallas kernels, after_att(): pl.pallas_call(partial(after_att_kernel, n, mpn), out_shape=(jax.ShapeDty...  51.5 us
    pallas_call x1, Pallas kernels, att_back(): pl.pallas_call(partial(att_back_kernel, n, mpn), out_shape=(jax.ShapeDtyp...  50.5 us
    pallas_call x1, Pallas kernels, mix_back(): pl.pallas_call(partial(mix_back_kernel, n, mpn), out_shape=(jax.ShapeDtyp...  48.6 us
    pallas_call x1, Pallas kernels, mix_out(): pl.pallas_call(partial(mix_out_kernel, n, mpn), out_shape=jax.ShapeDtypeS...  38.9 us
    unnamed x58, local copies, waits for them, and re-layouts  23.9 us
    pallas_call x1, Pallas kernels, ffn(): pl.pallas_call(ffn_kernel, out_shape=(jax.ShapeDtypeStruct((blocks, rows,...  22.1 us
    reduce_scatter x1, waiting for transfers between devices, body(): lax.psum_scatter(ffn_grad_part, 'mp', scatter_dimension=1, tiled=True)  17.2 us
  transfers between devices with their start and end apart: 6, of which 1 were waited for; matrix products, arithmetic and copies ran while one was open for 8% of the time, Pallas kernels for 79%

profile of v1, /device:TPU:2, one launch (start us, length us, event | category | flops | bytes accessed | tf_op | source)
XLA Modules:
  0.0 407.1 jit_solution(13885010688938446284)
XLA Ops:
  7.3 1.9 fusion.2
  9.2 0.7 broadcast_compare_fusion
  9.9 0.1 gt.17
  10.0 0.2 copy.55
  10.2 0.8 bitcast_select_fusion.1
  11.0 0.7 all-gather.6.cloned.1.call-update
  11.8 1.7 constant_dynamic-slice_fusion.11
  13.6 0.7 reshape_reshape.3.skip
  14.3 0.7 broadcast_in_dim_tile.4.valid
  15.0 4.6 %copy.54 = bf16[1,1024,1288]{2,1,0:T(8,128)(2,1)} copy(bf16[1,1024,1288]{1,2,0:T(8,128)(2,1)} %param.22) | data formatting | bytes 5275648 | tf_op args[4]
  19.5 2.3 copy-done.1
  21.8 15.7 %embed.1 = (f32[16,1024]{1,0:T(8,128)S(1)}, bf16[8,16,1024]{2,1,0:T(8,128)(2,1)S(1)}) custom-call(bf16[64,2048]{1,0:T(8,128)(2,1)S(1)} %bitcast.68, bf16[2048,1024]{1,0:T(8,128)(2,1)S(1)} %bitcast.66, f32[1,1024]{1,0:T(1,128)S(1)} %bitcast.84), custom_call_target="tpu_custom_call" | custom-call | tf_op jit(solution)/shard_map/embed/pallas_call | solution.py:139
  37.6 0.7 copy-done.9
  38.3 4.8 %mixer_fwd.1 = (f32[128,1288]{1,0:T(8,128)}, f32[128,512]{1,0:T(8,128)}, bf16[128,512]{1,0:T(8,128)(2,1)}, f32[128,1024]{1,0:T(8,128)}) custom-call(s32[3]{0:T(128)} %get-tuple-element.171.lengths, bf16[128,1024]{1,0:T(8,128)(2,1)} %bitcast.73, bf16[1024,1288]{1,0:T(8,128)(2,1)} %bitcast.88, f32[4,768]{1,0:T(4,128)} %bitcast.100, f32[1,768]{1,0:T(1,128)} %conv_bias.3, ...), custom_call_target="tpu_custom_call" | custom-call | tf_op jit(solution)/shard_map/mixer_fwd/pallas_call | solution.py:236
  43.1 1.0 copy-done.11
  44.2 38.9 %mix_out.1.patch_out = f32[4,16,1024]{2,1,0:T(8,128)S(1)} custom-call(f32[8,16,1024]{2,1,0:T(8,128)S(1)} %bitcast.75, f32[16,1024]{1,0:T(8,128)S(1)} %get-tuple-element.57.global_in), custom_call_target="tpu_custom_call" | custom-call | tf_op jit(solution)/shard_map/mix_out/pallas_call | solution.py:424
  83.0 0.7 copy-done.6
  83.7 9.7 %att_fwd.1 = (bf16[4,128,1024]{2,1,0:T(8,128)(2,1)}, bf16[3,4,128,256]{3,2,1,0:T(8,128)(2,1)}, bf16[4,128,256]{2,1,0:T(8,128)(2,1)}, bf16[4,128,1024]{2,1,0:T(8,128)(2,1)}) custom-call(bf16[4,16,8192]{2,1,0:T(8,128)(2,1)} %bytes_in.1, f32[4,16,1024]{2,1,0:T(8,128)} %copy-done.6, f32[1,1024]{1,0:T(1,128)} %bitcast.82, bf16[3,1024,256]{2,1,0:T(8,128)(2,1)} %qkv_weight.3, ...), custom_call_target="tpu_custom_call" | custom-call | tf_op jit(solution)/shard_map/att_fwd/pallas_call | solution.py:494
  93.5 0.8 dynamic-slice_bitcast_fusion.2.patch_out
  94.3 1.0 dynamic-slice_bitcast_fusion.1.own_bytes
  95.3 1.2 copy-done.8
  96.5 51.5 %after_att.1 = (f32[128,1024]{1,0:T(8,128)S(1)}, bf16[8,128,1024]{2,1,0:T(8,128)(2,1)S(1)}) custom-call(bf16[4,128,1024]{2,1,0:T(8,128)(2,1)S(1)} %copy-done.8, bf16[16,8192]{1,0:T(8,128)(2,1)S(1)} %dynamic-slice_bitcast_fusion.1.own_bytes, f32[16,1024]{1,0:T(8,128)S(1)} %dynamic-slice_bitcast_fusion.2.patch_out, f32[1,1024]{1,0:T(1,128)S(1)} %bitcast.87), custom_call_target="tpu_custom_call" | custom-call | tf_op jit(solution)/shard_map/after_att/pallas_call | solution.py:630
  148.0 1.3 copy-done.3
  149.3 0.8 copy-done.15
  150.1 0.8 bitcast_select_fusion.own_grad
  150.9 22.1 %ffn.1 = (bf16[8,128,1024]{2,1,0:T(8,128)(2,1)}, bf16[8,128,1024]{2,1,0:T(8,128)(2,1)}, bf16[3,1024,512]{2,1,0:T(8,128)(2,1)}) custom-call(bf16[8,128,1024]{2,1,0:T(8,128)(2,1)} %copy-done.3, bf16[8,128,1024]{2,1,0:T(8,128)(2,1)} %all-gather.4.cloned.1.call-done.grads_in, bf16[3,1024,512]{2,1,0:T(8,128)(2,1)} %all-gather.6.cloned.1.call-done.weight), custom_call_target="tpu_custom_call" | custom-call | tf_op jit(solution)/shard_map/ffn/pallas_call | solution.py:686
  173.0 52.5 %ffn_back.1 = (f32[128,1024]{1,0:T(8,128)}, bf16[4,128,1024]{2,1,0:T(8,128)(2,1)}, bf16[128,1024]{1,0:T(8,128)(2,1)}, f32[1,1024]{1,0:T(1,128)}) custom-call(bf16[8,128,1024]{2,1,0:T(8,128)(2,1)} %get-tuple-element.60.in_part, bf16[8,128,1024]{2,1,0:T(8,128)(2,1)} %get-tuple-element.61.down_part, f32[128,1024]{1,0:T(8,128)} %copy-done.15, ...), custom_call_target="tpu_custom_call" | custom-call | tf_op jit(solution)/shard_map/ffn_back/pallas_call | solution.py:768
  225.6 15.8 %att_bwd.1 = (bf16[4,128,1024]{2,1,0:T(8,128)(2,1)}, bf16[3,1024,256]{2,1,0:T(8,128)(2,1)}, bf16[256,1024]{1,0:T(8,128)(2,1)}) custom-call(bf16[4,128,1024]{2,1,0:T(8,128)(2,1)} %get-tuple-element.63.branch, bf16[4,128,1024]{2,1,0:T(8,128)(2,1)} %get-tuple-element.64.attn_in, bf16[3,4,128,256]{3,2,1,0:T(8,128)(2,1)} %get-tuple-element.65.qkv, ...), custom_call_target="tpu_custom_call" | custom-call | tf_op jit(solution)/shard_map/att_bwd/pallas_call | solution.py:558
  241.4 2.1 copy.62
  243.5 0.5 reduce-scatter.6.cloned.1.call-update
  244.1 0.5 reduce-scatter.8.cloned.1.call-update
  244.8 0.6 constant_dynamic-slice_fusion.8.low_half
  245.4 0.7 constant_dynamic-slice_fusion.9.normed_half
  246.1 4.6 %reshape.175 = bf16[512,2,1024]{2,1,0:T(2,128)(2,1)} reshape(bf16[8,64,2048]{2,1,0:T(8,128)(2,1)} %all-gather.8.cloned.1.call-done) | data formatting | bytes 4194304 | tf_op jit(solution)/shard_map/reshape | solution.py:1167
  250.6 1.3 constant_dynamic-slice_fusion.6
  251.9 0.7 copy.67
  252.6 0.2 copy.58
  252.8 0.2 copy.59
  253.0 50.5 %att_back.1 = (bf16[4,32,1024]{2,1,0:T(8,128)(2,1)S(1)}, bf16[4,128,256]{2,1,0:T(8,128)(2,1)S(1)}, f32[16,1024]{1,0:T(8,128)S(1)}, bf16[8,16,1024]{2,1,0:T(8,128)(2,1)S(1)}, f32[1,1024]{1,0:T(1,128)S(1)}) custom-call(bf16[4,128,1024]{2,1,0:T(8,128)(2,1)S(1)} %copy-done.7, bf16[16,8192]{1,0:T(8,128)(2,1)S(1)} %dynamic-slice_bitcast_fusion.1.own_bytes, ...), custom_call_target="tpu_custom_call" | custom-call | tf_op jit(solution)/shard_map/att_back/pallas_call | solution.py:891
  303.5 0.7 copy-done.16
  304.2 0.7 copy-done.17
  304.9 6.7 %mixer_bwd.1 = (f32[128,1024]{1,0:T(8,128)}, bf16[512,1288]{1,0:T(8,128)(2,1)}, bf16[256,1024]{1,0:T(8,128)(2,1)}, f32[16,768]{1,0:T(8,128)}) custom-call(s32[3]{0:T(128)} %get-tuple-element.171.lengths, bf16[128,1024]{1,0:T(8,128)(2,1)} %bitcast.79, bf16[128,512]{1,0:T(8,128)(2,1)} %constant_dynamic-slice_fusion.9.normed_half, ...), custom_call_target="tpu_custom_call" | custom-call | tf_op jit(solution)/shard_map/mixer_bwd/pallas_call | solution.py:328
  311.7 1.4 copy-done.4
  313.1 1.1 copy-done.13
  314.1 1.0 copy-done.14
  315.2 0.8 copy-done.18
  316.0 48.6 %mix_back.1 = (bf16[8,4,16,1024]{3,2,1,0:T(8,128)(2,1)S(1)}, f32[128,1288]{1,0:T(8,128)S(1)}, f32[64,1024]{1,0:T(8,128)S(1)}, f32[16,768]{1,0:T(8,128)S(1)}, f32[8,1024]{1,0:T(8,128)S(1)}) custom-call(f32[8,16,1024]{2,1,0:T(8,128)S(1)} %bitcast.76, f32[16,1024]{1,0:T(8,128)S(1)} %get-tuple-element.57.global_in, ...), custom_call_target="tpu_custom_call" | custom-call | tf_op jit(solution)/shard_map/mix_back/pallas_call | solution.py:1057
  364.6 0.9 copy.68
  365.5 1.1 copy.61
  366.7 0.6 reduce_sum.21
  367.3 0.7 constant_dynamic-slice_fusion.7
  368.0 5.2 %patch_back.1 = (f32[256,1024]{1,0:T(8,128)}, f32[4,16,2048]{2,1,0:T(8,128)}) custom-call(bf16[512,1024]{1,0:T(8,128)(2,1)} %bitcast.70, bf16[64,1024]{1,0:T(8,128)(2,1)} %bitcast.97, bf16[512,256]{1,0:T(8,128)(2,1)} %bitcast.94, bf16[2048,1024]{1,0:T(8,128)(2,1)} %bitcast.65, bf16[4,2,16,1024]{3,2,1,0:T(8,128)(2,1)} %bitcast.78), custom_call_target="tpu_custom_call" | custom-call | tf_op jit(solution)/shard_map/patch_back/pallas_call | solution.py:1109
  373.2 0.5 fusion.5
  373.7 0.6 constant_dynamic-slice_fusion.3
  374.3 0.6 constant_dynamic-slice_fusion.2
  374.9 0.5 fusion.3
  375.4 0.6 fusion
  376.0 0.5 fusion.7
  376.6 0.9 copy.63
  377.5 0.7 convert_element_type.18
  378.2 1.7 convert_element_type.17
  379.9 17.2 %reduce-scatter.8.cloned.1.call-done = bf16[3,256,512]{2,1,0:T(8,128)(2,1)} async-done(((bf16[3,1024,512]{2,1,0:T(8,128)(2,1)}), bf16[3,256,512]{2,1,0:T(8,128)(2,1)}) %reduce-scatter.8.cloned.1.call-update) | async-done | bytes 786448 | tf_op jit(solution)/shard_map/reduce_scatter | solution.py:1188
  397.0 2.5 convert_element_type.19
  399.5 0.7 copy.70
  (66 shorter events, 0.8 us)
Async XLA Ops:
  7.2 2.8 copy-start
  7.2 6.3 %copy-start.25 = (f32[1,8]{1,0:T(1,128)S(1)}, f32[1,8]{1,0:T(1,128)}, u32[]{:S(2)}) copy-start(f32[1,8]{1,0:T(1,128)} %param.27) | copy-start | bytes 100
  7.2 143.7 %all-gather.4.cloned.1.call-start = ((), (), s32[]{:S(2)}) async-start(), calls=%async_computation.3 | async-start | bytes 2359296 | tf_op jit(solution)/shard_map/all_gather | solution.py:1163
  11.0 140.0 %all-gather.6.cloned.1.call-start = ((), (), s32[]{:S(2)}) async-start(), calls=%async_computation.4 | async-start | bytes 3932160 | tf_op jit(solution)/shard_map/all_gather | solution.py:1153
  11.7 234.3 %all-gather.8.cloned.1.call-start = ((), (), s32[]{:S(2)}) async-start(), calls=%async_computation.5 | async-start | bytes 2359296 | tf_op jit(solution)/shard_map/all_gather | solution.py:1164
  13.5 363.1 %reduce-scatter.10.cloned.1.call-start = ((), (), s32[]{:S(2)}) async-start(), calls=%async_computation.8 | async-start | bytes 589824
  15.0 4.6 %copy-start.2 = (bf16[4,16,2048]{2,1,0:T(8,128)(2,1)S(1)}, bf16[4,16,2048]{2,1,0:T(8,128)(2,1)}, u32[]{:S(2)}) copy-start(bf16[4,16,2048]{2,1,0:T(8,128)(2,1)} %constant_dynamic-slice_fusion.11) | copy-start | bytes 786436
  15.0 4.6 %copy-start.20 = (f32[1024]{0:T(1024)S(1)}, f32[1024]{0:T(1024)}, u32[]{:S(2)}) copy-start(f32[1024]{0:T(1024)} %param.21) | copy-start | bytes 12292
  19.5 2.3 copy-start.1
  37.6 0.7 copy-start.9
  43.1 1.0 copy-start.11
  83.0 0.7 copy-start.6
  83.7 11.5 %copy-start.21 = (f32[1024]{0:T(1024)S(1)}, f32[1024]{0:T(1024)}, u32[]{:S(2)}) copy-start(f32[1024]{0:T(1024)} %param.33) | copy-start | bytes 12292
  95.3 1.2 copy-start.8
  148.0 1.3 copy-start.3
  149.3 0.8 copy-start.15
  243.5 134.7 %reduce-scatter.6.cloned.1.call-start = ((), (), s32[]{:S(2)}) async-start(), calls=%async_computation.6 | async-start | bytes 1769472 | tf_op jit(solution)/shard_map/reduce_scatter | solution.py:1193
  243.5 1.2 copy-start.23
  243.5 1.9 copy-start.10
  244.1 153.0 %reduce-scatter.8.cloned.1.call-start = ((), (), s32[]{:S(2)}) async-start(), calls=%async_computation.7 | async-start | bytes 3932160 | tf_op jit(solution)/shard_map/reduce_scatter | solution.py:1188
  246.1 6.5 %copy-start.22 = (bf16[128,1024]{1,0:T(8,128)(2,1)S(1)}, bf16[128,1024]{1,0:T(8,128)(2,1)}, u32[]{:S(2)}) copy-start(bf16[128,1024]{1,0:T(8,128)(2,1)} %get-tuple-element.69) | copy-start | bytes 786436
  250.6 2.3 copy-start.7
  250.6 2.3 copy-start.12
  250.6 2.3 copy-start.19
  303.5 0.7 copy-start.16
  304.2 0.7 copy-start.17
  304.9 6.7 %copy-start.24 = (f32[1,1024]{1,0:T(1,128)S(1)}, f32[1,1024]{1,0:T(1,128)}, u32[]{:S(2)}) copy-start(f32[1,1024]{1,0:T(1,128)} %get-tuple-element.81) | copy-start | bytes 12292
  311.7 1.4 copy-start.4
  313.1 1.1 copy-start.13
  314.1 1.0 copy-start.14
  315.2 0.8 copy-start.18
  364.6 3.4 copy-start.5
Sparse Core Ops, SparseCore 0:
  11.1 31.9 all-gather.3
  44.6 94.8 all-gather.5
  142.0 28.8 all-gather.7
  243.6 38.1 reduce-scatter.9
  285.8 42.0 reduce-scatter.5
  330.2 66.8 reduce-scatter.7

commit v2 on v0

v2 whole, which is shorter than its diff:
```python
from functools import partial
from types import SimpleNamespace

import jax
import jax.numpy as jnp
from jax import lax
from jax.experimental import pallas as pl
from jax.experimental.pallas import tpu as pltpu
from jax.sharding import PartitionSpec as P

STATE = 128
CONV = 4
SEQS = 3
GROUP_WIDTH = 512
GROUP_HEADS = 8
HEAD_DIM = 64
ATT_DIM = 64
CONV_CH = 768

norm_eps = 1e-06
highest = lax.Precision.HIGHEST
large_negative = -1e30
f32 = jnp.float32
bf16 = jnp.bfloat16
MESH = pl.DeviceIdType.MESH
VMEM = pl.BlockSpec(memory_space=pltpu.VMEM)
ANY = pl.BlockSpec(memory_space=pl.ANY)
SMEM = pl.BlockSpec(memory_space=pltpu.SMEM)
DMA = pltpu.SemaphoreType.DMA
WEIGHT_CUTS = 4
GRAD_CUTS = 4
SPILL_BYTES = 4 * 2**20


def dot(a, b, dims=((1,), (0,)), precision=None):
    return lax.dot_general(
        a, b, (dims, ((), ())), preferred_element_type=f32, precision=precision
    )


def inv_rms(values):
    return lax.rsqrt(jnp.mean(values * values, axis=-1, keepdims=True) + norm_eps)


def rms_back(values, gain, upstream):
    scale = inv_rms(values)
    weighted = upstream * gain
    inner = jnp.mean(weighted * values, axis=-1, keepdims=True)
    back = scale * weighted - values * (inner * scale * scale * scale)
    return back, upstream * (values * scale)


def silu_pair(values):
    sig = jax.nn.sigmoid(values)
    return values * sig, sig * (1.0 + values * (1.0 - sig))


def rcopy(src, dst, send_sem, recv_sem, dp, mp):
    return pltpu.make_async_remote_copy(
        src_ref=src,
        dst_ref=dst,
        send_sem=send_sem,
        recv_sem=recv_sem,
        device_id={"dp": dp, "mp": mp},
        device_id_type=MESH,
    )


def greet(barrier, dp, mp):
    pl.semaphore_signal(barrier, inc=1, device_id={"dp": dp, "mp": mp}, device_id_type=MESH)


def plain_params(mib=56):
    return pltpu.CompilerParams(vmem_limit_bytes=mib * 2**20)


def remote_params(cid, mib=40):
    return pltpu.CompilerParams(
        collective_id=cid, has_side_effects=True, vmem_limit_bytes=mib * 2**20
    )


def launch(name, kernel, ins, outs, scratch, params):
    names = [*ins, *outs, *scratch]

    def run(*refs):
        kernel(SimpleNamespace(**dict(zip(names, refs))))

    results = pl.pallas_call(
        run,
        out_shape=tuple(jax.ShapeDtypeStruct(shape, dtype) for shape, dtype, _ in outs.values()),
        in_specs=[spec for _, spec in ins.values()],
        out_specs=tuple(spec for _, _, spec in outs.values()),
        scratch_shapes=list(scratch.values()),
        compiler_params=params,
        name=name,
    )(*[array for array, _ in ins.values()])
    return SimpleNamespace(**dict(zip(outs, results)))


def place_of(n, mpn):
    i, j = lax.axis_index("dp"), lax.axis_index("mp")
    reps = n // mpn
    return SimpleNamespace(
        n=n, mpn=mpn, i=i, j=j, reps=reps, share=n // reps, half=n // 2,
        m=i // reps, h=i % reps, c=i % 2, mine=i // 2, other=i + 1 - 2 * (i % 2), inside=i // reps == j,
    )


def greet_all(p, barrier):
    for d in range(1, p.mpn):
        greet(barrier, p.i, (p.j + d) % p.mpn)
    for d in range(1, p.n):
        greet(barrier, (p.i + d) % p.n, p.j)
    for s in range(p.n):
        @pl.when(jnp.logical_not((s == p.i) & p.inside))
        def _():
            greet(barrier, s, p.m)
    for h in range(p.reps):
        for t in range(p.mpn):
            @pl.when(jnp.logical_not((p.j * p.reps + h == p.i) & (t == p.j)))
            def _():
                greet(barrier, p.j * p.reps + h, t)
    return p.mpn + 3 * p.n - 2 - 2 * p.inside.astype(jnp.int32)


def mp_start(p, src, dst, ss, rs):
    copies = []
    for d in range(1, p.mpn):
        t = (p.j + d) % p.mpn
        copy = rcopy(src(t), dst(p.j), ss.at[t], rs.at[p.j], p.i, t)
        copy.start()
        copies.append(copy)
    return copies


def mp_wait(p, d, dst, ss, rs):
    s = (p.j + d) % p.mpn
    rcopy(dst(s), dst(s), ss.at[s], rs.at[s], p.i, s).wait_recv()
    return s


def plane_start(p, own, slot, ss, rs, ssr):
    copies = []
    for d in range(1, p.half):
        q = (p.mine + d) % p.half
        copies.append(rcopy(own, slot(p.i), ss.at[q], rs.at[p.i], q * 2 + p.c, p.j))
    copies.append(rcopy(own, slot(p.i), ssr.at[p.mine], rs.at[p.i], p.other, p.j))
    for copy in copies:
        copy.start()
    return copies


def plane_relay(p, slot, ss, rs, ssr):
    copies = []
    for d in range(1, p.half):
        q = (p.mine + p.half - d) % p.half
        s = q * 2 + p.c
        rcopy(slot(s), slot(s), ss.at[q], rs.at[s], s, p.j).wait_recv()
        copy = rcopy(slot(s), slot(s), ssr.at[q], rs.at[s], p.other, p.j)
        copy.start()
        copies.append(copy)
    return copies


def plane_finish(p, slot, rs, ssr):
    for q in range(p.half):
        s = q * 2 + 1 - p.c
        rcopy(slot(s), slot(s), ssr.at[q], rs.at[s], p.other, p.j).wait_recv()


def reduce_start(p, block, pre, ssa, rsa):
    copies = []
    for d in range(1, p.half + 1):
        q = (p.mine + d) % p.half
        copy = rcopy(block(q * 2 + 1 - p.c), pre.at[q], ssa.at[q], rsa.at[q], p.other, p.j)
        copy.start()
        copies.append(copy)
    return copies


def cast_start(p, low, dst, ss, rs):
    for h in range(p.reps):
        for t in range(p.mpn):
            here = (p.j * p.reps + h == p.i) & (t == p.j)

            @pl.when(jnp.logical_not(here))
            def _():
                rcopy(low, dst.at[p.i], ss.at[h * p.mpn + t], rs.at[p.i], p.j * p.reps + h, t).start()

            @pl.when(here)
            def _():
                dst[p.i] = low[...]


def cast_wait(p, low, dst, ss, rs):
    for s in range(p.n):
        @pl.when(jnp.logical_not((s == p.i) & p.inside))
        def _():
            rcopy(low, dst.at[s], ss.at[0], rs.at[s], s, p.m).wait_recv()


def cast_sent(p, low, dst, ss, rs):
    for h in range(p.reps):
        for t in range(p.mpn):
            @pl.when(jnp.logical_not((p.j * p.reps + h == p.i) & (t == p.j)))
            def _():
                rcopy(low, dst.at[p.i], ss.at[h * p.mpn + t], rs.at[p.i], p.j * p.reps + h, t).wait_send()


def owner_copy(p, q, part, recv, ss, rs):
    block = q * p.reps + p.h
    return block, rcopy(part.at[block], recv.at[p.j], ss.at[q], rs.at[p.j], block, p.m)


def owner_start(p, part, recv, ss, rs):
    for q in range(p.share):
        block, copy = owner_copy(p, q, part, recv, ss, rs)

        @pl.when(jnp.logical_not((block == p.i) & p.inside))
        def _():
            copy.start()

    @pl.when(p.inside)
    def _():
        recv[p.j] = part[p.i]


def owner_wait(p, part, recv, ss, rs):
    for s in range(p.mpn):
        @pl.when(jnp.logical_not(p.inside & (s == p.j)))
        def _():
            rcopy(part.at[0], recv.at[s], ss.at[0], rs.at[s], p.j * p.reps + p.h, s).wait_recv()


def owner_sent(p, part, recv, ss, rs):
    for q in range(p.share):
        block, copy = owner_copy(p, q, part, recv, ss, rs)

        @pl.when(jnp.logical_not((block == p.i) & p.inside))
        def _():
            copy.wait_send()


class Bulk:
    def __init__(self, p, pieces):
        self.p, self.pieces, self.done, self.copies = p, pieces, 0, []

    def go(self, count):
        for src, dst, ss, rs in self.pieces[self.done : self.done + count]:
            self.copies += mp_start(self.p, src, dst, ss, rs)
        self.done += count

    def finish(self):
        self.go(len(self.pieces) - self.done)
        for src, dst, ss, rs in self.pieces:
            for d in range(1, self.p.mpn):
                mp_wait(self.p, d, dst, ss, rs)


def perm_matrix(rows, patches, per, limit):
    at = lax.broadcasted_iota(jnp.int32, (rows, rows), 0)
    source = lax.broadcasted_iota(jnp.int32, (rows, rows), 1)
    return ((source == (at % patches) * per + at // patches) & (at % patches < limit)).astype(bf16)


def seg_starts(lengths, places):
    end0 = lengths[0]
    end1 = end0 + lengths[1]
    end2 = end1 + lengths[2]
    return jnp.where(
        places >= end2, end2, jnp.where(places >= end1, end1, jnp.where(places >= end0, end0, 0))
    )


def conv_taps(conv_in, pos, lag):
    moved = conv_in if lag == 0 else pltpu.roll(conv_in, lag, 0)
    return jnp.where(pos >= lag, moved, 0.0)


def mixer_state(lengths, projected, conv_weight, conv_bias, step_bias, log_decay):
    patches = projected.shape[0]
    places = lax.broadcasted_iota(jnp.int32, (patches, 1), 0)
    start = seg_starts(lengths, places)
    pos = places - start
    conv_in = projected[:, GROUP_WIDTH : GROUP_WIDTH + CONV_CH]
    conv_out = conv_bias
    for lag in range(CONV):
        conv_out = conv_out + conv_taps(conv_in, pos, lag) * conv_weight[CONV - 1 - lag][None]
    step_raw = projected[:, GROUP_WIDTH + CONV_CH :] + step_bias
    step = jnp.maximum(step_raw, 0.0) + jnp.log1p(jnp.exp(-jnp.abs(step_raw)))
    logd = -step * jnp.exp(log_decay)
    across = lax.broadcasted_iota(jnp.int32, (patches, patches), 1)
    down = lax.broadcasted_iota(jnp.int32, (patches, patches), 0)
    mask = (across >= start) & (across <= down)
    running = dot(mask.astype(f32), logd, precision=highest)
    return pos, conv_in, conv_out, step_raw, step, logd, mask, running


def head_decay(mask, running, running_t, h):
    return jnp.exp(
        jnp.where(mask, running[:, h : h + 1] - running_t[h : h + 1, :], large_negative)
    )


def att_mask(rows, patches):
    across = lax.broadcasted_iota(jnp.int32, (rows, rows), 1)
    down = lax.broadcasted_iota(jnp.int32, (rows, rows), 0)
    return (across % patches == down % patches) & (across <= down)


def soft_rows(mask, query, key):
    scores = dot(query, key, ((1,), (1,))) * ATT_DIM ** (-0.5)
    scores = jnp.where(mask, scores, large_negative)
    probs = jnp.exp(scores - jnp.max(scores, axis=1, keepdims=True))
    return probs / jnp.sum(probs, axis=1, keepdims=True)


def mixer_fwd(r, lengths, normed):
    projected = dot(normed, r.in_v[...], ((1,), (1,)))
    r.projected[...] = projected
    _, _, conv_out, _, step, _, mask, running = mixer_state(
        lengths, projected, r.taps[...], r.conv_bias[...], r.step_bias[...], r.log_decay[...]
    )
    act = conv_out * jax.nn.sigmoid(conv_out)
    inputs = act[:, GROUP_WIDTH : GROUP_WIDTH + STATE]
    outputs = act[:, GROUP_WIDTH + STATE :]
    inner = dot(outputs, inputs, ((1,), (1,)))
    running_t, step_t = running.T, step.T
    pair = 2 * HEAD_DIM
    lane = lax.broadcasted_iota(jnp.int32, (1, pair), 1)
    pieces = []
    for c in range(GROUP_WIDTH // pair):
        values = act[:, c * pair : (c + 1) * pair]
        got = []
        for h in (2 * c, 2 * c + 1):
            weights = head_decay(mask, running, running_t, h) * inner * step_t[h : h + 1, :]
            got.append(dot(weights, values))
        pieces.append(jnp.where(lane < HEAD_DIM, got[0], got[1]))
    y = jnp.concatenate(pieces, axis=1) + r.skip[...] * act[:, :GROUP_WIDTH]
    r.mixer_y[...] = y
    gate = projected[:, :GROUP_WIDTH]
    gated = y * (gate * jax.nn.sigmoid(gate))
    low = (gated * inv_rms(gated) * r.group_gain[...]).astype(bf16)
    r.mixer_low[...] = low
    return dot(low, r.out_v[...])


def forward_kernel(n, mpn, r):
    p = place_of(n, mpn)
    i, j = p.i, p.j
    micro, patches, own_cols = r.own.shape
    positions, dim = r.pw.shape[0], r.pw.shape[1]
    slabs = r.bytes_v.shape[2] // dim
    rows = slabs * patches
    features = r.bytes_part.shape[-1]
    loads = 0

    def local(src, dst):
        nonlocal loads
        copy = pltpu.make_async_copy(src, dst, r.sem_load.at[loads])
        loads += 1
        copy.start()
        return copy

    load_own = local(r.byte_input.at[:, :, pl.ds(pl.multiple_of(j * own_cols, 128), own_cols)], r.own)
    load_pw = [local(r.patch_weight.at[k], r.pw.at[k]) for k in range(positions)]
    load_grad = local(r.out_grad.at[j], r.grad_raw)
    load_in = local(r.in_weight, r.in_v)
    load_out = local(r.out_weight, r.out_v)
    load_bytes = local(r.byte_input, r.bytes_v)
    load_qkv = local(r.qkv_weight, r.qkv_v)
    keep_w = local(r.ffn_weight, r.w_all.at[j])

    barrier = pltpu.get_barrier_semaphore()
    count = greet_all(p, barrier)
    load_own.wait()
    sums = None
    for k in range(positions):
        load_pw[k].wait()
        term = dot(r.own[:, :, k * dim : (k + 1) * dim].reshape(micro * patches, dim), r.pw[k])
        sums = term if sums is None else sums + term
    for t in range(micro):
        r.part[t] = sums[t * patches : (t + 1) * patches]
    load_grad.wait()
    lengths = lambda m: (r.seq_lengths[m, 0], r.seq_lengths[m, 1], r.seq_lengths[m, 2])
    l0, l1, l2 = lengths(j)
    perm = perm_matrix(rows, patches, slabs, l0 + l1 + l2 - i * patches)
    r.own_grad[...] = dot(perm, r.grad_raw[...]).astype(bf16)
    pl.semaphore_wait(barrier, count)

    sent = mp_start(p, lambda t: r.part.at[t], lambda s: r.recv.at[s], r.ss1, r.rs1)
    grad_slot = lambda s: r.grad_rows.at[s]
    sent += plane_start(p, r.own_grad, grad_slot, r.ssg, r.rsg, r.ssgr)
    keep_grad = local(r.own_grad, r.grad_rows.at[i])
    step = r.w_all.shape[2] // WEIGHT_CUTS
    pieces = []
    for w in range(3):
        for k in range(WEIGHT_CUTS):
            at = slice(k * step, (k + 1) * step)
            pieces.append((
                lambda t, w=w, at=at: r.ffn_weight.at[w, at],
                lambda s, w=w, at=at: r.w_all.at[s, w, at],
                r.ssw.at[w, k],
                r.rsw.at[w, k],
            ))
    bulk = Bulk(p, pieces)
    bulk.go(1)
    total = r.part[j]
    for d in range(1, mpn):
        total = total + r.recv[mp_wait(p, d, lambda s: r.recv.at[s], r.ss1, r.rs1)]
    r.global_in[...] = total
    r.low[...] = (total * inv_rms(total) * r.norm_in_gain[...]).astype(bf16)
    cast_start(p, r.low, r.normed, r.ss2, r.rs2)
    for d in range(1, n):
        t = (i + d) % n
        for k in range(positions):
            first = k * dim + t * (dim // n) // features * features
            copy = rcopy(
                r.own.at[:, :, pl.ds(pl.multiple_of(first, 128), features)],
                r.bytes_part.at[i, k], r.ssb.at[t, k], r.rsb.at[i, k], t, j,
            )
            copy.start()
            sent.append(copy)
    kept = []
    for k in range(positions):
        first = k * dim + i * (dim // n) // features * features
        kept.append(local(r.own.at[:, :, pl.ds(pl.multiple_of(first, 128), features)], r.bytes_part.at[i, k]))
    piece_rows = r.ao_full.shape[2]
    ao_own = r.out_proj.at[pl.ds(pl.multiple_of(i * piece_rows, piece_rows), piece_rows)]
    ao_slot = lambda s: r.ao_full.at[i, s]
    kept_ao = local(ao_own, r.ao_full.at[i, j])
    bulk.go(1)
    load_in.wait()
    load_out.wait()
    cast_wait(p, r.low, r.normed, r.ss2, r.rs2)
    sent += mp_start(p, lambda t: ao_own, ao_slot, r.ssa, r.rsa)
    bulk.go(1)

    part = mixer_fwd(r, lengths(p.m), r.normed[...].reshape(n * patches, dim))
    for b in range(n):
        r.mix_part[b] = part[b * patches : (b + 1) * patches]
    owner_start(p, r.mix_part, r.mix_recv, r.ss3, r.rs3)
    kept_ao.wait()
    for d in range(1, mpn):
        mp_wait(p, d, ao_slot, r.ssa, r.rsa)
    ao_block = lambda s: r.ao_full.at[s]
    sent += plane_start(p, r.ao_full.at[i], ao_block, r.ssap, r.rsap, r.ssar)
    owner_wait(p, r.mix_part, r.mix_recv, r.ss3, r.rs3)
    total = r.global_in[...]
    for s in range(mpn):
        total = total + r.mix_recv[s]
    r.global_own[...] = total
    r.patch_all[j] = total
    sent += mp_start(p, lambda t: r.global_own, lambda s: r.patch_all.at[s], r.ss4, r.rs4)
    bulk.go(2)
    sent += plane_relay(p, grad_slot, r.ssg, r.rsg, r.ssgr)
    load_bytes.wait()
    load_qkv.wait()
    for d in range(1, mpn):
        mp_wait(p, d, lambda s: r.patch_all.at[s], r.ss4, r.rs4)

    mask = att_mask(rows, patches)
    pair = 2 * ATT_DIM
    width = r.qkv_v.shape[2]
    lane = lax.broadcasted_iota(jnp.int32, (1, pair), 1)

    def heads_copy(t):
        return rcopy(r.heads.at[t], r.heads_own.at[j], r.ss5.at[t], r.rs5.at[j], i, t)

    def one_micro(d, _):
        m = (j + d) % mpn
        for k in range(slabs):
            here = r.bytes_v[m, :, k * dim : (k + 1) * dim].astype(f32) + r.patch_all[m]
            r.attn_in[m, k * patches : (k + 1) * patches, :] = (
                here * inv_rms(here) * r.attn_gain[...]
            ).astype(bf16)
        got = r.attn_in[m]
        for w in range(3):
            r.qkv[w, m] = dot(got, r.qkv_v[w]).astype(bf16)
        for c in range(width // pair):
            at = slice(c * pair, (c + 1) * pair)
            query, key, value = r.qkv[0, m, :, at], r.qkv[1, m, :, at], r.qkv[2, m, :, at]
            res = []
            for own in (lane < ATT_DIM, lane >= ATT_DIM):
                probs = soft_rows(mask, jnp.where(own, query, jnp.zeros_like(query)), key)
                res.append(dot(probs.astype(bf16), value))
            r.heads[m, :, at] = jnp.where(lane < ATT_DIM, res[0], res[1]).astype(bf16)

        @pl.when(d < mpn)
        def _():
            heads_copy(m).start()

        return 0

    lax.fori_loop(1, mpn + 1, one_micro, 0)
    bulk.go(len(pieces))
    r.heads_own[j] = r.heads[j]
    sent += plane_relay(p, ao_block, r.ssap, r.rsap, r.ssar)
    plane_finish(p, ao_block, r.rsap, r.ssar)
    for k in range(slabs):
        here = r.bytes_v[j, :, k * dim : (k + 1) * dim].astype(f32) + r.global_own[...]
        r.after[k * patches : (k + 1) * patches, :] = here
    branch = None
    for d in range(mpn):
        s = j if d == 0 else mp_wait(p, d, lambda s: r.heads_own.at[s], r.ss5, r.rs5)
        for b in range(n):
            at = slice(b * piece_rows, (b + 1) * piece_rows)
            r.ao_sorted[s, at, :] = r.ao_full[b, s]
        term = dot(r.heads_own[s], r.ao_sorted[s])
        branch = term if branch is None else branch + term
    after = r.after[...] + branch
    r.after[...] = after
    r.ffn_own[...] = (after * inv_rms(after) * r.ffn_gain[...]).astype(bf16)
    row_slot = lambda s: r.ffn_rows.at[s]
    sent += plane_start(p, r.ffn_own, row_slot, r.ssf, r.rsf, r.ssfr)
    keep_rows = local(r.ffn_own, r.ffn_rows.at[i])
    plane_finish(p, grad_slot, r.rsg, r.ssgr)
    for d in range(1, n):
        s = (i + d) % n
        for k in range(positions):
            rcopy(r.bytes_part.at[s, k], r.bytes_part.at[s, k], r.ssb.at[s, k], r.rsb.at[s, k], s, j).wait_recv()
    sent += plane_relay(p, row_slot, r.ssf, r.rsf, r.ssfr)
    plane_finish(p, row_slot, r.rsf, r.ssfr)
    bulk.finish()
    for copy in [keep_w, keep_grad, keep_rows] + kept:
        copy.wait()
    for copy in sent + bulk.copies:
        copy.wait_send()
    cast_sent(p, r.low, r.normed, r.ss2, r.rs2)
    owner_sent(p, r.mix_part, r.mix_recv, r.ss3, r.rs3)
    for d in range(1, mpn):
        heads_copy((j + d) % mpn).wait_send()


def forward(n, mpn, a):
    micro, patches, cols = a.byte_input.shape
    dim = a.norm_in_gain.shape[1]
    slabs = cols // dim
    rows = patches * slabs
    positions = a.patch_weight.shape[0]
    width = a.qkv_weight.shape[2]
    hidden = a.ffn_weight.shape[2]
    columns = a.in_weight.shape[0]
    features = max(dim // n, 128)
    ao_rows = a.attn_out_weight.shape[0]
    piece = ao_rows // n
    half = n // 2
    seq = n * patches
    ins = dict(
        seq_lengths=(a.seq_lengths, SMEM),
        byte_input=(a.byte_input, ANY), patch_weight=(a.patch_weight, ANY), out_grad=(a.out_grad, ANY),
        in_weight=(a.in_weight, ANY), out_weight=(a.out_weight, ANY), qkv_weight=(a.qkv_weight, ANY),
        out_proj=(a.attn_out_weight, ANY), ffn_weight=(a.ffn_weight, ANY),
        norm_in_gain=(a.norm_in_gain, VMEM), taps=(a.taps, VMEM), conv_bias=(a.conv_bias, VMEM),
        step_bias=(a.step_bias, VMEM), log_decay=(a.log_decay, VMEM), skip=(a.skip, VMEM),
        group_gain=(a.group_gain, VMEM), attn_gain=(a.attn_gain, VMEM), ffn_gain=(a.ffn_gain, VMEM),
    )
    outs = dict(
        grad_rows=((n, rows, dim), bf16, ANY),
        ffn_rows=((n, rows, dim), bf16, ANY),
        w_all=((mpn,) + a.ffn_weight.shape, bf16, ANY),
        bytes_part=((n, positions, micro, patches, features), bf16, ANY),
        own_grad=((rows, dim), bf16, VMEM),
        after=((rows, dim), f32, VMEM),
        heads_own=((mpn, rows, width), bf16, VMEM),
        qkv=((3, micro, rows, width), bf16, VMEM),
        attn_in=((micro, rows, dim), bf16, VMEM),
        ao_sorted=((mpn, ao_rows, dim), bf16, VMEM),
        global_in=((patches, dim), f32, VMEM),
        global_own=((patches, dim), f32, VMEM),
        normed=((n, patches, dim), bf16, VMEM),
        projected=((seq, columns), f32, VMEM),
        mixer_y=((seq, GROUP_WIDTH), f32, VMEM),
        mixer_low=((seq, GROUP_WIDTH), bf16, VMEM),
    )
    scratch = dict(
        own=pltpu.VMEM((micro, patches, positions * dim), bf16),
        pw=pltpu.VMEM(a.patch_weight.shape, bf16),
        grad_raw=pltpu.VMEM((rows, dim), bf16),
        in_v=pltpu.VMEM(a.in_weight.shape, bf16),
        out_v=pltpu.VMEM(a.out_weight.shape, bf16),
        bytes_v=pltpu.VMEM(a.byte_input.shape, bf16),
        qkv_v=pltpu.VMEM(a.qkv_weight.shape, bf16),
        part=pltpu.VMEM((micro, patches, dim), f32),
        recv=pltpu.VMEM((mpn, patches, dim), f32),
        low=pltpu.VMEM((patches, dim), bf16),
        ao_full=pltpu.VMEM((n, mpn, piece, dim), bf16),
        mix_part=pltpu.VMEM((n, patches, dim), f32),
        mix_recv=pltpu.VMEM((mpn, patches, dim), f32),
        patch_all=pltpu.VMEM((mpn, patches, dim), f32),
        heads=pltpu.VMEM((micro, rows, width), bf16),
        ffn_own=pltpu.VMEM((rows, dim), bf16),
        sem_load=DMA((16,)),
        ss1=DMA((mpn,)), rs1=DMA((mpn,)), ss2=DMA((n,)), rs2=DMA((n,)), ss3=DMA((mpn,)), rs3=DMA((mpn,)),
        ss4=DMA((mpn,)), rs4=DMA((mpn,)), ss5=DMA((mpn,)), rs5=DMA((mpn,)),
        ssg=DMA((half,)), rsg=DMA((n,)), ssgr=DMA((half,)),
        ssf=DMA((half,)), rsf=DMA((n,)), ssfr=DMA((half,)),
        ssb=DMA((n, positions)), rsb=DMA((n, positions)),
        ssa=DMA((mpn,)), rsa=DMA((mpn,)), ssap=DMA((half,)), rsap=DMA((n,)), ssar=DMA((half,)),
        ssw=DMA((3, WEIGHT_CUTS, mpn)), rsw=DMA((3, WEIGHT_CUTS, mpn)),
    )
    return launch("forward", partial(forward_kernel, n, mpn), ins, outs, scratch, remote_params(0, 60))


def ffn_kernel(rows_in, grads_in, parts, down_out, in_grad, weight_grad, weight, gate_low, up_low, hidden_low):
    blocks, rows, dim = rows_in.shape
    per = parts.shape[2]
    for s in range(parts.shape[0]):
        for w in range(3):
            weight[w, s * per : (s + 1) * per, :] = parts[s, w]

    def step(b, _):
        here, up = rows_in[b], grads_in[b]
        gate = dot(here, weight[0])
        other = dot(here, weight[1])
        act, slope = silu_pair(gate)
        hidden = (act * other).astype(bf16)
        hidden_low[b] = hidden
        down_out[b] = dot(hidden, weight[2], ((1,), (1,))).astype(bf16)
        hidden_grad = dot(up, weight[2])
        gate_grad = (hidden_grad * other * slope).astype(bf16)
        up_grad = (hidden_grad * act).astype(bf16)
        gate_low[b] = gate_grad
        up_low[b] = up_grad
        back = dot(gate_grad, weight[0], ((1,), (1,))) + dot(up_grad, weight[1], ((1,), (1,)))
        in_grad[b] = back.astype(bf16)
        return 0

    lax.fori_loop(0, blocks, step, 0)
    hidden = weight.shape[2]
    everything = rows_in[...].reshape(blocks * rows, dim)
    weight_grad[0] = dot(everything, gate_low[...].reshape(blocks * rows, hidden), ((0,), (0,))).astype(bf16)
    weight_grad[1] = dot(everything, up_low[...].reshape(blocks * rows, hidden), ((0,), (0,))).astype(bf16)
    weight_grad[2] = dot(
        grads_in[...].reshape(blocks * rows, dim), hidden_low[...].reshape(blocks * rows, hidden), ((0,), (0,))
    ).astype(bf16)


def ffn(rows_in, grads_in, parts):
    blocks, rows, dim = rows_in.shape
    hidden = parts.shape[3]
    return pl.pallas_call(
        ffn_kernel,
        out_shape=(
            jax.ShapeDtypeStruct((blocks, rows, dim), bf16),
            jax.ShapeDtypeStruct((blocks, rows, dim), bf16),
            jax.ShapeDtypeStruct((3, dim, hidden), bf16),
        ),
        in_specs=[VMEM] * 3,
        out_specs=(VMEM,) * 3,
        scratch_shapes=[pltpu.VMEM((3, dim, hidden), bf16)] + [pltpu.VMEM((blocks, rows, hidden), bf16)] * 3,
        compiler_params=plain_params(60),
        name="ffn",
    )(rows_in, grads_in, parts)


def mixer_bwd(r, p, lengths, upstream):
    projected = r.projected[...]
    patches = projected.shape[0]
    pos, conv_in, conv_out, step_raw, step, logd, mask, running = mixer_state(
        lengths, projected, r.taps[...], r.conv_bias[...], r.step_bias[...], r.log_decay[...]
    )
    act, act_slope = silu_pair(conv_out)
    inputs = act[:, GROUP_WIDTH : GROUP_WIDTH + STATE]
    outputs = act[:, GROUP_WIDTH + STATE :]
    inner = dot(outputs, inputs, ((1,), (1,)))
    running_t, step_t = running.T, step.T
    normed_grad = dot(upstream, r.out_v[...], ((1,), (1,)))
    y = r.mixer_y[...]
    gate = projected[:, :GROUP_WIDTH]
    gate_act, gate_slope = silu_pair(gate)
    gated_grad, gain_rows = rms_back(y * gate_act, r.group_gain[...], normed_grad)
    y_grad = gated_grad * gate_act
    gate_grad = gated_grad * y * gate_slope
    values = act[:, :GROUP_WIDTH]
    skip_cols = jnp.sum(y_grad * values, axis=0, keepdims=True)
    pair = 2 * HEAD_DIM
    lane = lax.broadcasted_iota(jnp.int32, (1, pair), 1)
    inner_grad = jnp.zeros_like(inner)
    value_pieces, row_sums, col_sums = [], [], []
    for c in range(GROUP_WIDTH // pair):
        at = slice(c * pair, (c + 1) * pair)
        got = []
        for h in (2 * c, 2 * c + 1):
            own = (lane < HEAD_DIM) if h % 2 == 0 else (lane >= HEAD_DIM)
            mine = jnp.where(own, y_grad[:, at], 0.0)
            decay = head_decay(mask, running, running_t, h)
            step_row = step_t[h : h + 1, :]
            weight_grad = dot(mine, values[:, at], ((1,), (1,))) * decay
            scaled = weight_grad * step_row
            inner_grad = inner_grad + scaled
            col_sums.append(jnp.sum(weight_grad * inner, axis=0, keepdims=True))
            row_sums.append(jnp.sum(scaled * inner, axis=1, keepdims=True))
            weights = decay * inner * step_row
            got.append(dot(weights, mine, ((0,), (0,))))
        value_pieces.append(got[0] + got[1])
    values_grad = jnp.concatenate(value_pieces, axis=1) + r.skip[...] * y_grad
    inputs_grad = dot(inner_grad, outputs, ((0,), (0,)))
    outputs_grad = dot(inner_grad, inputs)
    col_grad = jnp.concatenate(col_sums, axis=0).T
    running_grad = jnp.concatenate(row_sums, axis=1) - col_grad * step
    logd_grad = dot(mask.astype(f32), running_grad, ((0,), (0,)), precision=highest)
    step_grad = (col_grad - logd_grad * jnp.exp(r.log_decay[...])) * jax.nn.sigmoid(step_raw)
    conv_grad = jnp.concatenate([values_grad, inputs_grad, outputs_grad], axis=1) * act_slope
    conv_in_grad = jnp.zeros_like(conv_grad)
    small = r.small_part
    small[...] = jnp.zeros(small.shape, f32)
    for lag in range(CONV):
        small[CONV - 1 - lag : CONV - lag, :] = jnp.sum(
            conv_grad * conv_taps(conv_in, pos, lag), axis=0, keepdims=True
        )
        kept = jnp.where(pos >= lag, conv_grad, 0.0) * r.taps[CONV - 1 - lag : CONV - lag, :]
        conv_in_grad = conv_in_grad + (kept if lag == 0 else pltpu.roll(kept, patches - lag, 0))
    small[CONV : CONV + 1, :] = jnp.sum(conv_grad, axis=0, keepdims=True)
    small[CONV + 1 : CONV + 2, :GROUP_WIDTH] = jnp.sum(gain_rows, axis=0, keepdims=True)
    small[CONV + 2 : CONV + 3, :GROUP_WIDTH] = skip_cols
    small[CONV + 3 : CONV + 4, :GROUP_HEADS] = jnp.sum(step_grad, axis=0, keepdims=True)
    small[CONV + 4 : CONV + 5, :GROUP_HEADS] = jnp.sum(logd_grad * logd, axis=0, keepdims=True)
    return jnp.concatenate([gate_grad, conv_in_grad, step_grad], axis=1).astype(bf16)


def backward_kernel(n, mpn, spill, r):
    p = place_of(n, mpn)
    i, j = p.i, p.j
    micro, rows, dim = r.attn_in.shape
    patches = r.global_own.shape[0]
    slabs = rows // patches
    width = r.qkv_v.shape[2]
    feature = dim // n
    per = dim // mpn
    loads = 0

    def local(src, dst):
        nonlocal loads
        copy = pltpu.make_async_copy(src, dst, r.sem_load.at[loads])
        loads += 1
        copy.start()
        return copy

    def read(view):
        if not spill:
            return view[...]
        copy = pltpu.make_async_copy(view, r.stage.at[0], r.sem_stage.at[0])
        copy.start()
        copy.wait()
        return r.stage[0]

    def write(view, value):
        if not spill:
            view[...] = value
            return
        r.stage[1] = value
        copy = pltpu.make_async_copy(r.stage.at[1], view, r.sem_stage.at[1])
        copy.start()
        copy.wait()

    keep_w = local(r.w_grad.at[:, pl.ds(pl.multiple_of(j * per, per), per)], r.g_recv.at[j])
    load_bytes = local(r.byte_input.at[j], r.own_bytes)
    load_qkv = local(r.qkv_weight, r.qkv_v)
    load_out = local(r.out_weight, r.out_v)
    load_in = local(r.in_weight, r.in_v)
    barrier = pltpu.get_barrier_semaphore()
    pl.semaphore_wait(barrier, greet_all(p, barrier))

    def reduction(block, value, pre, recv, ss, plain):
        ssa, rsa, ssb, rsb = (ss.at[k] for k in range(4))
        get = (lambda view: view[...]) if plain else read
        put = (lambda view, v: view.__setitem__(..., v)) if plain else write

        def spread():
            copies = []
            for d in range(1, p.half):
                q = (p.mine + d) % p.half
                rcopy(pre.at[q], pre.at[q], ssa.at[q], rsa.at[q], p.other, j).wait_recv()
                total = value(q * 2 + p.c).astype(f32)
                put(pre.at[q], (total + get(pre.at[q]).astype(f32)).astype(bf16))
                copy = rcopy(pre.at[q], recv.at[p.mine], ssb.at[q], rsb.at[p.mine], q * 2 + p.c, j)
                copy.start()
                copies.append(copy)
            return copies

        def finish():
            mine = p.mine
            rcopy(pre.at[mine], pre.at[mine], ssa.at[mine], rsa.at[mine], p.other, j).wait_recv()
            total = value(i).astype(f32)
            total = total + get(pre.at[mine]).astype(f32)
            for d in range(1, p.half):
                q = (mine + d) % p.half
                rcopy(recv.at[q], recv.at[q], ssb.at[q], rsb.at[q], q * 2 + p.c, j).wait_recv()
                total = total + get(recv.at[q]).astype(f32)
            return total

        return SimpleNamespace(
            start=lambda: reduce_start(p, block, pre, ssa, rsa), spread=spread, finish=finish
        )

    block_in = lambda s: r.in_part.at[s]
    block_down = lambda s: r.down_part.at[s]
    at_feature = lambda s: pl.ds(pl.multiple_of(s * feature, feature), feature)
    block_ao = lambda s: r.ao_part.at[at_feature(s)]
    block_qkv = lambda s: r.qkv_part.at[:, at_feature(s)]
    sum_in = reduction(block_in, lambda s: read(block_in(s)), r.in_pre, r.in_recv, r.ss_in, False)
    sum_down = reduction(block_down, lambda s: read(block_down(s)), r.down_pre, r.down_recv, r.ss_down, False)
    sum_ao = reduction(block_ao, lambda s: block_ao(s)[...], r.ao_pre, r.ao_recv, r.ss_ao, True)
    sum_qkv = reduction(block_qkv, lambda s: block_qkv(s)[...], r.qkv_pre, r.qkv_recv, r.ss_qkv, True)

    pieces = []
    step = per // GRAD_CUTS
    for w in range(3):
        for k in range(GRAD_CUTS):
            pieces.append((
                lambda t, w=w, k=k: r.w_grad.at[w, pl.ds(pl.multiple_of(t * per + k * step, step), step)],
                lambda s, w=w, k=k: r.g_recv.at[s, w, k * step : (k + 1) * step],
                r.ssw.at[w, k],
                r.rsw.at[w, k],
            ))
    bulk = Bulk(p, pieces)

    sent = sum_in.start()
    bulk.go(1)
    sent += sum_in.spread()
    sent += sum_down.start()
    bulk.go(2)
    load_bytes.wait()
    for k in range(slabs):
        r.local_in[k * patches : (k + 1) * patches, :] = (
            r.own_bytes[:, k * dim : (k + 1) * dim].astype(f32) + r.global_own[...]
        )
    after = r.after[...]
    back, gain_rows = rms_back(after, r.ffn_gain[...], sum_in.finish())
    after_grad = r.own_grad[...].astype(f32) + back
    r.after_grad[...] = after_grad
    r.gains[...] = jnp.zeros(r.gains.shape, f32)
    r.gains[2:3, :] = jnp.sum(gain_rows, axis=0, keepdims=True)
    r.branch[...] = after_grad.astype(bf16)
    for d in range(mpn):
        t = (j + d) % mpn
        r.up[t] = dot(r.branch[...], r.ao_sorted[t], ((1,), (1,))).astype(bf16)
    sent += mp_start(p, lambda t: r.up.at[t], lambda s: r.up_recv.at[s], r.ss1, r.rs1)
    r.up_recv[j] = r.up[j]
    sent += sum_down.spread()
    load_qkv.wait()

    mask = att_mask(rows, patches)
    pair = 2 * ATT_DIM
    lane = lax.broadcasted_iota(jnp.int32, (1, pair), 1)

    def part_copy(t):
        return rcopy(r.att_part.at[t], r.att_recv.at[j], r.ss2.at[t], r.rs2.at[j], i, t)

    def one_micro(d, _):
        m = (j + d) % mpn

        @pl.when(d > 0)
        def _():
            rcopy(r.up_recv.at[m], r.up_recv.at[m], r.ss1.at[m], r.rs1.at[m], i, m).wait_recv()

        for c in range(width // pair):
            at = slice(c * pair, (c + 1) * pair)
            query, key, value = r.qkv[0, m, :, at], r.qkv[1, m, :, at], r.qkv[2, m, :, at]
            up = r.up_recv[m, :, at]
            got = [[], [], []]
            for own in (lane < ATT_DIM, lane >= ATT_DIM):
                mine = jnp.where(own, query, jnp.zeros_like(query))
                probs = soft_rows(mask, mine, key)
                my_up = jnp.where(own, up, jnp.zeros_like(up))
                probs_grad = dot(my_up, value, ((1,), (1,)))
                inner = jnp.sum(probs * probs_grad, axis=1, keepdims=True)
                score_grad = (probs * (probs_grad - inner) * ATT_DIM ** (-0.5)).astype(bf16)
                got[0].append(dot(score_grad, key))
                got[1].append(dot(score_grad, mine, ((0,), (0,))))
                got[2].append(dot(probs.astype(bf16), my_up, ((0,), (0,))))
            r.qkv_low[0, m, :, at] = jnp.where(lane < ATT_DIM, got[0][0], got[0][1]).astype(bf16)
            r.qkv_low[1, m, :, at] = (got[1][0] + got[1][1]).astype(bf16)
            r.qkv_low[2, m, :, at] = (got[2][0] + got[2][1]).astype(bf16)
        total = dot(r.qkv_low[0, m], r.qkv_v[0], ((1,), (1,)))
        total = total + dot(r.qkv_low[1, m], r.qkv_v[1], ((1,), (1,)))
        total = total + dot(r.qkv_low[2, m], r.qkv_v[2], ((1,), (1,)))
        r.att_part[m] = total.astype(bf16)

        @pl.when(d > 0)
        def _():
            part_copy(m).start()

        return 0

    lax.fori_loop(0, mpn, one_micro, 0)

    everything = r.attn_in[...].reshape(micro * rows, dim)
    for w in range(3):
        r.qkv_part[w] = dot(
            everything, r.qkv_low[w].reshape(micro * rows, width), ((0,), (0,))
        ).astype(bf16)
    sent += sum_qkv.start()
    for t in range(mpn):
        r.ao_part[:, t * width : (t + 1) * width] = dot(
            r.branch[...], r.heads_own[t], ((0,), (0,))
        ).astype(bf16)
    sent += sum_ao.start()
    lengths = lambda m: (r.seq_lengths[m, 0], r.seq_lengths[m, 1], r.seq_lengths[m, 2])
    l0, l1, l2 = lengths(j)
    perm = perm_matrix(rows, patches, slabs, l0 + l1 + l2 - i * patches)
    block = (r.after[...] + sum_down.finish()).astype(bf16)
    block = dot(perm, block, ((0,), (0,))).astype(bf16)
    for t in range(mpn):
        r.block[t] = block[:, t * width : (t + 1) * width]
    sent += sum_qkv.spread()
    total = r.att_part[j].astype(f32)
    for d in range(1, mpn):
        total = total + r.att_recv[mp_wait(p, d, lambda s: r.att_recv.at[s], r.ss2, r.rs2)].astype(f32)
    back, gain_rows = rms_back(r.local_in[...], r.attn_gain[...], total)
    local_grad = r.after_grad[...] + back
    global_grad = local_grad[:patches]
    for k in range(1, slabs):
        global_grad = global_grad + local_grad[k * patches : (k + 1) * patches]
    r.global_grad[...] = global_grad
    r.low[...] = global_grad.astype(bf16)
    cast_start(p, r.low, r.mixer, r.ss3, r.rs3)
    r.gains[1:2, :] = jnp.sum(gain_rows, axis=0, keepdims=True)
    share_rows = rows // mpn
    for t in range(mpn):
        r.local[t] = local_grad[t * share_rows : (t + 1) * share_rows].astype(bf16)
    load_out.wait()
    load_in.wait()
    cast_wait(p, r.low, r.mixer, r.ss3, r.rs3)
    bulk.go(2)
    sent += sum_ao.spread()

    upstream = r.mixer[...].reshape(n * patches, dim)
    proj_grad = mixer_bwd(r, p, lengths(p.m), upstream)
    part = dot(proj_grad, r.in_v[...])
    for b in range(n):
        r.mix_part[b] = part[b * patches : (b + 1) * patches]
    owner_start(p, r.mix_part, r.mix_recv, r.ss4, r.rs4)

    half_cols = dim // p.reps
    normed_half = r.normed[:, :, pl.ds(pl.multiple_of(p.h * half_cols, half_cols), half_cols)]
    in_grad = dot(proj_grad, normed_half.reshape(n * patches, half_cols), ((0,), (0,))).astype(bf16)
    columns = in_grad.shape[0]
    for e in range(p.share):
        r.in_w_part[e, :columns, :] = in_grad[:, e * feature : (e + 1) * feature]
        r.in_w_part[e, columns:, :] = jnp.zeros((r.in_w_part.shape[1] - columns, feature), bf16)
    out_grad = dot(r.mixer_low[...], upstream, ((0,), (0,))).astype(bf16)
    group_rows = GROUP_WIDTH // n
    for e in range(n):
        r.out_w_part[e] = out_grad[e * group_rows : (e + 1) * group_rows]
    bundles = (
        (lambda e: r.in_w_part.at[e], r.in_w_recv, r.ssi, r.rsi),
        (lambda e: r.out_w_part.at[p.h * p.share + e], r.out_w_recv, r.sso, r.rso),
        (lambda e: r.small_part, r.small_recv, r.sss, r.rss),
    )

    def bundle_copies(e):
        return [
            rcopy(src(e), dst.at[p.m], ss.at[e], rs.at[p.m], p.h * p.share + e, j)
            for src, dst, ss, rs in bundles
        ]

    def start_bundles():
        for e in range(p.share):
            @pl.when(p.h * p.share + e != i)
            def _():
                for copy in bundle_copies(e):
                    copy.start()

            @pl.when(p.h * p.share + e == i)
            def _():
                r.in_w_recv[p.m] = r.in_w_part[e]
                r.out_w_recv[p.m] = r.out_w_part[i]
                r.small_recv[p.m] = r.small_part[...]

    owner_wait(p, r.mix_part, r.mix_recv, r.ss4, r.rs4)
    total = r.mix_recv[0]
    for s in range(1, mpn):
        total = total + r.mix_recv[s]
    back, gain_rows = rms_back(r.global_in[...], r.norm_in_gain[...], total)
    r.line[j] = (r.global_grad[...] + back).astype(bf16)
    sent += mp_start(p, lambda t: r.line.at[j], lambda s: r.line.at[s], r.ss5, r.rs5)
    r.gains[0:1, :] = jnp.sum(gain_rows, axis=0, keepdims=True)
    r.gains_line[j] = r.gains[...]
    sent += mp_start(p, lambda t: r.gains, lambda s: r.gains_line.at[s], r.ssg, r.rsg)
    sent += mp_start(p, lambda t: r.local.at[t], lambda s: r.local_all.at[s], r.ss6, r.rs6)
    sent += mp_start(p, lambda t: r.block.at[t], lambda s: r.block_all.at[s], r.ss7, r.rs7)
    r.local_all[j] = r.local[j]
    r.block_all[j] = r.block[j]
    for d in range(1, mpn):
        mp_wait(p, d, lambda s: r.line.at[s], r.ss5, r.rs5)
    slot = lambda s: r.plane.at[s]
    sent += plane_start(p, r.line, slot, r.ssp, r.rsp, r.sspr)
    keep_line = local(r.line, r.plane.at[i])
    start_bundles()
    r.qkv_sum[...] = sum_qkv.finish()
    ao = sum_ao.finish().astype(bf16)
    for t in range(mpn):
        r.ao[t] = ao[:, t * width : (t + 1) * width]
    sent += mp_start(p, lambda t: r.ao.at[t], lambda s: r.ao_all.at[s], r.ss8, r.rs8)
    r.ao_all[j] = r.ao[j]
    bulk.go(len(pieces))
    for d in range(1, mpn):
        mp_wait(p, d, lambda s: r.gains_line.at[s], r.ssg, r.rsg)
    r.gains_plane[p.mine] = sum(r.gains_line[s] for s in range(mpn))
    for d in range(1, p.half):
        q = (p.mine + d) % p.half
        copy = rcopy(
            r.gains_plane.at[p.mine], r.gains_plane.at[p.mine], r.ssh.at[q], r.rsh.at[p.mine], q * 2 + p.c, j
        )
        copy.start()
        sent.append(copy)
    sent += plane_relay(p, slot, r.ssp, r.rsp, r.sspr)
    for d in range(1, p.half):
        q = (p.mine + d) % p.half
        rcopy(r.gains_plane.at[q], r.gains_plane.at[q], r.ssh.at[q], r.rsh.at[q], q * 2 + p.c, j).wait_recv()
    r.gains_pair[0] = sum(r.gains_plane[s] for s in range(p.half))
    pair_copy = rcopy(r.gains_pair.at[0], r.gains_pair.at[1], r.ssq.at[0], r.rsq.at[0], p.other, j)
    pair_copy.start()
    plane_finish(p, slot, r.rsp, r.sspr)
    for d in range(1, mpn):
        mp_wait(p, d, lambda s: r.local_all.at[s], r.ss6, r.rs6)
        mp_wait(p, d, lambda s: r.block_all.at[s], r.ss7, r.rs7)
        mp_wait(p, d, lambda s: r.ao_all.at[s], r.ss8, r.rs8)
    group = i // p.share
    for t in range(mpn):
        @pl.when(t * p.reps + group != i)
        def _():
            for src, dst, ss, rs in bundles:
                rcopy(src(0), dst.at[t], ss.at[0], rs.at[t], t * p.reps + group, j).wait_recv()
    pair_copy.wait()
    r.gains_all[...] = r.gains_pair[0] + r.gains_pair[1]
    bulk.finish()
    keep_w.wait()
    keep_line.wait()
    for copy in sent + bulk.copies:
        copy.wait_send()
    cast_sent(p, r.low, r.mixer, r.ss3, r.rs3)
    owner_sent(p, r.mix_part, r.mix_recv, r.ss4, r.rs4)
    for d in range(1, mpn):
        part_copy((j + d) % mpn).wait_send()
    for e in range(p.share):
        @pl.when(p.h * p.share + e != i)
        def _():
            for copy in bundle_copies(e):
                copy.wait_send()


def backward(n, mpn, a):
    micro, rows, dim = a.attn_in.shape
    patches = a.global_own.shape[0]
    width = a.qkv_weight.shape[2]
    hidden = a.w_grad.shape[2]
    columns = a.in_weight.shape[0]
    half, share = n // 2, mpn
    feature = dim // n
    per = dim // mpn
    seq = n * patches
    spill = n * rows * dim * 2 > SPILL_BYTES
    ins = dict(seq_lengths=(a.seq_lengths, SMEM))
    for name in ("byte_input", "w_grad", "in_weight", "out_weight", "qkv_weight"):
        ins[name] = (getattr(a, name), ANY)
    for name in ("in_part", "down_part"):
        ins[name] = (getattr(a, name), ANY if spill else VMEM)
    for name in (
        "after", "own_grad", "heads_own", "qkv", "attn_in", "ao_sorted", "global_in", "global_own", "normed",
        "projected", "mixer_y", "mixer_low", "norm_in_gain", "taps", "conv_bias", "step_bias", "log_decay",
        "skip", "group_gain", "attn_gain", "ffn_gain",
    ):
        ins[name] = (getattr(a, name), VMEM)
    padded = (columns + 15) // 16 * 16
    outs = dict(
        g_recv=((mpn, 3, per, hidden), bf16, ANY),
        plane=((n, mpn, patches, dim), bf16, ANY),
        qkv_sum=((3, feature, width), f32, VMEM),
        ao_all=((mpn, feature, width), bf16, VMEM),
        in_w_recv=((mpn, padded, feature), bf16, VMEM),
        out_w_recv=((mpn, GROUP_WIDTH // n, dim), bf16, VMEM),
        small_recv=((mpn, 16, CONV_CH), f32, VMEM),
        gains_all=((8, dim), f32, VMEM),
        local_all=((mpn, rows // mpn, dim), bf16, VMEM),
        block_all=((mpn, rows, width), bf16, VMEM),
    )
    scratch = {}
    for name in ("in_pre", "in_recv", "down_pre", "down_recv"):
        if spill:
            outs[name] = ((half, rows, dim), bf16, ANY)
        else:
            scratch[name] = pltpu.VMEM((half, rows, dim), bf16)
    if spill:
        scratch.update(stage=pltpu.VMEM((2, rows, dim), bf16), sem_stage=DMA((2,)))
    scratch.update(
        own_bytes=pltpu.VMEM(a.byte_input.shape[1:], bf16),
        in_v=pltpu.VMEM(a.in_weight.shape, bf16),
        out_v=pltpu.VMEM(a.out_weight.shape, bf16),
        qkv_v=pltpu.VMEM(a.qkv_weight.shape, bf16),
        local_in=pltpu.VMEM((rows, dim), f32),
        after_grad=pltpu.VMEM((rows, dim), f32),
        branch=pltpu.VMEM((rows, dim), bf16),
        up=pltpu.VMEM((mpn, rows, width), bf16),
        up_recv=pltpu.VMEM((mpn, rows, width), bf16),
        qkv_low=pltpu.VMEM((3, micro, rows, width), bf16),
        att_part=pltpu.VMEM((micro, rows, dim), bf16),
        att_recv=pltpu.VMEM((mpn, rows, dim), bf16),
        qkv_part=pltpu.VMEM((3, dim, width), bf16),
        qkv_pre=pltpu.VMEM((half, 3, feature, width), bf16),
        qkv_recv=pltpu.VMEM((half, 3, feature, width), bf16),
        ao_part=pltpu.VMEM((dim, mpn * width), bf16),
        ao_pre=pltpu.VMEM((half, feature, mpn * width), bf16),
        ao_recv=pltpu.VMEM((half, feature, mpn * width), bf16),
        ao=pltpu.VMEM((mpn, feature, width), bf16),
        block=pltpu.VMEM((mpn, rows, width), bf16),
        local=pltpu.VMEM((mpn, rows // mpn, dim), bf16),
        low=pltpu.VMEM((patches, dim), bf16),
        global_grad=pltpu.VMEM((patches, dim), f32),
        mixer=pltpu.VMEM((n, patches, dim), bf16),
        mix_part=pltpu.VMEM((n, patches, dim), f32),
        mix_recv=pltpu.VMEM((mpn, patches, dim), f32),
        line=pltpu.VMEM((mpn, patches, dim), bf16),
        in_w_part=pltpu.VMEM((share, padded, feature), bf16),
        out_w_part=pltpu.VMEM((n, GROUP_WIDTH // n, dim), bf16),
        small_part=pltpu.VMEM((16, CONV_CH), f32),
        gains=pltpu.VMEM((8, dim), f32),
        gains_line=pltpu.VMEM((mpn, 8, dim), f32),
        gains_plane=pltpu.VMEM((half, 8, dim), f32),
        gains_pair=pltpu.VMEM((2, 8, dim), f32),
        sem_load=DMA((8,)),
        ss_in=DMA((4, half)), ss_down=DMA((4, half)), ss_ao=DMA((4, half)), ss_qkv=DMA((4, half)),
        ss1=DMA((mpn,)), rs1=DMA((mpn,)), ss2=DMA((mpn,)), rs2=DMA((mpn,)), ss3=DMA((n,)), rs3=DMA((n,)),
        ss4=DMA((mpn,)), rs4=DMA((mpn,)), ss5=DMA((mpn,)), rs5=DMA((mpn,)), ss6=DMA((mpn,)), rs6=DMA((mpn,)),
        ss7=DMA((mpn,)), rs7=DMA((mpn,)), ss8=DMA((mpn,)), rs8=DMA((mpn,)),
        ssp=DMA((half,)), rsp=DMA((n,)), sspr=DMA((half,)),
        ssg=DMA((mpn,)), rsg=DMA((mpn,)), ssh=DMA((half,)), rsh=DMA((half,)), ssq=DMA((1,)), rsq=DMA((1,)),
        ssi=DMA((share,)), rsi=DMA((mpn,)), sso=DMA((share,)), rso=DMA((mpn,)),
        sss=DMA((share,)), rss=DMA((mpn,)),
        ssw=DMA((3, GRAD_CUTS, mpn)), rsw=DMA((3, GRAD_CUTS, mpn)),
    )
    return launch("backward", partial(backward_kernel, n, mpn, spill), ins, outs, scratch, remote_params(1, 60))


def finish_kernel(r):
    i = lax.axis_index("dp")
    mpn, patches, dim = r.plane.shape[1:]
    n = r.plane.shape[0]
    features = r.bytes_part.shape[-1]
    positions = r.patch_weight.shape[0]
    feature = dim // n
    everyone = r.plane[...].reshape(n * mpn * patches, dim)
    own = r.plane[i].reshape(mpn * patches, dim)
    for k in range(positions):
        mine = r.bytes_part[:, k].reshape(n * mpn * patches, features)
        got = dot(mine, everyone, ((0,), (0,)))
        if features != feature:
            cut = features // feature
            got = sum(
                jnp.where(i % cut == e, got[e * feature : (e + 1) * feature], 0.0) for e in range(cut)
            )
        r.patch_grad[k] = got
        piece = dot(own, r.patch_weight[k], ((1,), (1,)))
        for m in range(mpn):
            r.input_grad[m, :, k * dim : (k + 1) * dim] = (
                piece[m * patches : (m + 1) * patches]
                + r.local_all[m, k * patches : (k + 1) * patches, :].astype(f32)
            )
    for w in range(3):
        r.ffn_grad[w] = sum(r.g_recv[s, w].astype(f32) for s in range(mpn))
    r.ao_grad[...] = sum(r.ao_all[s].astype(f32) for s in range(mpn)).T
    columns = r.in_grad.shape[0]
    r.in_grad[...] = sum(r.in_w_recv[s, :columns, :].astype(f32) for s in range(mpn))
    r.out_grad[...] = sum(r.out_w_recv[s].astype(f32) for s in range(mpn))
    small = sum(r.small_recv[s] for s in range(mpn))

    def chosen(values, size):
        whole = values.shape[1]
        at = lax.broadcasted_iota(jnp.int32, (whole, size), 0)
        want = lax.broadcasted_iota(jnp.int32, (whole, size), 1) + i * size
        return dot(values, (at == want).astype(f32), precision=highest)

    conv = chosen(small, CONV_CH // n)
    r.conv_w_grad[...] = conv[:CONV]
    r.conv_b_grad[...] = conv[CONV : CONV + 1]
    group = chosen(small[:, :GROUP_WIDTH], GROUP_WIDTH // n)
    r.group_grad[...] = group[CONV + 1 : CONV + 2]
    heads = lax.broadcasted_iota(jnp.int32, (GROUP_WIDTH, GROUP_HEADS), 0) // HEAD_DIM
    pick = heads == lax.broadcasted_iota(jnp.int32, (GROUP_WIDTH, GROUP_HEADS), 1)
    skip = dot(small[:, :GROUP_WIDTH], pick.astype(f32), precision=highest)
    r.skip_grad[...] = skip[CONV + 2 : CONV + 3]
    r.step_grad[...] = small[CONV + 3 : CONV + 4, :GROUP_HEADS]
    r.decay_grad[...] = small[CONV + 4 : CONV + 5, :GROUP_HEADS]
    gains = chosen(r.gains_all[...], feature)
    r.norm_in_grad[...] = gains[0:1]
    r.attn_gain_grad[...] = gains[1:2]
    r.ffn_gain_grad[...] = gains[2:3]
    r.qkv_grad[...] = r.qkv_sum[...]
    r.block_out[...] = r.block_all[...]


def finish(a):
    n, mpn, patches, dim = a.plane.shape
    positions = a.patch_weight.shape[0]
    feature = dim // n
    columns = a.in_weight.shape[0]
    names = (
        "plane", "bytes_part", "patch_weight", "local_all", "g_recv", "ao_all", "in_w_recv", "out_w_recv",
        "small_recv", "gains_all", "qkv_sum", "block_all",
    )
    row = lambda size: ((1, size), f32, VMEM)
    outs = dict(
        patch_grad=((positions, feature, dim), f32, VMEM),
        input_grad=((mpn, patches, positions * dim), f32, VMEM),
        ffn_grad=(a.g_recv.shape[1:], f32, VMEM),
        ao_grad=(a.ao_all.shape[:0:-1], f32, VMEM),
        in_grad=((columns, feature), f32, VMEM),
        out_grad=(a.out_w_recv.shape[1:], f32, VMEM),
        conv_w_grad=((CONV, CONV_CH // n), f32, VMEM),
        conv_b_grad=row(CONV_CH // n),
        group_grad=row(GROUP_WIDTH // n),
        skip_grad=row(GROUP_HEADS),
        step_grad=row(GROUP_HEADS),
        decay_grad=row(GROUP_HEADS),
        norm_in_grad=row(feature),
        attn_gain_grad=row(feature),
        ffn_gain_grad=row(feature),
        qkv_grad=(a.qkv_sum.shape, f32, VMEM),
        block_out=(a.block_all.shape, bf16, VMEM),
    )
    ins = {name: (getattr(a, name), VMEM) for name in names}
    return launch("finish", finish_kernel, ins, outs, {}, plain_params())


def body(
    byte_input,
    seq_lengths,
    patch_weight,
    norm_in_gain,
    in_weight,
    conv_weight,
    conv_bias,
    step_bias,
    log_decay,
    skip_gain,
    group_gain,
    out_weight,
    attn_gain,
    qkv_weight,
    attn_out_weight,
    ffn_gain,
    ffn_weight,
    out_grad,
):
    n, mpn = lax.axis_size("dp"), lax.axis_size("mp")
    row = lambda v: v.reshape(1, -1)
    a = SimpleNamespace(
        byte_input=byte_input,
        seq_lengths=seq_lengths,
        patch_weight=patch_weight,
        norm_in_gain=row(norm_in_gain),
        in_weight=in_weight[0].T,
        taps=conv_weight[0].T,
        conv_bias=conv_bias,
        step_bias=step_bias,
        log_decay=log_decay,
        skip=row(jnp.repeat(skip_gain[0], HEAD_DIM)),
        group_gain=group_gain,
        out_weight=out_weight[0],
        attn_gain=row(attn_gain),
        qkv_weight=qkv_weight,
        attn_out_weight=attn_out_weight,
        ffn_gain=row(ffn_gain),
        ffn_weight=ffn_weight,
        out_grad=out_grad,
    )
    a.__dict__.update(forward(n, mpn, a).__dict__)
    a.down_part, a.in_part, a.w_grad = ffn(a.ffn_rows, a.grad_rows, a.w_all)
    a.__dict__.update(backward(n, mpn, a).__dict__)
    f = finish(a)
    return (
        f.block_out,
        f.input_grad,
        f.patch_grad,
        f.norm_in_grad[0],
        f.in_grad.T[None],
        f.conv_w_grad.T[None],
        f.conv_b_grad,
        f.step_grad,
        f.decay_grad,
        f.skip_grad,
        f.group_grad,
        f.out_grad[None],
        f.attn_gain_grad[0],
        f.qkv_grad,
        f.ao_grad,
        f.ffn_gain_grad[0],
        f.ffn_grad,
    )


def solution(mesh):
    in_specs = (
        P(None, "dp", None),
        P(),
        P("mp", None, None),
        P(),
        P("mp", None, None),
        P("mp", None, None),
        P("mp", None),
        P("mp", None),
        P("mp", None),
        P("mp", None),
        P("mp", None),
        P("mp", None, None),
        P(),
        P(None, None, "mp"),
        P("mp", None),
        P(),
        P(None, "mp", "dp"),
        P(None, "dp", None),
    )
    out_specs = (
        P(None, "dp", "mp"),
        P(None, "dp", "mp"),
        P("mp", "dp", None),
        P("dp"),
        P("mp", "dp", None),
        P("mp", "dp", None),
        P("mp", "dp"),
        P("mp", None),
        P("mp", None),
        P("mp", None),
        P("mp", "dp"),
        P("mp", "dp", None),
        P("dp"),
        P(None, "dp", "mp"),
        P("mp", "dp"),
        P("dp"),
        P(None, "mp", "dp"),
    )
    return jax.shard_map(body, mesh=mesh, in_specs=in_specs, out_specs=out_specs, check_vma=False)
```

time: 2730 us -> 324 us (0.12)
  waiting for transfers between devices: 1660 us -> 0 us
  Pallas kernels: 0 us -> 318 us
  matrix products: 282 us -> 0 us
  local copies, waits for them, and re-layouts: 277 us -> 1.38 us
  other arithmetic: 257 us -> 0 us
  blocking collectives: 192 us -> 0 us
    psum x6 -> x0, waiting for transfers between devices: 1000 us -> none  [the longest x1 841 us: body(): lax.psum(jnp.einsum('tc,kcf->ktf', ffn_rows_in, ffn_weight[:2], preferred...]
    reduce_scatter x13 -> x0, waiting for transfers between devices: 449 us -> none  [the longest x8 178 us: spread_rows(): return lax.psum_scatter(terms, 'dp', scatter_dimension=0, tiled=True)]
    pallas_call x0 -> x4, Pallas kernels: none -> 318 us  [the longest x3 296 us: launch(): pl.pallas_call(run, out_shape=tuple((jax.ShapeDtypeStruct(shape, dtype) f...]
    dot_general x152 -> x0, matrix products: 273 us -> none  [the longest x12 27 us: block_terms(): jnp.einsum('sgh,sghe,sgn->ghen', to_end, values, inputs, precision=highest)]
    unnamed x39 -> x0, waiting for transfers between devices: 187 us -> none
    all_gather x16 -> x0, blocking collectives: 182 us -> none  [the longest x8 75 us: gather_rows(): return lax.all_gather(features, 'dp', axis=0, tiled=True)]
    select_n x64 -> x0, other arithmetic: 92 us -> none  [turn(): return jax.tree.map(lambda a, b: jnp.where(reached, a, b), new, before)]
    unnamed x1112 -> x0, local copies, waits for them, and re-layouts: 72.3 us -> none
  transfers between devices with their start and end apart: 41 -> 0, of which waited for: 26 -> 0; matrix products, arithmetic and copies ran while one was open for 17% -> 0% of each run, Pallas kernels for 0% -> 0%
where the time goes in v2:
time: 324 us; the launch traced here: 320 us
  Pallas kernels  318 us (98%)
    pallas_call x3, Pallas kernels, launch(): pl.pallas_call(run, out_shape=tuple((jax.ShapeDtypeStruct(shape, dtype) f...  296 us
    pallas_call x1, Pallas kernels, ffn(): pl.pallas_call(ffn_kernel, out_shape=(jax.ShapeDtypeStruct((blocks, rows,...  22.4 us

profile of v2, /device:TPU:2, one launch (start us, length us, event | category | flops | bytes accessed | tf_op | source)
XLA Modules:
  0.0 320.4 jit_solution(3376718582259737569)
XLA Ops:
  0.7 0.7 broadcast_in_dim.12
  1.4 0.7 reshape_reshape.3.refs_14_.refs_25_
  2.0 117.7 %forward.1 = (bf16[8,128,1024]{2,1,0:T(8,128)(2,1)}, bf16[8,128,1024]{2,1,0:T(8,128)(2,1)}, bf16[4,3,256,512]{3,2,1,0:T(8,128)(2,1)}, bf16[8,2,4,16,128]{4,3,2,1...) custom-call(s32[4,3]{1,0:T(4,128)} %refs_0_.3, ...), custom_call_target="tpu_custom_call" | custom-call | tf_op jit(solution)/shard_map/forward/pallas_call | solution.py:89
  119.8 22.4 %ffn.1 = (bf16[8,128,1024]{2,1,0:T(8,128)(2,1)}, bf16[8,128,1024]{2,1,0:T(8,128)(2,1)}, bf16[3,1024,512]{2,1,0:T(8,128)(2,1)}) custom-call(bf16[8,128,1024]{2,1,0:T(8,128)(2,1)} %get-tuple-element.63.rows_in, bf16[8,128,1024]{2,1,0:T(8,128)(2,1)} %get-tuple-element.64.grads_in, bf16[4,3,256,512]{3,2,1,0:T(8,128)(2,1)} %get-tuple-element.65.parts), custom_call_target="tpu_custom_call" | custom-call | tf_op jit(solution)/shard_map/ffn/pallas_call | solution.py:643
  142.1 169.3 %backward.1 = (bf16[4,3,256,512]{3,2,1,0:T(8,128)(2,1)}, bf16[8,4,16,1024]{3,2,1,0:T(8,128)(2,1)}, f32[3,128,256]{2,1,0:T(8,128)}, bf16[4,128,256]{2,1,0:T(8,128...) custom-call(s32[4,3]{1,0:T(4,128)} %refs_0_.3, ...), custom_call_target="tpu_custom_call" | custom-call | tf_op jit(solution)/shard_map/backward/pallas_call | solution.py:89
  311.4 8.9 %finish.1 = (f32[2,128,1024]{2,1,0:T(8,128)}, f32[4,16,2048]{2,1,0:T(8,128)}, f32[3,256,512]{2,1,0:T(8,128)}, f32[256,128]{1,0:T(8,128)}, f32[1288,128]{1,0:T(8,...) custom-call(bf16[8,4,16,1024]{3,2,1,0:T(8,128)(2,1)} %get-tuple-elem, ...), custom_call_target="tpu_custom_call" | custom-call | tf_op jit(solution)/shard_map/finish/pallas_call | solution.py:89

commit v3 on v2

v3 whole, which is shorter than its diff:
```python
from functools import partial
from types import SimpleNamespace

import jax
import jax.numpy as jnp
from jax import lax
from jax.experimental import pallas as pl
from jax.experimental.pallas import tpu as pltpu
from jax.sharding import PartitionSpec as P

STATE = 128
CONV = 4
SEQS = 3
GROUP_WIDTH = 512
GROUP_HEADS = 8
HEAD_DIM = 64
ATT_DIM = 64
CONV_CH = 768

norm_eps = 1e-06
highest = lax.Precision.HIGHEST
large_negative = -1e30
f32 = jnp.float32
bf16 = jnp.bfloat16
MESH = pl.DeviceIdType.MESH
VMEM = pl.BlockSpec(memory_space=pltpu.VMEM)
ANY = pl.BlockSpec(memory_space=pl.ANY)
SMEM = pl.BlockSpec(memory_space=pltpu.SMEM)
DMA = pltpu.SemaphoreType.DMA
SMALL_PARAMS = (
    "norm_in_gain", "taps", "conv_bias", "step_bias", "log_decay", "skip", "group_gain", "attn_gain", "ffn_gain"
)
SPILL_BYTES = 4 * 2**20
FFN_COLS = 256
WEIGHT_CUTS = 2
PACE = (1, 1, 1, 1, 2, 6)
PACE_FFN = 2
PACE_BACK = (1, 1, 2, 1)
BUNDLES_FIRST = True


def dot(a, b, dims=((1,), (0,)), precision=None):
    return lax.dot_general(
        a, b, (dims, ((), ())), preferred_element_type=f32, precision=precision
    )


def inv_rms(values):
    return lax.rsqrt(jnp.mean(values * values, axis=-1, keepdims=True) + norm_eps)


def rms_back(values, gain, upstream):
    scale = inv_rms(values)
    weighted = upstream * gain
    inner = jnp.mean(weighted * values, axis=-1, keepdims=True)
    back = scale * weighted - values * (inner * scale * scale * scale)
    return back, upstream * (values * scale)


def silu_pair(values):
    sig = jax.nn.sigmoid(values)
    return values * sig, sig * (1.0 + values * (1.0 - sig))


def rcopy(src, dst, send_sem, recv_sem, dp, mp):
    return pltpu.make_async_remote_copy(
        src_ref=src,
        dst_ref=dst,
        send_sem=send_sem,
        recv_sem=recv_sem,
        device_id={"dp": dp, "mp": mp},
        device_id_type=MESH,
    )


def greet(barrier, dp, mp):
    pl.semaphore_signal(barrier, inc=1, device_id={"dp": dp, "mp": mp}, device_id_type=MESH)


def plain_params(mib=56):
    return pltpu.CompilerParams(vmem_limit_bytes=mib * 2**20)


def remote_params(cid, mib=40):
    return pltpu.CompilerParams(
        collective_id=cid, has_side_effects=True, vmem_limit_bytes=mib * 2**20
    )


def launch(name, kernel, ins, outs, scratch, params):
    names = [*ins, *outs, *scratch]

    def run(*refs):
        kernel(SimpleNamespace(**dict(zip(names, refs))))

    results = pl.pallas_call(
        run,
        out_shape=tuple(jax.ShapeDtypeStruct(shape, dtype) for shape, dtype, _ in outs.values()),
        in_specs=[spec for _, spec in ins.values()],
        out_specs=tuple(spec for _, _, spec in outs.values()),
        scratch_shapes=list(scratch.values()),
        compiler_params=params,
        name=name,
    )(*[array for array, _ in ins.values()])
    return SimpleNamespace(**dict(zip(outs, results)))


def place_of(n, mpn):
    i, j = lax.axis_index("dp"), lax.axis_index("mp")
    reps = n // mpn
    return SimpleNamespace(
        n=n, mpn=mpn, i=i, j=j, reps=reps, share=n // reps, half=n // 2,
        m=i // reps, h=i % reps, c=i % 2, mine=i // 2, other=i + 1 - 2 * (i % 2), inside=i // reps == j,
    )


def greet_all(p, barrier):
    for d in range(1, p.mpn):
        greet(barrier, p.i, (p.j + d) % p.mpn)
    for d in range(1, p.n):
        greet(barrier, (p.i + d) % p.n, p.j)
    for s in range(p.n):
        @pl.when(jnp.logical_not((s == p.i) & p.inside))
        def _():
            greet(barrier, s, p.m)
    for h in range(p.reps):
        for t in range(p.mpn):
            @pl.when(jnp.logical_not((p.j * p.reps + h == p.i) & (t == p.j)))
            def _():
                greet(barrier, p.j * p.reps + h, t)
    return p.mpn + 3 * p.n - 2 - 2 * p.inside.astype(jnp.int32)


class Exchange:
    def __init__(self, p, src, dst, ss, rs):
        self.p, self.src, self.dst, self.ss, self.rs = p, src, dst, ss, rs

    def copy(self, t):
        p = self.p
        return rcopy(self.src(t), self.dst(p.j), self.ss.at[t], self.rs.at[p.j], p.i, t)

    def start(self):
        for d in range(1, self.p.mpn):
            self.copy((self.p.j + d) % self.p.mpn).start()
        return self

    def wait(self, d):
        s = (self.p.j + d) % self.p.mpn
        rcopy(self.dst(s), self.dst(s), self.ss.at[s], self.rs.at[s], self.p.i, s).wait_recv()
        return s

    def wait_all(self):
        for d in range(1, self.p.mpn):
            self.wait(d)

    def sent(self):
        for d in range(1, self.p.mpn):
            self.copy((self.p.j + d) % self.p.mpn).wait_send()


class Bulk:
    def __init__(self, exchanges):
        self.exchanges, self.begun = exchanges, 0

    def go(self, count):
        for exchange in self.exchanges[self.begun : self.begun + count]:
            exchange.start()
        self.begun += count

    def sent(self):
        for exchange in self.exchanges:
            exchange.sent()


class PlaneGather:
    def __init__(self, p, own, slot, ss, rs, ssr):
        self.p, self.own, self.slot, self.ss, self.rs, self.ssr = p, own, slot, ss, rs, ssr

    def direct(self, q):
        p = self.p
        return rcopy(self.own, self.slot(p.i), self.ss.at[q], self.rs.at[p.i], q * 2 + p.c, p.j)

    def across(self, q):
        p = self.p
        s = q * 2 + p.c
        return rcopy(self.slot(s), self.slot(s), self.ssr.at[q], self.rs.at[s], p.other, p.j)

    def own_across(self):
        p = self.p
        return rcopy(self.own, self.slot(p.i), self.ssr.at[p.mine], self.rs.at[p.i], p.other, p.j)

    def others(self):
        return [(self.p.mine + d) % self.p.half for d in range(1, self.p.half)]

    def start(self):
        self.own_across().start()
        for q in self.others():
            self.direct(q).start()
        return self

    def relay_one(self, q):
        s = q * 2 + self.p.c
        rcopy(self.slot(s), self.slot(s), self.ss.at[q], self.rs.at[s], s, self.p.j).wait_recv()
        self.across(q).start()

    def wait_across(self, q):
        s = q * 2 + 1 - self.p.c
        rcopy(self.slot(s), self.slot(s), self.ssr.at[q], self.rs.at[s], self.p.other, self.p.j).wait_recv()

    def relay(self):
        for q in reversed(self.others()):
            self.relay_one(q)

    def finish(self):
        for q in range(self.p.half):
            self.wait_across(q)

    def sent(self):
        self.own_across().wait_send()
        for q in self.others():
            self.direct(q).wait_send()
            self.across(q).wait_send()


class Reduction:
    def __init__(self, p, block, value, pre, recv, ss, get, put):
        self.p, self.block, self.value, self.pre, self.recv, self.get, self.put = p, block, value, pre, recv, get, put
        self.ssa, self.rsa, self.ssb, self.rsb = (ss.at[k] for k in range(4))

    def first(self, q):
        p = self.p
        return rcopy(self.block(q * 2 + 1 - p.c), self.pre.at[q], self.ssa.at[q], self.rsa.at[q], p.other, p.j)

    def second(self, q):
        p = self.p
        return rcopy(self.pre.at[q], self.recv.at[p.mine], self.ssb.at[q], self.rsb.at[p.mine], q * 2 + p.c, p.j)

    def others(self):
        return [(self.p.mine + d) % self.p.half for d in range(1, self.p.half)]

    def start(self):
        for q in self.others() + [self.p.mine]:
            self.first(q).start()

    def spread_one(self, q):
        p = self.p
        rcopy(self.pre.at[q], self.pre.at[q], self.ssa.at[q], self.rsa.at[q], p.other, p.j).wait_recv()
        total = self.value(q * 2 + p.c).astype(f32)
        self.put(self.pre.at[q], (total + self.get(self.pre.at[q]).astype(f32)).astype(bf16))
        self.second(q).start()

    def spread(self):
        for q in self.others():
            self.spread_one(q)

    def finish(self):
        p, mine = self.p, self.p.mine
        rcopy(self.pre.at[mine], self.pre.at[mine], self.ssa.at[mine], self.rsa.at[mine], p.other, p.j).wait_recv()
        total = self.value(p.i).astype(f32)
        total = total + self.get(self.pre.at[mine]).astype(f32)
        for q in self.others():
            rcopy(self.recv.at[q], self.recv.at[q], self.ssb.at[q], self.rsb.at[q], q * 2 + p.c, p.j).wait_recv()
            total = total + self.get(self.recv.at[q]).astype(f32)
        return total

    def sent(self):
        for q in self.others() + [self.p.mine]:
            self.first(q).wait_send()
        for q in self.others():
            self.second(q).wait_send()


def plain_get(view):
    return view[...]


def plain_put(view, value):
    view[...] = value


class Cast:
    def __init__(self, p, low, dst, ss, rs):
        self.p, self.low, self.dst, self.ss, self.rs = p, low, dst, ss, rs

    def each(self, act):
        p = self.p
        for h in range(p.reps):
            for t in range(p.mpn):
                here = (p.j * p.reps + h == p.i) & (t == p.j)

                @pl.when(jnp.logical_not(here))
                def _():
                    act(rcopy(
                        self.low, self.dst.at[p.i], self.ss.at[h * p.mpn + t], self.rs.at[p.i], p.j * p.reps + h, t
                    ))

    def start(self):
        self.each(lambda copy: copy.start())

        @pl.when(self.p.inside)
        def _():
            self.dst[self.p.i] = self.low[...]

    def wait(self):
        p = self.p
        for s in range(p.n):
            @pl.when(jnp.logical_not((s == p.i) & p.inside))
            def _():
                rcopy(self.low, self.dst.at[s], self.ss.at[0], self.rs.at[s], s, p.m).wait_recv()

    def sent(self):
        self.each(lambda copy: copy.wait_send())


class ToOwner:
    def __init__(self, p, part, recv, ss, rs):
        self.p, self.part, self.recv, self.ss, self.rs = p, part, recv, ss, rs

    def each(self, act):
        p = self.p
        for q in range(p.share):
            block = q * p.reps + p.h

            @pl.when(jnp.logical_not((block == p.i) & p.inside))
            def _():
                act(rcopy(self.part.at[block], self.recv.at[p.j], self.ss.at[q], self.rs.at[p.j], block, p.m))

    def start(self):
        self.each(lambda copy: copy.start())

        @pl.when(self.p.inside)
        def _():
            self.recv[self.p.j] = self.part[self.p.i]

    def wait(self):
        p = self.p
        for s in range(p.mpn):
            @pl.when(jnp.logical_not(p.inside & (s == p.j)))
            def _():
                rcopy(
                    self.part.at[0], self.recv.at[s], self.ss.at[0], self.rs.at[s], p.j * p.reps + p.h, s
                ).wait_recv()

    def total(self):
        self.wait()
        return sum(self.recv[s].astype(f32) for s in range(self.p.mpn))

    def sent(self):
        self.each(lambda copy: copy.wait_send())


def perm_matrix(rows, patches, per, limit):
    at = lax.broadcasted_iota(jnp.int32, (rows, rows), 0)
    source = lax.broadcasted_iota(jnp.int32, (rows, rows), 1)
    return ((source == (at % patches) * per + at // patches) & (at % patches < limit)).astype(bf16)


class Loads:
    def __init__(self, sems):
        self.sems, self.count = sems, 0

    def __call__(self, src, dst):
        copy = pltpu.make_async_copy(src, dst, self.sems.at[self.count])
        self.count += 1
        copy.start()
        return copy


def own_lengths(r, m):
    return r.seq_lengths[m, 0], r.seq_lengths[m, 1], r.seq_lengths[m, 2]


def seg_starts(lengths, places):
    end0 = lengths[0]
    end1 = end0 + lengths[1]
    end2 = end1 + lengths[2]
    return jnp.where(
        places >= end2, end2, jnp.where(places >= end1, end1, jnp.where(places >= end0, end0, 0))
    )


def conv_taps(conv_in, pos, lag):
    moved = conv_in if lag == 0 else pltpu.roll(conv_in, lag, 0)
    return jnp.where(pos >= lag, moved, 0.0)


def mixer_state(lengths, projected, conv_weight, conv_bias, step_bias, log_decay):
    patches = projected.shape[0]
    places = lax.broadcasted_iota(jnp.int32, (patches, 1), 0)
    start = seg_starts(lengths, places)
    pos = places - start
    conv_in = projected[:, GROUP_WIDTH : GROUP_WIDTH + CONV_CH]
    conv_out = conv_bias
    for lag in range(CONV):
        conv_out = conv_out + conv_taps(conv_in, pos, lag) * conv_weight[CONV - 1 - lag][None]
    step_raw = projected[:, GROUP_WIDTH + CONV_CH :] + step_bias
    step = jnp.maximum(step_raw, 0.0) + jnp.log1p(jnp.exp(-jnp.abs(step_raw)))
    logd = -step * jnp.exp(log_decay)
    across = lax.broadcasted_iota(jnp.int32, (patches, patches), 1)
    down = lax.broadcasted_iota(jnp.int32, (patches, patches), 0)
    mask = (across >= start) & (across <= down)
    running = dot(mask.astype(f32), logd, precision=highest)
    return pos, conv_in, conv_out, step_raw, step, logd, mask, running


def head_decay(mask, running, running_t, h):
    return jnp.exp(
        jnp.where(mask, running[:, h : h + 1] - running_t[h : h + 1, :], large_negative)
    )


def att_mask(rows, patches):
    across = lax.broadcasted_iota(jnp.int32, (rows, rows), 1)
    down = lax.broadcasted_iota(jnp.int32, (rows, rows), 0)
    return (across % patches == down % patches) & (across <= down)


def soft_rows(mask, query, key):
    scores = dot(query, key, ((1,), (1,))) * ATT_DIM ** (-0.5)
    scores = jnp.where(mask, scores, large_negative)
    probs = jnp.exp(scores - jnp.max(scores, axis=1, keepdims=True))
    return probs / jnp.sum(probs, axis=1, keepdims=True)


def mixer_fwd(r, lengths, normed):
    projected = dot(normed, r.in_v[...], ((1,), (1,)))
    r.projected[...] = projected
    _, _, conv_out, _, step, _, mask, running = mixer_state(
        lengths, projected, r.taps[...], r.conv_bias[...], r.step_bias[...], r.log_decay[...]
    )
    act = conv_out * jax.nn.sigmoid(conv_out)
    inputs = act[:, GROUP_WIDTH : GROUP_WIDTH + STATE]
    outputs = act[:, GROUP_WIDTH + STATE :]
    inner = dot(outputs, inputs, ((1,), (1,)))
    running_t, step_t = running.T, step.T
    pair = 2 * HEAD_DIM
    lane = lax.broadcasted_iota(jnp.int32, (1, pair), 1)
    pieces = []
    for c in range(GROUP_WIDTH // pair):
        values = act[:, c * pair : (c + 1) * pair]
        got = []
        for h in (2 * c, 2 * c + 1):
            weights = head_decay(mask, running, running_t, h) * inner * step_t[h : h + 1, :]
            got.append(dot(weights, values))
        pieces.append(jnp.where(lane < HEAD_DIM, got[0], got[1]))
    y = jnp.concatenate(pieces, axis=1) + r.skip[...] * act[:, :GROUP_WIDTH]
    r.mixer_y[...] = y
    gate = projected[:, :GROUP_WIDTH]
    gated = y * (gate * jax.nn.sigmoid(gate))
    low = (gated * inv_rms(gated) * r.group_gain[...]).astype(bf16)
    r.mixer_low[...] = low
    return dot(low, r.out_v[...])


def forward_steps(p, r, load, land):
    n, mpn, i, j = p.n, p.mpn, p.i, p.j
    micro, patches, own_cols = r.own.shape
    positions, dim = r.pw.shape[0], r.pw.shape[1]
    slabs = r.bytes_v.shape[2] // dim
    rows = slabs * patches
    features = r.bytes_part.shape[-1]
    per, hidden = r.ffn_weight.shape[1:]

    load_own = load(r.byte_input.at[:, :, pl.ds(pl.multiple_of(j * own_cols, 128), own_cols)], r.own)
    load_pw = [load(r.patch_weight.at[k], r.pw.at[k]) for k in range(positions)]
    load_grad = load(r.out_grad.at[j], r.grad_raw)
    load_in = load(r.in_weight, r.in_v)
    load_out = load(r.out_weight, r.out_v)
    load_bytes = load(r.byte_input, r.bytes_v)
    load_qkv = load(r.qkv_weight, r.qkv_v)
    kept = [load(r.ffn_weight.at[w], land(j, w, slice(None), slice(None))) for w in range(3)]

    barrier = pltpu.get_barrier_semaphore()
    count = greet_all(p, barrier)
    load_own.wait()
    sums = None
    for k in range(positions):
        load_pw[k].wait()
        term = dot(r.own[:, :, k * dim : (k + 1) * dim].reshape(micro * patches, dim), r.pw[k])
        sums = term if sums is None else sums + term
    for t in range(micro):
        r.part[t] = sums[t * patches : (t + 1) * patches]
        r.part_low[t] = sums[t * patches : (t + 1) * patches].astype(bf16)
    load_grad.wait()
    perm = perm_matrix(rows, patches, slabs, sum(own_lengths(r, j)) - i * patches)
    r.own_grad[...] = dot(perm, r.grad_raw[...]).astype(bf16)
    r.grad_rows_own(i, r.own_grad[...])
    pl.semaphore_wait(barrier, count)

    embed = Exchange(p, lambda t: r.part_low.at[t], lambda s: r.recv.at[s], r.ss1, r.rs1).start()
    grads = PlaneGather(p, r.own_grad, lambda s: r.grad_rows.at[s], r.ssg, r.rsg, r.ssgr).start()
    halves = max(hidden // FFN_COLS, 1)
    cuts = WEIGHT_CUTS if per // WEIGHT_CUTS >= 16 else 1
    step = per // cuts
    pieces = []
    for hh in range(halves):
        cols = slice(hh * (hidden // halves), (hh + 1) * (hidden // halves))
        for w in range(3):
            for k in range(cuts):
                at = slice(k * step, (k + 1) * step)
                pieces.append(Exchange(
                    p,
                    lambda t, w=w, at=at, cols=cols: r.ffn_weight.at[w, at, cols],
                    lambda s, w=w, at=at, cols=cols: land(s, w, at, cols),
                    r.ssw.at[len(pieces)],
                    r.rsw.at[len(pieces)],
                ))
    bulk = Bulk(pieces)
    bulk.go(PACE[0])
    total = r.part[j]
    for d in range(1, mpn):
        total = total + r.recv[embed.wait(d)].astype(f32)
    r.global_in[...] = total
    r.low[...] = (total * inv_rms(total) * r.norm_in_gain[...]).astype(bf16)
    cast = Cast(p, r.low, r.normed, r.ss2, r.rs2)
    cast.start()
    def columns_of(t, k):
        first = k * dim + t * (dim // n) // features * features
        return r.own.at[:, :, pl.ds(pl.multiple_of(first, 128), features)]

    def bytes_copy(t, k):
        return rcopy(columns_of(t, k), r.bytes_part.at[i, k], r.ssb.at[t, k], r.rsb.at[i, k], t, j)

    for d in range(1, n):
        for k in range(positions):
            bytes_copy((i + d) % n, k).start()
    kept += [load(columns_of(i, k), r.bytes_part.at[i, k]) for k in range(positions)]
    piece = r.out_proj.shape[0] // n
    at_piece = lambda s: pl.ds(pl.multiple_of(s * piece, piece), piece)
    kept_ao = load(r.out_proj.at[at_piece(i)], r.ao_sorted.at[j, at_piece(i)])
    bulk.go(PACE[1])
    load_in.wait()
    load_out.wait()
    cast.wait()
    ao_line = Exchange(
        p, lambda t: r.out_proj.at[at_piece(i)], lambda s: r.ao_sorted.at[s, at_piece(i)], r.ssa, r.rsa
    ).start()
    bulk.go(PACE[2])

    part = mixer_fwd(r, own_lengths(r, p.m), r.normed[...].reshape(n * patches, dim))
    for b in range(n):
        r.mix_part[b] = part[b * patches : (b + 1) * patches].astype(bf16)
    to_owner = ToOwner(p, r.mix_part, r.mix_recv, r.ss3, r.rs3)
    to_owner.start()
    kept_ao.wait()
    ao_line.wait_all()
    ao_block = lambda s: r.ao_sorted.at[:, at_piece(s)]
    ao_plane = PlaneGather(p, ao_block(i), ao_block, r.ssap, r.rsap, r.ssar).start()
    total = r.global_in[...] + to_owner.total()
    r.global_own[...] = total
    r.patch_all[j] = total.astype(bf16)
    patch_line = Exchange(p, lambda t: r.patch_all.at[j], lambda s: r.patch_all.at[s], r.ss4, r.rs4).start()
    bulk.go(PACE[3])
    grads.relay()
    load_bytes.wait()
    load_qkv.wait()
    patch_line.wait_all()

    mask = att_mask(rows, patches)
    pair = 2 * ATT_DIM
    width = r.qkv_v.shape[2]
    lane = lax.broadcasted_iota(jnp.int32, (1, pair), 1)
    heads_line = Exchange(p, lambda t: r.heads.at[t], lambda s: r.heads_own.at[s], r.ss5, r.rs5)

    def one_micro(d, _):
        m = (j + d) % mpn
        for k in range(slabs):
            here = r.bytes_v[m, :, k * dim : (k + 1) * dim].astype(f32) + r.patch_all[m].astype(f32)
            r.attn_in[m, k * patches : (k + 1) * patches, :] = (
                here * inv_rms(here) * r.attn_gain[...]
            ).astype(bf16)
        got = r.attn_in[m]
        for w in range(3):
            r.qkv[w, m] = dot(got, r.qkv_v[w]).astype(bf16)
        for c in range(width // pair):
            at = slice(c * pair, (c + 1) * pair)
            query, key, value = r.qkv[0, m, :, at], r.qkv[1, m, :, at], r.qkv[2, m, :, at]
            res = []
            for own in (lane < ATT_DIM, lane >= ATT_DIM):
                probs = soft_rows(mask, jnp.where(own, query, jnp.zeros_like(query)), key)
                res.append(dot(probs.astype(bf16), value))
            r.heads[m, :, at] = jnp.where(lane < ATT_DIM, res[0], res[1]).astype(bf16)

        @pl.when(d < mpn)
        def _():
            heads_line.copy(m).start()

        return 0

    lax.fori_loop(1, mpn + 1, one_micro, 0)
    bulk.go(PACE[4])
    r.heads_own[j] = r.heads[j]
    ao_plane.relay()
    ao_plane.finish()
    for k in range(slabs):
        here = r.bytes_v[j, :, k * dim : (k + 1) * dim].astype(f32) + r.global_own[...]
        r.after[k * patches : (k + 1) * patches, :] = here
    branch = None
    for d in range(mpn):
        s = j if d == 0 else heads_line.wait(d)
        term = dot(r.heads_own[s], r.ao_sorted[s])
        branch = term if branch is None else branch + term
    after = r.after[...] + branch
    r.after[...] = after
    r.ffn_own[...] = (after * inv_rms(after) * r.ffn_gain[...]).astype(bf16)
    rows_gather = PlaneGather(p, r.ffn_own, lambda s: r.ffn_rows.at[s], r.ssf, r.rsf, r.ssfr).start()
    r.ffn_rows_own(i, r.ffn_own[...])
    bulk.go(PACE[5])

    def settle():
        for d in range(1, n):
            s = (i + d) % n
            for k in range(positions):
                rcopy(r.bytes_part.at[s, k], r.bytes_part.at[s, k], r.ssb.at[s, k], r.rsb.at[s, k], s, j).wait_recv()
        for thing in (embed, grads, bulk, cast, ao_line, to_owner, ao_plane, patch_line, heads_line, rows_gather):
            thing.sent()
        for d in range(1, n):
            for k in range(positions):
                bytes_copy((i + d) % n, k).wait_send()

    return SimpleNamespace(grads=grads, rows=rows_gather, bulk=bulk, halves=halves, kept=kept, settle=settle)


def forward_kernel(n, mpn, r):
    p = place_of(n, mpn)
    load = Loads(r.sem_load)
    kept = []
    r.grad_rows_own = lambda s, value: kept.append(load(r.own_grad, r.grad_rows.at[s]))
    r.ffn_rows_own = lambda s, value: kept.append(load(r.ffn_own, r.ffn_rows.at[s]))
    st = forward_steps(p, r, load, lambda s, w, rows, cols: r.w_all.at[s, w, rows, cols])
    st.grads.finish()
    st.rows.relay()
    st.rows.finish()
    st.bulk.go(len(st.bulk.exchanges))
    for exchange in st.bulk.exchanges:
        exchange.wait_all()
    st.settle()
    for copy in kept + st.kept:
        copy.wait()


def forward_ins(a):
    ins = dict(seq_lengths=(a.seq_lengths, SMEM))
    for name in ("byte_input", "patch_weight", "out_grad", "in_weight", "out_weight", "qkv_weight", "ffn_weight"):
        ins[name] = (getattr(a, name), ANY)
    ins["out_proj"] = (a.attn_out_weight, ANY)
    for name in SMALL_PARAMS:
        ins[name] = (getattr(a, name), VMEM)
    return ins


def forward_results(n, mpn, a):
    micro, patches, cols = a.byte_input.shape
    dim = a.norm_in_gain.shape[1]
    rows = patches * (cols // dim)
    positions = a.patch_weight.shape[0]
    width = a.qkv_weight.shape[2]
    seq = n * patches
    large = dict(
        grad_rows=((n, rows, dim), bf16),
        ffn_rows=((n, rows, dim), bf16),
        w_all=((mpn,) + a.ffn_weight.shape, bf16),
        bytes_part=((n, positions, micro, patches, max(dim // n, 128)), bf16),
    )
    small = dict(
        own_grad=((rows, dim), bf16),
        after=((rows, dim), f32),
        heads_own=((mpn, rows, width), bf16),
        qkv=((3, micro, rows, width), bf16),
        attn_in=((micro, rows, dim), bf16),
        ao_sorted=((mpn,) + a.attn_out_weight.shape, bf16),
        global_in=((patches, dim), f32),
        global_own=((patches, dim), f32),
        normed=((n, patches, dim), bf16),
        projected=((seq, a.in_weight.shape[0]), f32),
        mixer_y=((seq, GROUP_WIDTH), f32),
        mixer_low=((seq, GROUP_WIDTH), bf16),
    )
    return large, small


def forward_scratch(n, mpn, a):
    micro, patches, cols = a.byte_input.shape
    dim = a.norm_in_gain.shape[1]
    rows = patches * (cols // dim)
    positions = a.patch_weight.shape[0]
    width = a.qkv_weight.shape[2]
    half = n // 2
    pieces = max(a.ffn_weight.shape[2] // FFN_COLS, 1) * 3 * WEIGHT_CUTS
    line, plane = DMA((mpn,)), DMA((half,))
    return dict(
        own=pltpu.VMEM((micro, patches, positions * dim), bf16),
        pw=pltpu.VMEM(a.patch_weight.shape, bf16),
        grad_raw=pltpu.VMEM((rows, dim), bf16),
        in_v=pltpu.VMEM(a.in_weight.shape, bf16),
        out_v=pltpu.VMEM(a.out_weight.shape, bf16),
        bytes_v=pltpu.VMEM(a.byte_input.shape, bf16),
        qkv_v=pltpu.VMEM(a.qkv_weight.shape, bf16),
        part=pltpu.VMEM((micro, patches, dim), f32),
        part_low=pltpu.VMEM((micro, patches, dim), bf16),
        recv=pltpu.VMEM((mpn, patches, dim), bf16),
        low=pltpu.VMEM((patches, dim), bf16),
        mix_part=pltpu.VMEM((n, patches, dim), bf16),
        mix_recv=pltpu.VMEM((mpn, patches, dim), bf16),
        patch_all=pltpu.VMEM((mpn, patches, dim), bf16),
        heads=pltpu.VMEM((micro, rows, width), bf16),
        ffn_own=pltpu.VMEM((rows, dim), bf16),
        sem_load=DMA((24,)),
        ss1=line, rs1=line, ss2=DMA((n,)), rs2=DMA((n,)), ss3=line, rs3=line, ss4=line, rs4=line, ss5=line, rs5=line,
        ssg=plane, rsg=DMA((n,)), ssgr=plane, ssf=plane, rsf=DMA((n,)), ssfr=plane,
        ssb=DMA((n, positions)), rsb=DMA((n, positions)),
        ssa=line, rsa=line, ssap=plane, rsap=DMA((n,)), ssar=plane,
        ssw=DMA((pieces, mpn)), rsw=DMA((pieces, mpn)),
    )


def forward(n, mpn, a):
    large, small = forward_results(n, mpn, a)
    outs = {name: value + (ANY,) for name, value in large.items()}
    outs.update({name: value + (VMEM,) for name, value in small.items()})
    return launch(
        "forward", partial(forward_kernel, n, mpn), forward_ins(a), outs, forward_scratch(n, mpn, a),
        remote_params(0, 62),
    )


def ffn_kernel(rows_in, grads_in, parts, down_out, in_grad, weight_grad, weight, gate_low, up_low, hidden_low):
    blocks, rows, dim = rows_in.shape
    per = parts.shape[2]
    for s in range(parts.shape[0]):
        for w in range(3):
            weight[w, s * per : (s + 1) * per, :] = parts[s, w]

    def step(b, _):
        here, up = rows_in[b], grads_in[b]
        gate = dot(here, weight[0])
        other = dot(here, weight[1])
        act, slope = silu_pair(gate)
        hidden = (act * other).astype(bf16)
        hidden_low[b] = hidden
        down_out[b] = dot(hidden, weight[2], ((1,), (1,))).astype(bf16)
        hidden_grad = dot(up, weight[2])
        gate_grad = (hidden_grad * other * slope).astype(bf16)
        up_grad = (hidden_grad * act).astype(bf16)
        gate_low[b] = gate_grad
        up_low[b] = up_grad
        back = dot(gate_grad, weight[0], ((1,), (1,))) + dot(up_grad, weight[1], ((1,), (1,)))
        in_grad[b] = back.astype(bf16)
        return 0

    lax.fori_loop(0, blocks, step, 0)
    hidden = weight.shape[2]
    everything = rows_in[...].reshape(blocks * rows, dim)
    weight_grad[0] = dot(everything, gate_low[...].reshape(blocks * rows, hidden), ((0,), (0,))).astype(bf16)
    weight_grad[1] = dot(everything, up_low[...].reshape(blocks * rows, hidden), ((0,), (0,))).astype(bf16)
    weight_grad[2] = dot(
        grads_in[...].reshape(blocks * rows, dim), hidden_low[...].reshape(blocks * rows, hidden), ((0,), (0,))
    ).astype(bf16)


def ffn(rows_in, grads_in, parts):
    blocks, rows, dim = rows_in.shape
    hidden = parts.shape[3]
    return pl.pallas_call(
        ffn_kernel,
        out_shape=(
            jax.ShapeDtypeStruct((blocks, rows, dim), bf16),
            jax.ShapeDtypeStruct((blocks, rows, dim), bf16),
            jax.ShapeDtypeStruct((3, dim, hidden), bf16),
        ),
        in_specs=[VMEM] * 3,
        out_specs=(VMEM,) * 3,
        scratch_shapes=[pltpu.VMEM((3, dim, hidden), bf16)] + [pltpu.VMEM((blocks, rows, hidden), bf16)] * 3,
        compiler_params=plain_params(60),
        name="ffn",
    )(rows_in, grads_in, parts)


def mixer_bwd(r, p, lengths, upstream):
    projected = r.projected[...]
    patches = projected.shape[0]
    pos, conv_in, conv_out, step_raw, step, logd, mask, running = mixer_state(
        lengths, projected, r.taps[...], r.conv_bias[...], r.step_bias[...], r.log_decay[...]
    )
    act, act_slope = silu_pair(conv_out)
    inputs = act[:, GROUP_WIDTH : GROUP_WIDTH + STATE]
    outputs = act[:, GROUP_WIDTH + STATE :]
    inner = dot(outputs, inputs, ((1,), (1,)))
    running_t, step_t = running.T, step.T
    normed_grad = dot(upstream, r.out_v[...], ((1,), (1,)))
    y = r.mixer_y[...]
    gate = projected[:, :GROUP_WIDTH]
    gate_act, gate_slope = silu_pair(gate)
    gated_grad, gain_rows = rms_back(y * gate_act, r.group_gain[...], normed_grad)
    y_grad = gated_grad * gate_act
    gate_grad = gated_grad * y * gate_slope
    values = act[:, :GROUP_WIDTH]
    skip_cols = jnp.sum(y_grad * values, axis=0, keepdims=True)
    pair = 2 * HEAD_DIM
    lane = lax.broadcasted_iota(jnp.int32, (1, pair), 1)
    inner_grad = jnp.zeros_like(inner)
    value_pieces, row_sums, col_sums = [], [], []
    for c in range(GROUP_WIDTH // pair):
        at = slice(c * pair, (c + 1) * pair)
        got = []
        for h in (2 * c, 2 * c + 1):
            own = (lane < HEAD_DIM) if h % 2 == 0 else (lane >= HEAD_DIM)
            mine = jnp.where(own, y_grad[:, at], 0.0)
            decay = head_decay(mask, running, running_t, h)
            step_row = step_t[h : h + 1, :]
            weight_grad = dot(mine, values[:, at], ((1,), (1,))) * decay
            scaled = weight_grad * step_row
            inner_grad = inner_grad + scaled
            col_sums.append(jnp.sum(weight_grad * inner, axis=0, keepdims=True))
            row_sums.append(jnp.sum(scaled * inner, axis=1, keepdims=True))
            weights = decay * inner * step_row
            got.append(dot(weights, mine, ((0,), (0,))))
        value_pieces.append(got[0] + got[1])
    values_grad = jnp.concatenate(value_pieces, axis=1) + r.skip[...] * y_grad
    inputs_grad = dot(inner_grad, outputs, ((0,), (0,)))
    outputs_grad = dot(inner_grad, inputs)
    col_grad = jnp.concatenate(col_sums, axis=0).T
    running_grad = jnp.concatenate(row_sums, axis=1) - col_grad * step
    logd_grad = dot(mask.astype(f32), running_grad, ((0,), (0,)), precision=highest)
    step_grad = (col_grad - logd_grad * jnp.exp(r.log_decay[...])) * jax.nn.sigmoid(step_raw)
    conv_grad = jnp.concatenate([values_grad, inputs_grad, outputs_grad], axis=1) * act_slope
    conv_in_grad = jnp.zeros_like(conv_grad)
    small = r.small_part
    small[...] = jnp.zeros(small.shape, f32)
    for lag in range(CONV):
        small[CONV - 1 - lag : CONV - lag, :] = jnp.sum(
            conv_grad * conv_taps(conv_in, pos, lag), axis=0, keepdims=True
        )
        kept = jnp.where(pos >= lag, conv_grad, 0.0) * r.taps[CONV - 1 - lag : CONV - lag, :]
        conv_in_grad = conv_in_grad + (kept if lag == 0 else pltpu.roll(kept, patches - lag, 0))
    small[CONV : CONV + 1, :] = jnp.sum(conv_grad, axis=0, keepdims=True)
    small[CONV + 1 : CONV + 2, :GROUP_WIDTH] = jnp.sum(gain_rows, axis=0, keepdims=True)
    small[CONV + 2 : CONV + 3, :GROUP_WIDTH] = skip_cols
    small[CONV + 3 : CONV + 4, :GROUP_HEADS] = jnp.sum(step_grad, axis=0, keepdims=True)
    small[CONV + 4 : CONV + 5, :GROUP_HEADS] = jnp.sum(logd_grad * logd, axis=0, keepdims=True)
    return jnp.concatenate([gate_grad, conv_in_grad, step_grad], axis=1).astype(bf16)


def grad_pieces(p, r, halves, grad_of, dim, hidden):
    per = dim // p.mpn
    step = per // WEIGHT_CUTS
    pieces = []
    for hh in range(halves):
        cols = slice(hh * (hidden // halves), (hh + 1) * (hidden // halves))
        for w in range(3):
            for k in range(WEIGHT_CUTS):
                at = slice(k * step, (k + 1) * step)
                pieces.append(Exchange(
                    p,
                    lambda t, w=w, k=k, cols=cols: grad_of(
                        w, pl.ds(pl.multiple_of(t * per + k * step, step), step), cols
                    ),
                    lambda s, w=w, at=at, cols=cols: r.g_recv.at[s, w, at, cols],
                    r.bsw.at[len(pieces)],
                    r.brw.at[len(pieces)],
                ))
    return Bulk(pieces)


def ffn_sums(p, r, get, put):
    in_block = lambda s: r.in_part.at[s]
    down_block = lambda s: r.down_part.at[s]
    return (
        Reduction(p, in_block, lambda s: get(in_block(s)), r.in_pre, r.in_recv, r.bs_in, get, put),
        Reduction(p, down_block, lambda s: get(down_block(s)), r.down_pre, r.down_recv, r.bs_down, get, put),
    )


def backward_steps(p, r, load, own_slab, ready, sum_in, sum_down, bulk):
    n, mpn, i, j = p.n, p.mpn, p.i, p.j
    micro, rows, dim = r.attn_in.shape
    patches = r.global_own.shape[0]
    slabs = rows // patches
    width = r.qkv_v.shape[2]
    feature = dim // n
    at_feature = lambda s: pl.ds(pl.multiple_of(s * feature, feature), feature)
    block_ao = lambda s: r.ao_part.at[at_feature(s)]
    block_qkv = lambda s: r.qkv_part.at[:, at_feature(s)]
    sum_ao = Reduction(
        p, block_ao, lambda s: block_ao(s)[...], r.ao_pre, r.ao_recv, r.bs_ao, plain_get, plain_put
    )
    sum_qkv = Reduction(
        p, block_qkv, lambda s: block_qkv(s)[...], r.qkv_pre, r.qkv_recv, r.bs_qkv, plain_get, plain_put
    )

    ready("bytes")
    for k in range(slabs):
        r.local_in[k * patches : (k + 1) * patches, :] = own_slab(k).astype(f32) + r.global_own[...]
    after = r.after[...]
    back, gain_rows = rms_back(after, r.ffn_gain[...], sum_in.finish())
    after_grad = r.own_grad[...].astype(f32) + back
    r.after_grad[...] = after_grad
    r.gains[...] = jnp.zeros(r.gains.shape, f32)
    r.gains[2:3, :] = jnp.sum(gain_rows, axis=0, keepdims=True)
    r.branch[...] = after_grad.astype(bf16)
    up_line = Exchange(p, lambda t: r.up.at[t], lambda s: r.up_recv.at[s], r.bs1, r.br1)
    for d in range(1, mpn + 1):
        t = (j + d) % mpn
        r.up[t] = dot(r.branch[...], r.ao_sorted[t], ((1,), (1,))).astype(bf16)
        if d < mpn:
            up_line.copy(t).start()
    r.up_recv[j] = r.up[j]
    bulk.go(PACE_BACK[0])
    sum_down.spread()
    ready("qkv")

    mask = att_mask(rows, patches)
    pair = 2 * ATT_DIM
    lane = lax.broadcasted_iota(jnp.int32, (1, pair), 1)
    att_line = Exchange(p, lambda t: r.att_part.at[t], lambda s: r.att_recv.at[s], r.bs2, r.br2)

    def one_micro(d, _):
        m = (j + d) % mpn

        @pl.when(d > 0)
        def _():
            up_line.wait(d)

        for c in range(width // pair):
            at = slice(c * pair, (c + 1) * pair)
            query, key, value = r.qkv[0, m, :, at], r.qkv[1, m, :, at], r.qkv[2, m, :, at]
            up = r.up_recv[m, :, at]
            got = [[], [], []]
            for own in (lane < ATT_DIM, lane >= ATT_DIM):
                mine = jnp.where(own, query, jnp.zeros_like(query))
                probs = soft_rows(mask, mine, key)
                my_up = jnp.where(own, up, jnp.zeros_like(up))
                probs_grad = dot(my_up, value, ((1,), (1,)))
                inner = jnp.sum(probs * probs_grad, axis=1, keepdims=True)
                score_grad = (probs * (probs_grad - inner) * ATT_DIM ** (-0.5)).astype(bf16)
                got[0].append(dot(score_grad, key))
                got[1].append(dot(score_grad, mine, ((0,), (0,))))
                got[2].append(dot(probs.astype(bf16), my_up, ((0,), (0,))))
            r.qkv_low[0, m, :, at] = jnp.where(lane < ATT_DIM, got[0][0], got[0][1]).astype(bf16)
            r.qkv_low[1, m, :, at] = (got[1][0] + got[1][1]).astype(bf16)
            r.qkv_low[2, m, :, at] = (got[2][0] + got[2][1]).astype(bf16)
        total = dot(r.qkv_low[0, m], r.qkv_v[0], ((1,), (1,)))
        total = total + dot(r.qkv_low[1, m], r.qkv_v[1], ((1,), (1,)))
        total = total + dot(r.qkv_low[2, m], r.qkv_v[2], ((1,), (1,)))
        r.att_part[m] = total.astype(bf16)

        @pl.when(d > 0)
        def _():
            att_line.copy(m).start()

        return 0

    lax.fori_loop(0, mpn, one_micro, 0)

    everything = r.attn_in[...].reshape(micro * rows, dim)
    for w in range(3):
        r.qkv_part[w] = dot(
            everything, r.qkv_low[w].reshape(micro * rows, width), ((0,), (0,))
        ).astype(bf16)
    sum_qkv.start()
    for t in range(mpn):
        r.ao_part[:, t * width : (t + 1) * width] = dot(
            r.branch[...], r.heads_own[t], ((0,), (0,))
        ).astype(bf16)
    sum_ao.start()
    sum_qkv.spread()
    perm = perm_matrix(rows, patches, slabs, sum(own_lengths(r, j)) - i * patches)
    block = (r.after[...] + sum_down.finish()).astype(bf16)
    block = dot(perm, block, ((0,), (0,))).astype(bf16)
    for t in range(mpn):
        r.block[t] = block[:, t * width : (t + 1) * width]
    total = r.att_part[j].astype(f32)
    for d in range(1, mpn):
        total = total + r.att_recv[att_line.wait(d)].astype(f32)
    back, gain_rows = rms_back(r.local_in[...], r.attn_gain[...], total)
    local_grad = r.after_grad[...] + back
    global_grad = local_grad[:patches]
    for k in range(1, slabs):
        global_grad = global_grad + local_grad[k * patches : (k + 1) * patches]
    r.global_grad[...] = global_grad
    r.b_low[...] = global_grad.astype(bf16)
    cast = Cast(p, r.b_low, r.mixer, r.bs3, r.br3)
    cast.start()
    bulk.go(PACE_BACK[1])
    r.gains[1:2, :] = jnp.sum(gain_rows, axis=0, keepdims=True)
    share_rows = rows // mpn
    for t in range(mpn):
        r.local[t] = local_grad[t * share_rows : (t + 1) * share_rows].astype(bf16)
    local_line = Exchange(p, lambda t: r.local.at[t], lambda s: r.local_all.at[s], r.bs6, r.br6)
    block_line = Exchange(p, lambda t: r.block.at[t], lambda s: r.block_all.at[s], r.bs7, r.br7)
    ready("mixer")
    cast.wait()
    sum_ao.spread()
    bulk.go(PACE_BACK[2])

    upstream = r.mixer[...].reshape(n * patches, dim)
    proj_grad = mixer_bwd(r, p, own_lengths(r, p.m), upstream)
    part = dot(proj_grad, r.in_v[...])
    for b in range(n):
        r.b_part[b] = part[b * patches : (b + 1) * patches].astype(bf16)
    to_owner = ToOwner(p, r.b_part, r.b_recv, r.bs4, r.br4)
    to_owner.start()
    bulk.go(PACE_BACK[3])

    half_cols = dim // p.reps
    normed_half = r.normed[:, :, pl.ds(pl.multiple_of(p.h * half_cols, half_cols), half_cols)]
    in_grad = dot(proj_grad, normed_half.reshape(n * patches, half_cols), ((0,), (0,))).astype(bf16)
    columns = in_grad.shape[0]
    for e in range(p.share):
        r.in_w_part[e, :columns, :] = in_grad[:, e * feature : (e + 1) * feature]
        r.in_w_part[e, columns:, :] = jnp.zeros((r.in_w_part.shape[1] - columns, feature), bf16)
    out_grad = dot(r.mixer_low[...], upstream, ((0,), (0,))).astype(bf16)
    group_rows = GROUP_WIDTH // n
    for e in range(n):
        r.out_w_part[e] = out_grad[e * group_rows : (e + 1) * group_rows]
    bundles = (
        (lambda e: r.in_w_part.at[e], r.in_w_recv, r.bsi, r.bri),
        (lambda e: r.out_w_part.at[p.h * p.share + e], r.out_w_recv, r.bso, r.bro),
        (lambda e: r.small_part, r.small_recv, r.bss, r.brs),
    )

    def each_bundle(act):
        for e in range(p.share):
            @pl.when(p.h * p.share + e != i)
            def _():
                for src, dst, ss, rs in bundles:
                    act(rcopy(src(e), dst.at[p.m], ss.at[e], rs.at[p.m], p.h * p.share + e, j))

    def start_bundles():
        each_bundle(lambda copy: copy.start())
        for e in range(p.share):
            @pl.when(p.h * p.share + e == i)
            def _():
                r.in_w_recv[p.m] = r.in_w_part[e]
                r.out_w_recv[p.m] = r.out_w_part[i]
                r.small_recv[p.m] = r.small_part[...]

    if BUNDLES_FIRST:
        start_bundles()
    back, gain_rows = rms_back(r.global_in[...], r.norm_in_gain[...], to_owner.total())
    r.line[j] = (r.global_grad[...] + back).astype(bf16)
    line = Exchange(p, lambda t: r.line.at[j], lambda s: r.line.at[s], r.bs5, r.br5).start()
    r.gains[0:1, :] = jnp.sum(gain_rows, axis=0, keepdims=True)
    r.gains_line[j] = r.gains[...]
    gains_line = Exchange(p, lambda t: r.gains, lambda s: r.gains_line.at[s], r.bsg, r.brg).start()
    local_line.start()
    block_line.start()
    r.local_all[j] = r.local[j]
    r.block_all[j] = r.block[j]
    line.wait_all()
    slot = lambda s: r.plane.at[s]
    plane = PlaneGather(p, r.line, slot, r.bsp, r.brp, r.bspr).start()
    keep_line = load(r.line, r.plane.at[i])
    if not BUNDLES_FIRST:
        start_bundles()
    r.qkv_sum[...] = sum_qkv.finish()
    ao = sum_ao.finish().astype(bf16)
    for t in range(mpn):
        r.ao[t] = ao[:, t * width : (t + 1) * width]
    ao_line = Exchange(p, lambda t: r.ao.at[t], lambda s: r.ao_all.at[s], r.bs8, r.br8).start()
    r.ao_all[j] = r.ao[j]
    bulk.go(len(bulk.exchanges))
    gains_line.wait_all()
    r.gains_plane[p.mine] = sum(r.gains_line[s] for s in range(mpn))

    def gains_copy(q):
        return rcopy(
            r.gains_plane.at[p.mine], r.gains_plane.at[p.mine], r.bsh.at[q], r.brh.at[p.mine], q * 2 + p.c, j
        )

    others = [(p.mine + d) % p.half for d in range(1, p.half)]
    for q in others:
        gains_copy(q).start()
    plane.relay()
    for q in others:
        rcopy(r.gains_plane.at[q], r.gains_plane.at[q], r.bsh.at[q], r.brh.at[q], q * 2 + p.c, j).wait_recv()
    r.gains_pair[0] = sum(r.gains_plane[s] for s in range(p.half))
    pair_copy = rcopy(r.gains_pair.at[0], r.gains_pair.at[1], r.bsq.at[0], r.brq.at[0], p.other, j)
    pair_copy.start()
    plane.finish()
    local_line.wait_all()
    block_line.wait_all()
    ao_line.wait_all()
    group = i // p.share
    for t in range(mpn):
        @pl.when(t * p.reps + group != i)
        def _():
            for src, dst, ss, rs in bundles:
                rcopy(src(0), dst.at[t], ss.at[0], rs.at[t], t * p.reps + group, j).wait_recv()
    pair_copy.wait()
    r.gains_all[...] = r.gains_pair[0] + r.gains_pair[1]
    for exchange in bulk.exchanges:
        exchange.wait_all()
    keep_line.wait()
    for thing in (
        sum_in, sum_down, sum_ao, sum_qkv, bulk, up_line, att_line, cast, to_owner, line, gains_line, local_line,
        block_line, plane, ao_line,
    ):
        thing.sent()
    for q in others:
        gains_copy(q).wait_send()
    each_bundle(lambda copy: copy.wait_send())


def backward_kernel(n, mpn, spill, r):
    p = place_of(n, mpn)
    load = Loads(r.b_load)

    def read(view):
        if not spill:
            return view[...]
        copy = pltpu.make_async_copy(view, r.stage.at[0], r.sem_stage.at[0])
        copy.start()
        copy.wait()
        return r.stage[0]

    def write(view, value):
        if not spill:
            view[...] = value
            return
        r.stage[1] = value
        copy = pltpu.make_async_copy(r.stage.at[1], view, r.sem_stage.at[1])
        copy.start()
        copy.wait()

    per = r.w_grad.shape[1] // mpn
    keep_w = load(r.w_grad.at[:, pl.ds(pl.multiple_of(p.j * per, per), per)], r.g_recv.at[p.j])
    loads = dict(
        bytes=[load(r.byte_input.at[p.j], r.own_bytes)],
        qkv=[load(r.qkv_weight, r.qkv_v)],
        mixer=[load(r.out_weight, r.out_v), load(r.in_weight, r.in_v)],
    )

    def ready(what):
        for copy in loads[what]:
            copy.wait()

    barrier = pltpu.get_barrier_semaphore()
    pl.semaphore_wait(barrier, greet_all(p, barrier))
    bulk = grad_pieces(p, r, 1, lambda w, at, cols: r.w_grad.at[w, at, cols], *r.w_grad.shape[1:])
    sum_in, sum_down = ffn_sums(p, r, read, write)
    sum_in.start()
    sum_in.spread()
    sum_down.start()
    dim = r.after.shape[1]
    own_slab = lambda k: r.own_bytes[:, k * dim : (k + 1) * dim]
    backward_steps(p, r, load, own_slab, ready, sum_in, sum_down, bulk)
    keep_w.wait()


def backward_results(n, mpn, a):
    micro, patches, cols = a.byte_input.shape
    dim = a.norm_in_gain.shape[1]
    rows = patches * (cols // dim)
    width = a.qkv_weight.shape[2]
    hidden = a.ffn_weight.shape[2]
    feature = dim // n
    padded = (a.in_weight.shape[0] + 15) // 16 * 16
    return dict(
        g_recv=((mpn, 3, dim // mpn, hidden), bf16, ANY),
        plane=((n, mpn, patches, dim), bf16, ANY),
        qkv_sum=((3, feature, width), f32, VMEM),
        ao_all=((mpn, feature, width), bf16, VMEM),
        in_w_recv=((mpn, padded, feature), bf16, VMEM),
        out_w_recv=((mpn, GROUP_WIDTH // n, dim), bf16, VMEM),
        small_recv=((mpn, 16, CONV_CH), f32, VMEM),
        gains_all=((8, dim), f32, VMEM),
        local_all=((mpn, rows // mpn, dim), bf16, VMEM),
        block_all=((mpn, rows, width), bf16, VMEM),
    )


def backward_scratch(n, mpn, a):
    micro, patches, cols = a.byte_input.shape
    dim = a.norm_in_gain.shape[1]
    rows = patches * (cols // dim)
    width = a.qkv_weight.shape[2]
    hidden = a.ffn_weight.shape[2]
    half, share = n // 2, mpn
    feature = dim // n
    padded = (a.in_weight.shape[0] + 15) // 16 * 16
    pieces = max(hidden // FFN_COLS, 1) * 3 * WEIGHT_CUTS
    line, plane = DMA((mpn,)), DMA((half,))
    return dict(
        local_in=pltpu.VMEM((rows, dim), f32),
        after_grad=pltpu.VMEM((rows, dim), f32),
        branch=pltpu.VMEM((rows, dim), bf16),
        up=pltpu.VMEM((mpn, rows, width), bf16),
        up_recv=pltpu.VMEM((mpn, rows, width), bf16),
        qkv_low=pltpu.VMEM((3, micro, rows, width), bf16),
        att_part=pltpu.VMEM((micro, rows, dim), bf16),
        att_recv=pltpu.VMEM((mpn, rows, dim), bf16),
        qkv_part=pltpu.VMEM((3, dim, width), bf16),
        qkv_pre=pltpu.VMEM((half, 3, feature, width), bf16),
        qkv_recv=pltpu.VMEM((half, 3, feature, width), bf16),
        ao_part=pltpu.VMEM((dim, mpn * width), bf16),
        ao_pre=pltpu.VMEM((half, feature, mpn * width), bf16),
        ao_recv=pltpu.VMEM((half, feature, mpn * width), bf16),
        ao=pltpu.VMEM((mpn, feature, width), bf16),
        block=pltpu.VMEM((mpn, rows, width), bf16),
        local=pltpu.VMEM((mpn, rows // mpn, dim), bf16),
        b_low=pltpu.VMEM((patches, dim), bf16),
        global_grad=pltpu.VMEM((patches, dim), f32),
        mixer=pltpu.VMEM((n, patches, dim), bf16),
        b_part=pltpu.VMEM((n, patches, dim), bf16),
        b_recv=pltpu.VMEM((mpn, patches, dim), bf16),
        line=pltpu.VMEM((mpn, patches, dim), bf16),
        in_w_part=pltpu.VMEM((share, padded, feature), bf16),
        out_w_part=pltpu.VMEM((n, GROUP_WIDTH // n, dim), bf16),
        small_part=pltpu.VMEM((16, CONV_CH), f32),
        gains=pltpu.VMEM((8, dim), f32),
        gains_line=pltpu.VMEM((mpn, 8, dim), f32),
        gains_plane=pltpu.VMEM((half, 8, dim), f32),
        gains_pair=pltpu.VMEM((2, 8, dim), f32),
        b_load=DMA((16,)),
        bs_in=DMA((4, half)), bs_down=DMA((4, half)), bs_ao=DMA((4, half)), bs_qkv=DMA((4, half)),
        bs1=line, br1=line, bs2=line, br2=line, bs3=DMA((n,)), br3=DMA((n,)), bs4=line, br4=line,
        bs5=line, br5=line, bs6=line, br6=line, bs7=line, br7=line, bs8=line, br8=line,
        bsp=plane, brp=DMA((n,)), bspr=plane,
        bsg=line, brg=line, bsh=plane, brh=plane, bsq=DMA((1,)), brq=DMA((1,)),
        bsi=DMA((share,)), bri=line, bso=DMA((share,)), bro=line, bss=DMA((share,)), brs=line,
        bsw=DMA((pieces, mpn)), brw=DMA((pieces, mpn)),
    )


def sum_buffers(n, a, make):
    micro, patches, cols = a.byte_input.shape
    dim = a.norm_in_gain.shape[1]
    shape = (n // 2, patches * (cols // dim), dim)
    return {name: make(shape) for name in ("in_pre", "in_recv", "down_pre", "down_recv")}


def backward(n, mpn, a):
    spill = a.in_part.size * 2 > SPILL_BYTES
    ins = dict(seq_lengths=(a.seq_lengths, SMEM))
    for name in ("byte_input", "w_grad", "in_weight", "out_weight", "qkv_weight"):
        ins[name] = (getattr(a, name), ANY)
    for name in ("in_part", "down_part"):
        ins[name] = (getattr(a, name), ANY if spill else VMEM)
    for name in SMALL_PARAMS + (
        "after", "own_grad", "heads_own", "qkv", "attn_in", "ao_sorted", "global_in", "global_own", "normed",
        "projected", "mixer_y", "mixer_low",
    ):
        ins[name] = (getattr(a, name), VMEM)
    outs = backward_results(n, mpn, a)
    scratch = backward_scratch(n, mpn, a)
    scratch.update(
        own_bytes=pltpu.VMEM(a.byte_input.shape[1:], bf16),
        in_v=pltpu.VMEM(a.in_weight.shape, bf16),
        out_v=pltpu.VMEM(a.out_weight.shape, bf16),
        qkv_v=pltpu.VMEM(a.qkv_weight.shape, bf16),
    )
    if spill:
        outs.update(sum_buffers(n, a, lambda shape: (shape, bf16, ANY)))
        scratch.update(stage=pltpu.VMEM((2,) + a.in_part.shape[1:], bf16), sem_stage=DMA((2,)))
    else:
        scratch.update(sum_buffers(n, a, lambda shape: pltpu.VMEM(shape, bf16)))
    return launch(
        "backward", partial(backward_kernel, n, mpn, spill), ins, outs, scratch, remote_params(1, 63)
    )


def ffn_steps(p, r, st, load, sum_in, sum_down, bulk, grad_of):
    n, half = p.n, p.half
    rows, dim = r.own_grad.shape
    hidden = r.w_v.shape[2]
    cols = hidden // st.halves
    per = dim // p.mpn
    pair = 2 * rows
    st.grads.finish()
    grads_all = lambda: r.grad_rows[...].reshape(n * rows, dim)
    rows_all = lambda: r.ffn_rows[...].reshape(n * rows, dim)
    kept = []
    if st.halves == 1:
        st.rows.relay()
        st.rows.finish()
    count = len(st.bulk.exchanges) // st.halves
    for hh in range(st.halves):
        at = slice(hh * cols, (hh + 1) * cols)
        last = hh == st.halves - 1
        if last:
            st.bulk.go(len(st.bulk.exchanges))
        for exchange in st.bulk.exchanges[hh * count : (hh + 1) * count]:
            exchange.wait_all()
        if hh == 0:
            for copy in st.kept:
                copy.wait()

        def compute(q):
            here = r.ffn_rows[pl.ds(2 * q, 2)].reshape(pair, dim)
            up = r.grad_rows[pl.ds(2 * q, 2)].reshape(pair, dim)
            gate = dot(here, r.w_v[0, :, at])
            other = dot(here, r.w_v[1, :, at])
            act, slope = silu_pair(gate)
            hidden_low = (act * other).astype(bf16)
            here_at = pl.ds(pl.multiple_of(q * pair, pair), pair)
            r.hidden_low[hh, here_at, :] = hidden_low
            down = dot(hidden_low, r.w_v[2, :, at], ((1,), (1,)))
            hidden_grad = dot(up, r.w_v[2, :, at])
            gate_grad = (hidden_grad * other * slope).astype(bf16)
            up_grad = (hidden_grad * act).astype(bf16)
            r.gate_low[hh, here_at, :] = gate_grad
            r.up_low[hh, here_at, :] = up_grad
            back = dot(gate_grad, r.w_v[0, :, at], ((1,), (1,))) + dot(up_grad, r.w_v[1, :, at], ((1,), (1,)))
            if hh > 0:
                back = back + r.in_part[pl.ds(2 * q, 2)].reshape(pair, dim).astype(f32)
                down = down + r.down_part[pl.ds(2 * q, 2)].reshape(pair, dim).astype(f32)
            r.in_part[pl.ds(2 * q, 2)] = back.astype(bf16).reshape(2, rows, dim)
            r.down_part[pl.ds(2 * q, 2)] = down.astype(bf16).reshape(2, rows, dim)

        def first_pass(d, _):
            q = (p.mine + half - d) % half

            @pl.when(d > 0)
            def _():
                st.rows.relay_one(q)

            st.rows.wait_across(q)
            compute(q)
            return 0

        def last_pass(d, _):
            q = (p.mine + d) % half
            compute(q)
            sum_in.first(q).start()

            @pl.when(d > 1)
            def _():
                sum_in.spread_one((p.mine + d - 1) % half)

            return 0

        if last:
            lax.fori_loop(1, half + 1, last_pass, 0)
            sum_down.start()
        else:
            lax.fori_loop(0, half, first_pass, 0)
        everything = slice(0, dim)
        grad_of(0, everything, at)[...] = dot(rows_all(), r.gate_low[hh], ((0,), (0,))).astype(bf16)
        grad_of(1, everything, at)[...] = dot(rows_all(), r.up_low[hh], ((0,), (0,))).astype(bf16)
        grad_of(2, everything, at)[...] = dot(grads_all(), r.hidden_low[hh], ((0,), (0,))).astype(bf16)
        mine = pl.ds(pl.multiple_of(p.j * per, per), per)
        kept += [load(grad_of(w, mine, at), r.g_recv.at[p.j, w, :, at]) for w in range(3)]
        if not last:
            bulk.go(PACE_FFN)
    return kept


def layer_kernel(n, mpn, r):
    p = place_of(n, mpn)
    dim = r.after.shape[1]

    def put_rows(ref):
        def put(s, value):
            ref[s] = value

        return put

    r.grad_rows_own = put_rows(r.grad_rows)
    r.ffn_rows_own = put_rows(r.ffn_rows)
    per = r.ffn_weight.shape[1]

    def land(s, w, rows, cols):
        first = (0 if rows.start is None else rows.start) + s * per
        size = per if rows.start is None else rows.stop - rows.start
        return r.w_v.at[w, pl.ds(pl.multiple_of(first, size), size), cols]

    load = Loads(r.sem_load)
    st = forward_steps(p, r, load, land)
    hidden = r.w_v.shape[2]

    def grad_of(w, at, cols):
        first = w % 2 * hidden
        return r.pw.at[w // 2, at, first + cols.start : first + cols.stop]

    bulk = grad_pieces(p, r, st.halves, grad_of, dim, hidden)
    sum_in, sum_down = ffn_sums(p, r, plain_get, plain_put)
    load = Loads(r.b_load)
    kept = ffn_steps(p, r, st, load, sum_in, sum_down, bulk, grad_of)
    own_slab = lambda k: r.bytes_v[p.j, :, k * dim : (k + 1) * dim]
    backward_steps(p, r, load, own_slab, lambda what: None, sum_in, sum_down, bulk)
    st.settle()
    for copy in kept:
        copy.wait()


def layer(n, mpn, a):
    dim = a.norm_in_gain.shape[1]
    hidden = a.ffn_weight.shape[2]
    halves = max(hidden // FFN_COLS, 1)
    large, small = forward_results(n, mpn, a)
    rows = small["own_grad"][0][0]
    outs = dict(bytes_part=large.pop("bytes_part") + (ANY,))
    outs.update(backward_results(n, mpn, a))
    large.pop("w_all")
    scratch = forward_scratch(n, mpn, a)
    scratch.update(backward_scratch(n, mpn, a))
    for name, (shape, dtype) in (*large.items(), *small.items()):
        scratch[name] = pltpu.VMEM(shape, dtype)
    scratch.update(sum_buffers(n, a, lambda shape: pltpu.VMEM(shape, bf16)))
    scratch.update(
        w_v=pltpu.VMEM((3, dim, hidden), bf16),
        in_part=pltpu.VMEM((n, rows, dim), bf16),
        down_part=pltpu.VMEM((n, rows, dim), bf16),
        gate_low=pltpu.VMEM((halves, n * rows, hidden // halves), bf16),
        up_low=pltpu.VMEM((halves, n * rows, hidden // halves), bf16),
        hidden_low=pltpu.VMEM((halves, n * rows, hidden // halves), bf16),
    )
    return launch(
        "layer", partial(layer_kernel, n, mpn), forward_ins(a), outs, scratch, remote_params(2, 63)
    )


def finish_kernel(r):
    i = lax.axis_index("dp")
    mpn, patches, dim = r.plane.shape[1:]
    n = r.plane.shape[0]
    features = r.bytes_part.shape[-1]
    positions = r.patch_weight.shape[0]
    feature = dim // n
    everyone = r.plane[...].reshape(n * mpn * patches, dim)
    own = r.plane[i].reshape(mpn * patches, dim)
    for k in range(positions):
        mine = r.bytes_part[:, k].reshape(n * mpn * patches, features)
        got = dot(mine, everyone, ((0,), (0,)))
        if features != feature:
            cut = features // feature
            got = sum(
                jnp.where(i % cut == e, got[e * feature : (e + 1) * feature], 0.0) for e in range(cut)
            )
        r.patch_grad[k] = got
        piece = dot(own, r.patch_weight[k], ((1,), (1,)))
        for m in range(mpn):
            r.input_grad[m, :, k * dim : (k + 1) * dim] = (
                piece[m * patches : (m + 1) * patches]
                + r.local_all[m, k * patches : (k + 1) * patches, :].astype(f32)
            )
    for w in range(3):
        r.ffn_grad[w] = sum(r.g_recv[s, w].astype(f32) for s in range(mpn))
    r.ao_grad[...] = sum(r.ao_all[s].astype(f32) for s in range(mpn)).T
    columns = r.in_grad.shape[0]
    r.in_grad[...] = sum(r.in_w_recv[s, :columns, :].astype(f32) for s in range(mpn))
    r.out_grad[...] = sum(r.out_w_recv[s].astype(f32) for s in range(mpn))
    small = sum(r.small_recv[s] for s in range(mpn))

    def chosen(values, size):
        whole = values.shape[1]
        at = lax.broadcasted_iota(jnp.int32, (whole, size), 0)
        want = lax.broadcasted_iota(jnp.int32, (whole, size), 1) + i * size
        return dot(values, (at == want).astype(f32), precision=highest)

    conv = chosen(small, CONV_CH // n)
    r.conv_w_grad[...] = conv[:CONV]
    r.conv_b_grad[...] = conv[CONV : CONV + 1]
    group = chosen(small[:, :GROUP_WIDTH], GROUP_WIDTH // n)
    r.group_grad[...] = group[CONV + 1 : CONV + 2]
    heads = lax.broadcasted_iota(jnp.int32, (GROUP_WIDTH, GROUP_HEADS), 0) // HEAD_DIM
    pick = heads == lax.broadcasted_iota(jnp.int32, (GROUP_WIDTH, GROUP_HEADS), 1)
    skip = dot(small[:, :GROUP_WIDTH], pick.astype(f32), precision=highest)
    r.skip_grad[...] = skip[CONV + 2 : CONV + 3]
    r.step_grad[...] = small[CONV + 3 : CONV + 4, :GROUP_HEADS]
    r.decay_grad[...] = small[CONV + 4 : CONV + 5, :GROUP_HEADS]
    gains = chosen(r.gains_all[...], feature)
    r.norm_in_grad[...] = gains[0:1]
    r.attn_gain_grad[...] = gains[1:2]
    r.ffn_gain_grad[...] = gains[2:3]
    r.qkv_grad[...] = r.qkv_sum[...]
    r.block_out[...] = r.block_all[...]


def finish(a):
    n, mpn, patches, dim = a.plane.shape
    positions = a.patch_weight.shape[0]
    feature = dim // n
    columns = a.in_weight.shape[0]
    names = (
        "plane", "bytes_part", "patch_weight", "local_all", "g_recv", "ao_all", "in_w_recv", "out_w_recv",
        "small_recv", "gains_all", "qkv_sum", "block_all",
    )
    row = lambda size: ((1, size), f32, VMEM)
    outs = dict(
        patch_grad=((positions, feature, dim), f32, VMEM),
        input_grad=((mpn, patches, positions * dim), f32, VMEM),
        ffn_grad=(a.g_recv.shape[1:], f32, VMEM),
        ao_grad=(a.ao_all.shape[:0:-1], f32, VMEM),
        in_grad=((columns, feature), f32, VMEM),
        out_grad=(a.out_w_recv.shape[1:], f32, VMEM),
        conv_w_grad=((CONV, CONV_CH // n), f32, VMEM),
        conv_b_grad=row(CONV_CH // n),
        group_grad=row(GROUP_WIDTH // n),
        skip_grad=row(GROUP_HEADS),
        step_grad=row(GROUP_HEADS),
        decay_grad=row(GROUP_HEADS),
        norm_in_grad=row(feature),
        attn_gain_grad=row(feature),
        ffn_gain_grad=row(feature),
        qkv_grad=(a.qkv_sum.shape, f32, VMEM),
        block_out=(a.block_all.shape, bf16, VMEM),
    )
    ins = {name: (getattr(a, name), VMEM) for name in names}
    return launch("finish", finish_kernel, ins, outs, {}, plain_params())


def body(
    byte_input,
    seq_lengths,
    patch_weight,
    norm_in_gain,
    in_weight,
    conv_weight,
    conv_bias,
    step_bias,
    log_decay,
    skip_gain,
    group_gain,
    out_weight,
    attn_gain,
    qkv_weight,
    attn_out_weight,
    ffn_gain,
    ffn_weight,
    out_grad,
):
    n, mpn = lax.axis_size("dp"), lax.axis_size("mp")
    row = lambda v: v.reshape(1, -1)
    a = SimpleNamespace(
        byte_input=byte_input,
        seq_lengths=seq_lengths,
        patch_weight=patch_weight,
        norm_in_gain=row(norm_in_gain),
        in_weight=in_weight[0].T,
        taps=conv_weight[0].T,
        conv_bias=conv_bias,
        step_bias=step_bias,
        log_decay=log_decay,
        skip=row(jnp.repeat(skip_gain[0], HEAD_DIM)),
        group_gain=group_gain,
        out_weight=out_weight[0],
        attn_gain=row(attn_gain),
        qkv_weight=qkv_weight,
        attn_out_weight=attn_out_weight,
        ffn_gain=row(ffn_gain),
        ffn_weight=ffn_weight,
        out_grad=out_grad,
    )
    dim, hidden = ffn_gain.shape[0], ffn_weight.shape[2]
    if n * out_grad.shape[1] * dim * 2 <= SPILL_BYTES and 2 * hidden <= dim:
        a.__dict__.update(layer(n, mpn, a).__dict__)
    else:
        a.__dict__.update(forward(n, mpn, a).__dict__)
        a.down_part, a.in_part, a.w_grad = ffn(a.ffn_rows, a.grad_rows, a.w_all)
        a.__dict__.update(backward(n, mpn, a).__dict__)
    f = finish(a)
    return (
        f.block_out,
        f.input_grad,
        f.patch_grad,
        f.norm_in_grad[0],
        f.in_grad.T[None],
        f.conv_w_grad.T[None],
        f.conv_b_grad,
        f.step_grad,
        f.decay_grad,
        f.skip_grad,
        f.group_grad,
        f.out_grad[None],
        f.attn_gain_grad[0],
        f.qkv_grad,
        f.ao_grad,
        f.ffn_gain_grad[0],
        f.ffn_grad,
    )


def solution(mesh):
    in_specs = (
        P(None, "dp", None),
        P(),
        P("mp", None, None),
        P(),
        P("mp", None, None),
        P("mp", None, None),
        P("mp", None),
        P("mp", None),
        P("mp", None),
        P("mp", None),
        P("mp", None),
        P("mp", None, None),
        P(),
        P(None, None, "mp"),
        P("mp", None),
        P(),
        P(None, "mp", "dp"),
        P(None, "dp", None),
    )
    out_specs = (
        P(None, "dp", "mp"),
        P(None, "dp", "mp"),
        P("mp", "dp", None),
        P("dp"),
        P("mp", "dp", None),
        P("mp", "dp", None),
        P("mp", "dp"),
        P("mp", None),
        P("mp", None),
        P("mp", None),
        P("mp", "dp"),
        P("mp", "dp", None),
        P("dp"),
        P(None, "dp", "mp"),
        P("mp", "dp"),
        P("dp"),
        P(None, "mp", "dp"),
    )
    return jax.shard_map(body, mesh=mesh, in_specs=in_specs, out_specs=out_specs, check_vma=False)
```

time: 324 us -> 271 us (0.84)
  Pallas kernels: 318 us -> 264 us
    pallas_call x3 -> x2, Pallas kernels: 296 us -> 264 us  [launch(): pl.pallas_call(run, out_shape=tuple((jax.ShapeDtypeStruct(shape, dtype) f...]
    pallas_call x1 -> x0, Pallas kernels: 22.4 us -> none  [ffn(): pl.pallas_call(ffn_kernel, out_shape=(jax.ShapeDtypeStruct((blocks, rows,...]
where the time goes in v3:
time: 271 us; the launch traced here: 266 us
  Pallas kernels  264 us (97%)
    pallas_call x2, Pallas kernels, launch(): pl.pallas_call(run, out_shape=tuple((jax.ShapeDtypeStruct(shape, dtype) f...  264 us

profile of v3, /device:TPU:2, one launch (start us, length us, event | category | flops | bytes accessed | tf_op | source)
XLA Modules:
  0.0 266.2 jit_solution(130047585097407074)
XLA Ops:
  0.7 0.7 broadcast_in_dim.12
  1.4 0.7 reshape_reshape.3.refs_14_
  2.0 255.1 %layer.1 = (bf16[8,2,4,16,128]{4,3,2,1,0:T(8,128)(2,1)}, bf16[4,3,256,512]{3,2,1,0:T(8,128)(2,1)}, bf16[8,4,16,1024]{3,2,1,0:T(8,128)(2,1)}, f32[3,128,256]{2,1,...) custom-call(s32[4,3]{1,0:T(4,128)} %refs_0_.1, ...), custom_call_target="tpu_custom_call" | custom-call | tf_op jit(solution)/shard_map/layer/pallas_call | solution.py:96
  257.1 8.8 %finish.1 = (f32[2,128,1024]{2,1,0:T(8,128)}, f32[4,16,2048]{2,1,0:T(8,128)}, f32[3,256,512]{2,1,0:T(8,128)}, f32[256,128]{1,0:T(8,128)}, f32[1288,128]{1,0:T(8,...) custom-call(bf16[8,4,16,1024]{3,2,1,0:T(8,128)(2,1)} %get-tuple-elem, ...), custom_call_target="tpu_custom_call" | custom-call | tf_op jit(solution)/shard_map/finish/pallas_call | solution.py:96

commit v4 on v3

--- a/solution.py
+++ b/solution.py
@@ -33,10 +33,9 @@
 SPILL_BYTES = 4 * 2**20
 FFN_COLS = 256
 WEIGHT_CUTS = 2
-PACE = (1, 1, 1, 1, 2, 6)
-PACE_FFN = 2
-PACE_BACK = (1, 1, 2, 1)
-BUNDLES_FIRST = True
+PACE = (1, 1, 1, 0, 1, 3, 6)
+PACE_FFN = 6
+PACE_BACK = (0, 2, 2, 1, 1)
 
 
 def dot(a, b, dims=((1,), (0,)), precision=None):
@@ -105,12 +104,12 @@
     return SimpleNamespace(**dict(zip(outs, results)))
 
 
-def place_of(n, mpn):
+def place_of(n, mpn, line):
     i, j = lax.axis_index("dp"), lax.axis_index("mp")
     reps = n // mpn
     return SimpleNamespace(
         n=n, mpn=mpn, i=i, j=j, reps=reps, share=n // reps, half=n // 2,
-        m=i // reps, h=i % reps, c=i % 2, mine=i // 2, other=i + 1 - 2 * (i % 2), inside=i // reps == j,
+        m=i // reps, h=i % reps, c=i % 2, mine=i // 2, other=i + 1 - 2 * (i % 2), inside=i // reps == j, line=line,
     )
 
 
@@ -119,16 +118,19 @@
         greet(barrier, p.i, (p.j + d) % p.mpn)
     for d in range(1, p.n):
         greet(barrier, (p.i + d) % p.n, p.j)
-    for s in range(p.n):
+    for q in range(p.half):
+        s = q * 2 + p.c
+
         @pl.when(jnp.logical_not((s == p.i) & p.inside))
         def _():
             greet(barrier, s, p.m)
-    for h in range(p.reps):
+
+    for h in range(0, p.reps, 2):
         for t in range(p.mpn):
-            @pl.when(jnp.logical_not((p.j * p.reps + h == p.i) & (t == p.j)))
+            @pl.when(jnp.logical_not((p.j * p.reps + h + p.c == p.i) & (t == p.j)))
             def _():
-                greet(barrier, p.j * p.reps + h, t)
-    return p.mpn + 3 * p.n - 2 - 2 * p.inside.astype(jnp.int32)
+                greet(barrier, p.j * p.reps + h + p.c, t)
+    return p.mpn + p.n - 2 + p.half + p.reps // 2 * p.mpn - 2 * p.inside.astype(jnp.int32)
 
 
 class Exchange:
@@ -158,14 +160,146 @@
             self.copy((self.p.j + d) % self.p.mpn).wait_send()
 
 
+class LineGather(Exchange):
+    def begin(self):
+        for d in range(1, self.p.mpn):
+            def send():
+                self.copy((self.p.j + d) % self.p.mpn).start()
+
+            self.unless_far(d, send)
+
+    def unless_far(self, d, act):
+        if d == 2 or not self.p.line:
+            act()
+        else:
+            pl.when(self.p.j != (3 if d == 1 else 0))(act)
+
+    def onward(self, at):
+        s, t = (0, 3) if at == 2 else (3, 0)
+        return rcopy(self.dst(s), self.dst(s), self.ss.at[at], self.rs.at[s], self.p.i, t)
+
+    def relay(self):
+        if not self.p.line:
+            return
+        for at in (1, 2):
+            @pl.when(self.p.j == at)
+            def _():
+                self.wait(2)
+                self.onward(at).start()
+
+    def wait_all(self):
+        for d in range(1, self.p.mpn):
+            if d == 2 and self.p.line:
+                @pl.when((self.p.j == 0) | (self.p.j == 3))
+                def _():
+                    self.wait(2)
+            else:
+                self.wait(d)
+
+    def sent(self):
+        for d in range(1, self.p.mpn):
+            def done():
+                self.copy((self.p.j + d) % self.p.mpn).wait_send()
+
+            self.unless_far(d, done)
+        if self.p.line:
+            for at in (1, 2):
+                @pl.when(self.p.j == at)
+                def _():
+                    self.onward(at).wait_send()
+
+
+class LineReduce(Exchange):
+    def __init__(self, p, src, dst, ss, rs, held, hs):
+        super().__init__(p, src, dst, ss, rs)
+        self.held, self.hs = held, hs
+
+    def begin(self):
+        p = self.p
+        for d in range(1, p.mpn):
+            t = (p.j + d) % p.mpn
+            if not p.line:
+                self.copy(t).start()
+            elif d == 2:
+                @pl.when((p.j == 0) | (p.j == 3))
+                def _():
+                    self.copy(t).start()
+            else:
+                end = 3 if d == 1 else 0
+
+                @pl.when(p.j != end)
+                def _():
+                    self.copy(t).start()
+
+                @pl.when(p.j == end)
+                def _():
+                    rcopy(self.src(t), self.held, self.ss.at[t], self.hs, p.i, 2 if end == 3 else 1).start()
+
+    def send(self, t):
+        p = self.p
+        if not p.line:
+            self.copy(t).start()
+            return
+        apart = jnp.abs(t - p.j)
+        taking = (apart == 2) & ((p.j == 1) | (p.j == 2))
+
+        @pl.when(apart == 3)
+        def _():
+            rcopy(self.src(t), self.held, self.ss.at[t], self.hs, p.i, jnp.where(p.j == 0, 1, 2)).start()
+
+        @pl.when((apart < 3) & jnp.logical_not(taking))
+        def _():
+            self.copy(t).start()
+
+        pl.when(taking)(self.relay)
+
+    def relay(self):
+        p = self.p
+        if not p.line:
+            return
+
+        @pl.when((p.j == 1) | (p.j == 2))
+        def _():
+            t = (p.j + 2) % p.mpn
+            rcopy(self.held, self.held, self.ss.at[t], self.hs, p.i, t).wait_recv()
+            self.held[...] = (self.held[...].astype(f32) + self.src(t)[...].astype(f32)).astype(bf16)
+            rcopy(self.held, self.dst(p.j), self.ss.at[t], self.rs.at[p.j], p.i, t).start()
+
+    def wait_all(self):
+        for d in range(1, self.p.mpn):
+            if d == 2 or not self.p.line:
+                self.wait(d)
+            else:
+                @pl.when(self.p.j != (3 if d == 1 else 0))
+                def _():
+                    self.wait(d)
+
+
+def absent(line, j, s):
+    return line & (((j == 3) & (s == 0)) | ((j == 0) & (s == 3)))
+
+
 class Bulk:
     def __init__(self, exchanges):
-        self.exchanges, self.begun = exchanges, 0
+        self.exchanges, self.begun, self.before, self.relayed = exchanges, 0, 0, 0
+
+    def relay(self, last):
+        for exchange in self.exchanges[self.relayed : last]:
+            exchange.relay()
+        self.relayed = max(last, self.relayed)
 
     def go(self, count):
+        count = min(count, len(self.exchanges) - self.begun)
+        self.relay(self.before)
+        self.before = self.begun
         for exchange in self.exchanges[self.begun : self.begun + count]:
-            exchange.start()
+            exchange.begin()
         self.begun += count
+
+    def wait(self, first, last):
+        self.relay(last)
+        for exchange in self.exchanges[first:last]:
+            exchange.wait_all()
 
     def sent(self):
         for exchange in self.exchanges:
@@ -279,20 +413,23 @@
 
 
 class Cast:
-    def __init__(self, p, low, dst, ss, rs):
-        self.p, self.low, self.dst, self.ss, self.rs = p, low, dst, ss, rs
+    def __init__(self, p, low, dst, ss, rs, ssr):
+        self.p, self.low, self.dst, self.ss, self.rs, self.ssr = p, low, dst, ss, rs, ssr
 
     def each(self, act):
         p = self.p
-        for h in range(p.reps):
+        for h in range(0, p.reps, 2):
             for t in range(p.mpn):
-                here = (p.j * p.reps + h == p.i) & (t == p.j)
-
-                @pl.when(jnp.logical_not(here))
+                to = p.j * p.reps + h + p.c
+
+                @pl.when(jnp.logical_not((to == p.i) & (t == p.j)))
                 def _():
-                    act(rcopy(
-                        self.low, self.dst.at[p.i], self.ss.at[h * p.mpn + t], self.rs.at[p.i], p.j * p.reps + h, t
-                    ))
+                    act(rcopy(self.low, self.dst.at[p.i], self.ss.at[h // 2 * p.mpn + t], self.rs.at[p.i], to, t))
+
+    def across(self, q):
+        p = self.p
+        s = q * 2 + p.c
+        return rcopy(self.dst.at[s], self.dst.at[s], self.ssr.at[q], self.rs.at[s], p.other, p.j)
 
     def start(self):
         self.each(lambda copy: copy.start())
@@ -303,50 +440,60 @@
 
     def wait(self):
         p = self.p
-        for s in range(p.n):
+        for q in range(p.half):
+            s = q * 2 + p.c
+
             @pl.when(jnp.logical_not((s == p.i) & p.inside))
             def _():
                 rcopy(self.low, self.dst.at[s], self.ss.at[0], self.rs.at[s], s, p.m).wait_recv()
 
+            self.across(q).start()
+        for q in range(p.half):
+            s = q * 2 + 1 - p.c
+            rcopy(self.dst.at[s], self.dst.at[s], self.ssr.at[q], self.rs.at[s], p.other, p.j).wait_recv()
+
     def sent(self):
         self.each(lambda copy: copy.wait_send())
+        for q in range(self.p.half):
+            self.across(q).wait_send()
 
 
 class ToOwner:
-    def __init__(self, p, part, recv, ss, rs):
-        self.p, self.part, self.recv, self.ss, self.rs = p, part, recv, ss, rs
+    def __init__(self, p, part, mid, recv, ss, rs, ss_line, rs_line):
+        self.p, self.part, self.mid, self.recv, self.ss, self.rs = p, part, mid, recv, ss, rs
+        self.line = Exchange(p, lambda t: mid.at[t], lambda s: recv.at[s], ss_line, rs_line)
 
     def each(self, act):
         p = self.p
         for q in range(p.share):
             block = q * p.reps + p.h
 
-            @pl.when(jnp.logical_not((block == p.i) & p.inside))
+            @pl.when(block != p.i)
             def _():
-                act(rcopy(self.part.at[block], self.recv.at[p.j], self.ss.at[q], self.rs.at[p.j], block, p.m))
+                act(rcopy(self.part.at[block], self.mid.at[p.m], self.ss.at[q], self.rs.at[p.m], block, p.j))
 
     def start(self):
         self.each(lambda copy: copy.start())
-
-        @pl.when(self.p.inside)
-        def _():
-            self.recv[self.p.j] = self.part[self.p.i]
-
-    def wait(self):
+        self.mid[self.p.m] = self.part[self.p.i]
+
+    def pass_on(self):
         p = self.p
         for s in range(p.mpn):
-            @pl.when(jnp.logical_not(p.inside & (s == p.j)))
+            @pl.when(s != p.m)
             def _():
                 rcopy(
-                    self.part.at[0], self.recv.at[s], self.ss.at[0], self.rs.at[s], p.j * p.reps + p.h, s
+                    self.part.at[0], self.mid.at[s], self.ss.at[0], self.rs.at[s], s * p.reps + p.h, p.j
                 ).wait_recv()
+        self.line.start()
+        self.recv[p.j] = self.mid[p.j]
 
     def total(self):
-        self.wait()
+        self.line.wait_all()
         return sum(self.recv[s].astype(f32) for s in range(self.p.mpn))
 
     def sent(self):
         self.each(lambda copy: copy.wait_send())
+        self.line.sent()
 
 
 def perm_matrix(rows, patches, per, limit):
@@ -481,14 +628,9 @@
     for t in range(micro):
         r.part[t] = sums[t * patches : (t + 1) * patches]
         r.part_low[t] = sums[t * patches : (t + 1) * patches].astype(bf16)
-    load_grad.wait()
-    perm = perm_matrix(rows, patches, slabs, sum(own_lengths(r, j)) - i * patches)
-    r.own_grad[...] = dot(perm, r.grad_raw[...]).astype(bf16)
-    r.grad_rows_own(i, r.own_grad[...])
     pl.semaphore_wait(barrier, count)
 
     embed = Exchange(p, lambda t: r.part_low.at[t], lambda s: r.recv.at[s], r.ss1, r.rs1).start()
-    grads = PlaneGather(p, r.own_grad, lambda s: r.grad_rows.at[s], r.ssg, r.rsg, r.ssgr).start()
     halves = max(hidden // FFN_COLS, 1)
     cuts = WEIGHT_CUTS if per // WEIGHT_CUTS >= 16 else 1
     step = per // cuts
@@ -498,7 +640,7 @@
         for w in range(3):
             for k in range(cuts):
                 at = slice(k * step, (k + 1) * step)
-                pieces.append(Exchange(
+                pieces.append(LineGather(
                     p,
                     lambda t, w=w, at=at, cols=cols: r.ffn_weight.at[w, at, cols],
                     lambda s, w=w, at=at, cols=cols: land(s, w, at, cols),
@@ -507,12 +649,16 @@
                 ))
     bulk = Bulk(pieces)
     bulk.go(PACE[0])
+    load_grad.wait()
+    perm = perm_matrix(rows, patches, slabs, sum(own_lengths(r, j)) - i * patches)
+    r.own_grad[...] = dot(perm, r.grad_raw[...]).astype(bf16)
+    r.grad_rows_own(i, r.own_grad[...])
     total = r.part[j]
     for d in range(1, mpn):
         total = total + r.recv[embed.wait(d)].astype(f32)
     r.global_in[...] = total
     r.low[...] = (total * inv_rms(total) * r.norm_in_gain[...]).astype(bf16)
-    cast = Cast(p, r.low, r.normed, r.ss2, r.rs2)
+    cast = Cast(p, r.low, r.normed, r.ss2, r.rs2, r.ssc)
     cast.start()
     def columns_of(t, k):
         first = k * dim + t * (dim // n) // features * features
@@ -528,30 +674,54 @@
     piece = r.out_proj.shape[0] // n
     at_piece = lambda s: pl.ds(pl.multiple_of(s * piece, piece), piece)
     kept_ao = load(r.out_proj.at[at_piece(i)], r.ao_sorted.at[j, at_piece(i)])
+    ao_line = LineGather(
+        p, lambda t: r.out_proj.at[at_piece(i)], lambda s: r.ao_sorted.at[s, at_piece(i)], r.ssa, r.rsa
+    )
+    ao_line.begin()
     bulk.go(PACE[1])
     load_in.wait()
     load_out.wait()
     cast.wait()
-    ao_line = Exchange(
-        p, lambda t: r.out_proj.at[at_piece(i)], lambda s: r.ao_sorted.at[s, at_piece(i)], r.ssa, r.rsa
-    ).start()
+    feature = dim // n
+    blocks = max(feature, 128)
+
+    def normed_copy(q):
+        t = q * p.reps + p.h
+        return rcopy(normed_block(t), r.normed_cols.at[p.m], r.ssn.at[q], r.rsn.at[p.m], t, j)
+
+    def normed_block(t):
+        return r.normed.at[:, :, pl.ds(pl.multiple_of(t * feature // blocks * blocks, 128), blocks)]
+
+    def each_normed(act, here):
+        for q in range(p.share):
+            at_home = q * p.reps + p.h == i
+            pl.when(jnp.logical_not(at_home))(partial(act, q))
+            pl.when(at_home)(here)
+
+    def keep_normed():
+        return pltpu.make_async_copy(normed_block(i), r.normed_cols.at[p.m], r.ssn.at[p.share])
+
+    each_normed(lambda q: normed_copy(q).start(), lambda: keep_normed().start())
     bulk.go(PACE[2])
 
     part = mixer_fwd(r, own_lengths(r, p.m), r.normed[...].reshape(n * patches, dim))
     for b in range(n):
         r.mix_part[b] = part[b * patches : (b + 1) * patches].astype(bf16)
-    to_owner = ToOwner(p, r.mix_part, r.mix_recv, r.ss3, r.rs3)
+    to_owner = ToOwner(p, r.mix_part, r.mix_mid, r.mix_recv, r.ss3, r.rs3, r.sso, r.rso)
     to_owner.start()
     kept_ao.wait()
+    ao_line.relay()
+    to_owner.pass_on()
+    bulk.go(PACE[3])
     ao_line.wait_all()
     ao_block = lambda s: r.ao_sorted.at[:, at_piece(s)]
     ao_plane = PlaneGather(p, ao_block(i), ao_block, r.ssap, r.rsap, r.ssar).start()
+    grads = PlaneGather(p, r.own_grad, lambda s: r.grad_rows.at[s], r.ssg, r.rsg, r.ssgr).start()
     total = r.global_in[...] + to_owner.total()
     r.global_own[...] = total
     r.patch_all[j] = total.astype(bf16)
     patch_line = Exchange(p, lambda t: r.patch_all.at[j], lambda s: r.patch_all.at[s], r.ss4, r.rs4).start()
-    bulk.go(PACE[3])
-    grads.relay()
+    bulk.go(PACE[4])
     load_bytes.wait()
     load_qkv.wait()
     patch_line.wait_all()
@@ -588,10 +758,11 @@
         return 0
 
     lax.fori_loop(1, mpn + 1, one_micro, 0)
-    bulk.go(PACE[4])
+    bulk.go(PACE[5])
     r.heads_own[j] = r.heads[j]
     ao_plane.relay()
     ao_plane.finish()
+    grads.relay()
     for k in range(slabs):
         here = r.bytes_v[j, :, k * dim : (k + 1) * dim].astype(f32) + r.global_own[...]
         r.after[k * patches : (k + 1) * patches, :] = here
@@ -605,13 +776,20 @@
     r.ffn_own[...] = (after * inv_rms(after) * r.ffn_gain[...]).astype(bf16)
     rows_gather = PlaneGather(p, r.ffn_own, lambda s: r.ffn_rows.at[s], r.ssf, r.rsf, r.ssfr).start()
     r.ffn_rows_own(i, r.ffn_own[...])
-    bulk.go(PACE[5])
+    bulk.go(PACE[6])
 
     def settle():
         for d in range(1, n):
             s = (i + d) % n
             for k in range(positions):
                 rcopy(r.bytes_part.at[s, k], r.bytes_part.at[s, k], r.ssb.at[s, k], r.rsb.at[s, k], s, j).wait_recv()
+        for s in range(mpn):
+            @pl.when(s * p.reps + p.h != i)
+            def _():
+                rcopy(
+                    r.normed_cols.at[s], r.normed_cols.at[s], r.ssn.at[0], r.rsn.at[s], s * p.reps + p.h, j
+                ).wait_recv()
+        each_normed(lambda q: normed_copy(q).wait_send(), lambda: keep_normed().wait())
         for thing in (embed, grads, bulk, cast, ao_line, to_owner, ao_plane, patch_line, heads_line, rows_gather):
             thing.sent()
         for d in range(1, n):
@@ -622,7 +800,7 @@
 
 
 def forward_kernel(n, mpn, r):
-    p = place_of(n, mpn)
+    p = place_of(n, mpn, False)
     load = Loads(r.sem_load)
     kept = []
     r.grad_rows_own = lambda s, value: kept.append(load(r.own_grad, r.grad_rows.at[s]))
@@ -632,8 +810,7 @@
     st.rows.relay()
     st.rows.finish()
     st.bulk.go(len(st.bulk.exchanges))
-    for exchange in st.bulk.exchanges:
-        exchange.wait_all()
+    st.bulk.wait(0, len(st.bulk.exchanges))
     st.settle()
     for copy in kept + st.kept:
         copy.wait()
@@ -661,6 +838,7 @@
         ffn_rows=((n, rows, dim), bf16),
         w_all=((mpn,) + a.ffn_weight.shape, bf16),
         bytes_part=((n, positions, micro, patches, max(dim // n, 128)), bf16),
+        normed_cols=((mpn, n, patches, max(dim // n, 128)), bf16),
     )
     small = dict(
         own_grad=((rows, dim), bf16),
@@ -701,15 +879,16 @@
         recv=pltpu.VMEM((mpn, patches, dim), bf16),
         low=pltpu.VMEM((patches, dim), bf16),
         mix_part=pltpu.VMEM((n, patches, dim), bf16),
+        mix_mid=pltpu.VMEM((mpn, patches, dim), bf16),
         mix_recv=pltpu.VMEM((mpn, patches, dim), bf16),
         patch_all=pltpu.VMEM((mpn, patches, dim), bf16),
         heads=pltpu.VMEM((micro, rows, width), bf16),
         ffn_own=pltpu.VMEM((rows, dim), bf16),
-        sem_load=DMA((24,)),
-        ss1=line, rs1=line, ss2=DMA((n,)), rs2=DMA((n,)), ss3=line, rs3=line, ss4=line, rs4=line, ss5=line, rs5=line,
+        sem_load=DMA((32,)),
+        ss1=line, rs1=line, ss2=DMA((n,)), rs2=DMA((n,)), ssc=plane, ss3=line, rs3=line, sso=line, rso=line, ss4=line, rs4=line, ss5=line, rs5=line,
         ssg=plane, rsg=DMA((n,)), ssgr=plane, ssf=plane, rsf=DMA((n,)), ssfr=plane,
         ssb=DMA((n, positions)), rsb=DMA((n, positions)),
-        ssa=line, rsa=line, ssap=plane, rsap=DMA((n,)), ssar=plane,
+        ssn=DMA((mpn + 1,)), rsn=line, ssa=line, rsa=line, ssap=plane, rsap=DMA((n,)), ssar=plane,
         ssw=DMA((pieces, mpn)), rsw=DMA((pieces, mpn)),
     )
 
@@ -850,7 +1029,7 @@
         for w in range(3):
             for k in range(WEIGHT_CUTS):
                 at = slice(k * step, (k + 1) * step)
-                pieces.append(Exchange(
+                pieces.append(LineReduce(
                     p,
                     lambda t, w=w, k=k, cols=cols: grad_of(
                         w, pl.ds(pl.multiple_of(t * per + k * step, step), step), cols
@@ -858,6 +1037,8 @@
                     lambda s, w=w, at=at, cols=cols: r.g_recv.at[s, w, at, cols],
                     r.bsw.at[len(pieces)],
                     r.brw.at[len(pieces)],
+                    r.g_held.at[len(pieces)] if p.line else None,
+                    r.bsr.at[len(pieces)] if p.line else None,
                 ))
     return Bulk(pieces)
 
@@ -898,9 +1079,10 @@
     r.gains[...] = jnp.zeros(r.gains.shape, f32)
     r.gains[2:3, :] = jnp.sum(gain_rows, axis=0, keepdims=True)
     r.branch[...] = after_grad.astype(bf16)
+    up_turn = jnp.where(j < mpn // 2, mpn - 1, 1)
     up_line = Exchange(p, lambda t: r.up.at[t], lambda s: r.up_recv.at[s], r.bs1, r.br1)
     for d in range(1, mpn + 1):
-        t = (j + d) % mpn
+        t = (j + d * up_turn) % mpn
         r.up[t] = dot(r.branch[...], r.ao_sorted[t], ((1,), (1,))).astype(bf16)
         if d < mpn:
             up_line.copy(t).start()
@@ -912,14 +1094,18 @@
     mask = att_mask(rows, patches)
     pair = 2 * ATT_DIM
     lane = lax.broadcasted_iota(jnp.int32, (1, pair), 1)
-    att_line = Exchange(p, lambda t: r.att_part.at[t], lambda s: r.att_recv.at[s], r.bs2, r.br2)
+    att_line = LineReduce(
+        p, lambda t: r.att_part.at[t], lambda s: r.att_recv.at[s], r.bs2, r.br2,
+        r.att_held if p.line else None, r.bsz.at[0],
+    )
+    turn = jnp.where(j < mpn // 2, mpn - 1, 1)
 
     def one_micro(d, _):
-        m = (j + d) % mpn
+        m = (j + d * turn) % mpn
 
         @pl.when(d > 0)
         def _():
-            up_line.wait(d)
+            up_line.wait(d * turn)
 
         for c in range(width // pair):
             at = slice(c * pair, (c + 1) * pair)
@@ -946,7 +1132,7 @@
 
         @pl.when(d > 0)
         def _():
-            att_line.copy(m).start()
+            att_line.send(m)
 
         return 0
 
@@ -958,20 +1144,21 @@
             everything, r.qkv_low[w].reshape(micro * rows, width), ((0,), (0,))
         ).astype(bf16)
     sum_qkv.start()
+    sum_qkv.spread()
     for t in range(mpn):
         r.ao_part[:, t * width : (t + 1) * width] = dot(
             r.branch[...], r.heads_own[t], ((0,), (0,))
         ).astype(bf16)
     sum_ao.start()
-    sum_qkv.spread()
     perm = perm_matrix(rows, patches, slabs, sum(own_lengths(r, j)) - i * patches)
     block = (r.after[...] + sum_down.finish()).astype(bf16)
     block = dot(perm, block, ((0,), (0,))).astype(bf16)
     for t in range(mpn):
         r.block[t] = block[:, t * width : (t + 1) * width]
     total = r.att_part[j].astype(f32)
-    for d in range(1, mpn):
-        total = total + r.att_recv[att_line.wait(d)].astype(f32)
+    att_line.wait_all()
+    for s in range(mpn):
+        total = total + jnp.where((s == j) | absent(p.line, j, s), 0.0, r.att_recv[s].astype(f32))
     back, gain_rows = rms_back(r.local_in[...], r.attn_gain[...], total)
     local_grad = r.after_grad[...] + back
     global_grad = local_grad[:patches]
@@ -979,8 +1166,9 @@
         global_grad = global_grad + local_grad[k * patches : (k + 1) * patches]
     r.global_grad[...] = global_grad
     r.b_low[...] = global_grad.astype(bf16)
-    cast = Cast(p, r.b_low, r.mixer, r.bs3, r.br3)
+    cast = Cast(p, r.b_low, r.mixer, r.bs3, r.br3, r.bsc)
     cast.start()
+    sum_ao.spread()
     bulk.go(PACE_BACK[1])
     r.gains[1:2, :] = jnp.sum(gain_rows, axis=0, keepdims=True)
     share_rows = rows // mpn
@@ -990,7 +1178,6 @@
     block_line = Exchange(p, lambda t: r.block.at[t], lambda s: r.block_all.at[s], r.bs7, r.br7)
     ready("mixer")
     cast.wait()
-    sum_ao.spread()
     bulk.go(PACE_BACK[2])
 
     upstream = r.mixer[...].reshape(n * patches, dim)
@@ -998,51 +1185,50 @@
     part = dot(proj_grad, r.in_v[...])
     for b in range(n):
         r.b_part[b] = part[b * patches : (b + 1) * patches].astype(bf16)
-    to_owner = ToOwner(p, r.b_part, r.b_recv, r.bs4, r.br4)
+    to_owner = ToOwner(p, r.b_part, r.b_mid, r.b_recv, r.bs4, r.br4, r.bs9, r.br9)
     to_owner.start()
     bulk.go(PACE_BACK[3])
 
-    half_cols = dim // p.reps
-    normed_half = r.normed[:, :, pl.ds(pl.multiple_of(p.h * half_cols, half_cols), half_cols)]
-    in_grad = dot(proj_grad, normed_half.reshape(n * patches, half_cols), ((0,), (0,))).astype(bf16)
-    columns = in_grad.shape[0]
-    for e in range(p.share):
-        r.in_w_part[e, :columns, :] = in_grad[:, e * feature : (e + 1) * feature]
-        r.in_w_part[e, columns:, :] = jnp.zeros((r.in_w_part.shape[1] - columns, feature), bf16)
+    r.proj_grad[...] = proj_grad
+    size = n * patches // p.reps
+    proj_own = r.proj_grad.at[pl.ds(pl.multiple_of(p.h * size, size), size)]
+    proj_plane = PlaneGather(p, proj_own, lambda s: r.proj_all.at[s], r.bsi, r.bri, r.bsir).start()
+    keep_proj = load(proj_own, r.proj_all.at[i])
     out_grad = dot(r.mixer_low[...], upstream, ((0,), (0,))).astype(bf16)
     group_rows = GROUP_WIDTH // n
     for e in range(n):
         r.out_w_part[e] = out_grad[e * group_rows : (e + 1) * group_rows]
     bundles = (
-        (lambda e: r.in_w_part.at[e], r.in_w_recv, r.bsi, r.bri),
-        (lambda e: r.out_w_part.at[p.h * p.share + e], r.out_w_recv, r.bso, r.bro),
-        (lambda e: r.small_part, r.small_recv, r.bss, r.brs),
+        (lambda t: r.out_w_part.at[t], r.out_w_recv, r.bso, r.bro),
+        (lambda t: r.small_part, r.small_recv, r.bss, r.brs),
     )
 
     def each_bundle(act):
-        for e in range(p.share):
-            @pl.when(p.h * p.share + e != i)
+        for q in range(p.share):
+            t = q * p.reps + p.h
+
+            @pl.when(t != i)
             def _():
                 for src, dst, ss, rs in bundles:
-                    act(rcopy(src(e), dst.at[p.m], ss.at[e], rs.at[p.m], p.h * p.share + e, j))
-
-    def start_bundles():
-        each_bundle(lambda copy: copy.start())
-        for e in range(p.share):
-            @pl.when(p.h * p.share + e == i)
-            def _():
-                r.in_w_recv[p.m] = r.in_w_part[e]
-                r.out_w_recv[p.m] = r.out_w_part[i]
-                r.small_recv[p.m] = r.small_part[...]
-
-    if BUNDLES_FIRST:
-        start_bundles()
+                    act(rcopy(src(t), dst.at[p.m], ss.at[q], rs.at[p.m], t, j))
+
+    to_owner.pass_on()
+    bulk.go(PACE_BACK[4])
+    each_bundle(lambda copy: copy.start())
+    r.out_w_recv[p.m] = r.out_w_part[i]
+    r.small_recv[p.m] = r.small_part[...]
     back, gain_rows = rms_back(r.global_in[...], r.norm_in_gain[...], to_owner.total())
     r.line[j] = (r.global_grad[...] + back).astype(bf16)
     line = Exchange(p, lambda t: r.line.at[j], lambda s: r.line.at[s], r.bs5, r.br5).start()
     r.gains[0:1, :] = jnp.sum(gain_rows, axis=0, keepdims=True)
-    r.gains_line[j] = r.gains[...]
-    gains_line = Exchange(p, lambda t: r.gains, lambda s: r.gains_line.at[s], r.bsg, r.brg).start()
+    others = [(p.mine + d) % p.half for d in range(1, p.half)]
+
+    def gains_copy(q):
+        return rcopy(r.gains, r.gains_plane.at[p.mine], r.bsh.at[q], r.brh.at[p.mine], q * 2 + p.c, j)
+
+    for q in others:
+        gains_copy(q).start()
+    r.gains_plane[p.mine] = r.gains[...]
     local_line.start()
     block_line.start()
     r.local_all[j] = r.local[j]
@@ -1051,8 +1237,7 @@
     slot = lambda s: r.plane.at[s]
     plane = PlaneGather(p, r.line, slot, r.bsp, r.brp, r.bspr).start()
     keep_line = load(r.line, r.plane.at[i])
-    if not BUNDLES_FIRST:
-        start_bundles()
+    proj_plane.relay()
     r.qkv_sum[...] = sum_qkv.finish()
     ao = sum_ao.finish().astype(bf16)
     for t in range(mpn):
@@ -1060,41 +1245,38 @@
     ao_line = Exchange(p, lambda t: r.ao.at[t], lambda s: r.ao_all.at[s], r.bs8, r.br8).start()
     r.ao_all[j] = r.ao[j]
     bulk.go(len(bulk.exchanges))
-    gains_line.wait_all()
-    r.gains_plane[p.mine] = sum(r.gains_line[s] for s in range(mpn))
-
-    def gains_copy(q):
-        return rcopy(
-            r.gains_plane.at[p.mine], r.gains_plane.at[p.mine], r.bsh.at[q], r.brh.at[p.mine], q * 2 + p.c, j
-        )
-
-    others = [(p.mine + d) % p.half for d in range(1, p.half)]
     for q in others:
-        gains_copy(q).start()
-    plane.relay()
-    for q in others:
-        rcopy(r.gains_plane.at[q], r.gains_plane.at[q], r.bsh.at[q], r.brh.at[q], q * 2 + p.c, j).wait_recv()
+        rcopy(r.gains, r.gains_plane.at[q], r.bsh.at[q], r.brh.at[q], q * 2 + p.c, j).wait_recv()
     r.gains_pair[0] = sum(r.gains_plane[s] for s in range(p.half))
     pair_copy = rcopy(r.gains_pair.at[0], r.gains_pair.at[1], r.bsq.at[0], r.brq.at[0], p.other, j)
     pair_copy.start()
+    plane.relay()
+    pair_copy.wait()
+    r.gains_pair[0] = r.gains_pair[0] + r.gains_pair[1]
+    width_i = r.gains_all.shape[1]
+    first = i * feature // width_i * width_i
+    r.gains_all[...] = r.gains_pair[0, :, pl.ds(pl.multiple_of(first, 128), width_i)]
+    gains_line = Exchange(p, lambda t: r.gains_all, lambda s: r.gains_line.at[s], r.bsg, r.brg).start()
     plane.finish()
     local_line.wait_all()
     block_line.wait_all()
     ao_line.wait_all()
-    group = i // p.share
-    for t in range(mpn):
-        @pl.when(t * p.reps + group != i)
+    for s in range(mpn):
+        @pl.when(s * p.reps + p.h != i)
         def _():
             for src, dst, ss, rs in bundles:
-                rcopy(src(0), dst.at[t], ss.at[0], rs.at[t], t * p.reps + group, j).wait_recv()
-    pair_copy.wait()
-    r.gains_all[...] = r.gains_pair[0] + r.gains_pair[1]
-    for exchange in bulk.exchanges:
-        exchange.wait_all()
+                rcopy(src(0), dst.at[s], ss.at[0], rs.at[s], s * p.reps + p.h, j).wait_recv()
+    proj_plane.finish()
+    gains_line.wait_all()
+    r.gains_line[j] = r.gains_all[...]
+    gains_line.sent()
+    r.gains_all[...] = sum(r.gains_line[s] for s in range(mpn))
+    bulk.wait(0, len(bulk.exchanges))
     keep_line.wait()
+    keep_proj.wait()
     for thing in (
-        sum_in, sum_down, sum_ao, sum_qkv, bulk, up_line, att_line, cast, to_owner, line, gains_line, local_line,
-        block_line, plane, ao_line,
+        sum_in, sum_down, sum_ao, sum_qkv, bulk, up_line, att_line, cast, to_owner, line, local_line,
+        block_line, plane, proj_plane, ao_line,
     ):
         thing.sent()
     for q in others:
@@ -1103,7 +1285,7 @@
 
 
 def backward_kernel(n, mpn, spill, r):
-    p = place_of(n, mpn)
+    p = place_of(n, mpn, False)
     load = Loads(r.b_load)
 
     def read(view):
@@ -1155,16 +1337,15 @@
     width = a.qkv_weight.shape[2]
     hidden = a.ffn_weight.shape[2]
     feature = dim // n
-    padded = (a.in_weight.shape[0] + 15) // 16 * 16
     return dict(
         g_recv=((mpn, 3, dim // mpn, hidden), bf16, ANY),
         plane=((n, mpn, patches, dim), bf16, ANY),
         qkv_sum=((3, feature, width), f32, VMEM),
         ao_all=((mpn, feature, width), bf16, VMEM),
-        in_w_recv=((mpn, padded, feature), bf16, VMEM),
+        proj_all=((n, n * patches // (n // mpn), a.in_weight.shape[0]), bf16, ANY),
         out_w_recv=((mpn, GROUP_WIDTH // n, dim), bf16, VMEM),
         small_recv=((mpn, 16, CONV_CH), f32, VMEM),
-        gains_all=((8, dim), f32, VMEM),
+        gains_all=((8, max(feature, 128)), f32, VMEM),
         local_all=((mpn, rows // mpn, dim), bf16, VMEM),
         block_all=((mpn, rows, width), bf16, VMEM),
     )
@@ -1178,7 +1359,6 @@
     hidden = a.ffn_weight.shape[2]
     half, share = n // 2, mpn
     feature = dim // n
-    padded = (a.in_weight.shape[0] + 15) // 16 * 16
     pieces = max(hidden // FFN_COLS, 1) * 3 * WEIGHT_CUTS
     line, plane = DMA((mpn,)), DMA((half,))
     return dict(
@@ -1203,22 +1383,23 @@
         global_grad=pltpu.VMEM((patches, dim), f32),
         mixer=pltpu.VMEM((n, patches, dim), bf16),
         b_part=pltpu.VMEM((n, patches, dim), bf16),
+        b_mid=pltpu.VMEM((mpn, patches, dim), bf16),
         b_recv=pltpu.VMEM((mpn, patches, dim), bf16),
         line=pltpu.VMEM((mpn, patches, dim), bf16),
-        in_w_part=pltpu.VMEM((share, padded, feature), bf16),
+        proj_grad=pltpu.VMEM((n * patches, a.in_weight.shape[0]), bf16),
         out_w_part=pltpu.VMEM((n, GROUP_WIDTH // n, dim), bf16),
         small_part=pltpu.VMEM((16, CONV_CH), f32),
         gains=pltpu.VMEM((8, dim), f32),
-        gains_line=pltpu.VMEM((mpn, 8, dim), f32),
+        gains_line=pltpu.VMEM((mpn, 8, max(feature, 128)), f32),
         gains_plane=pltpu.VMEM((half, 8, dim), f32),
         gains_pair=pltpu.VMEM((2, 8, dim), f32),
         b_load=DMA((16,)),
         bs_in=DMA((4, half)), bs_down=DMA((4, half)), bs_ao=DMA((4, half)), bs_qkv=DMA((4, half)),
-        bs1=line, br1=line, bs2=line, br2=line, bs3=DMA((n,)), br3=DMA((n,)), bs4=line, br4=line,
+        bs1=line, br1=line, bs2=line, br2=line, bs3=DMA((n,)), br3=DMA((n,)), bsc=plane, bs4=line, br4=line, bs9=line, br9=line,
         bs5=line, br5=line, bs6=line, br6=line, bs7=line, br7=line, bs8=line, br8=line,
         bsp=plane, brp=DMA((n,)), bspr=plane,
         bsg=line, brg=line, bsh=plane, brh=plane, bsq=DMA((1,)), brq=DMA((1,)),
-        bsi=DMA((share,)), bri=line, bso=DMA((share,)), bro=line, bss=DMA((share,)), brs=line,
+        bsz=DMA((1,)), bsi=plane, bri=DMA((n,)), bsir=plane, bso=DMA((share,)), bro=line, bss=DMA((share,)), brs=line,
         bsw=DMA((pieces, mpn)), brw=DMA((pieces, mpn)),
     )
 
@@ -1280,8 +1461,7 @@
         last = hh == st.halves - 1
         if last:
             st.bulk.go(len(st.bulk.exchanges))
-        for exchange in st.bulk.exchanges[hh * count : (hh + 1) * count]:
-            exchange.wait_all()
+        st.bulk.wait(hh * count, (hh + 1) * count)
         if hh == 0:
             for copy in st.kept:
                 copy.wait()
@@ -1347,7 +1527,7 @@
 
 
 def layer_kernel(n, mpn, r):
-    p = place_of(n, mpn)
+    p = place_of(n, mpn, mpn == 4)
     dim = r.after.shape[1]
 
     def put_rows(ref):
@@ -1390,7 +1570,7 @@
     halves = max(hidden // FFN_COLS, 1)
     large, small = forward_results(n, mpn, a)
     rows = small["own_grad"][0][0]
-    outs = dict(bytes_part=large.pop("bytes_part") + (ANY,))
+    outs = {name: large.pop(name) + (ANY,) for name in ("bytes_part", "normed_cols")}
     outs.update(backward_results(n, mpn, a))
     large.pop("w_all")
     scratch = forward_scratch(n, mpn, a)
@@ -1399,6 +1579,9 @@
         scratch[name] = pltpu.VMEM(shape, dtype)
     scratch.update(sum_buffers(n, a, lambda shape: pltpu.VMEM(shape, bf16)))
     scratch.update(
+        g_held=pltpu.VMEM((halves * 3 * WEIGHT_CUTS, dim // mpn // WEIGHT_CUTS, hidden // halves), bf16),
+        att_held=pltpu.VMEM((rows, dim), bf16),
+        bsr=DMA((halves * 3 * WEIGHT_CUTS,)),
         w_v=pltpu.VMEM((3, dim, hidden), bf16),
         in_part=pltpu.VMEM((n, rows, dim), bf16),
         down_part=pltpu.VMEM((n, rows, dim), bf16),
@@ -1411,8 +1594,8 @@
     )
 
 
-def finish_kernel(r):
-    i = lax.axis_index("dp")
+def finish_kernel(line, r):
+    i, j = lax.axis_index("dp"), lax.axis_index("mp")
     mpn, patches, dim = r.plane.shape[1:]
     n = r.plane.shape[0]
     features = r.bytes_part.shape[-1]
@@ -1436,17 +1619,26 @@
                 + r.local_all[m, k * patches : (k + 1) * patches, :].astype(f32)
             )
     for w in range(3):
-        r.ffn_grad[w] = sum(r.g_recv[s, w].astype(f32) for s in range(mpn))
+        r.ffn_grad[w] = sum(
+            jnp.where(absent(line, j, s), 0.0, r.g_recv[s, w].astype(f32)) for s in range(mpn)
+        )
     r.ao_grad[...] = sum(r.ao_all[s].astype(f32) for s in range(mpn)).T
     columns = r.in_grad.shape[0]
-    r.in_grad[...] = sum(r.in_w_recv[s, :columns, :].astype(f32) for s in range(mpn))
+    got = dot(
+        r.proj_all[...].reshape(n * mpn * patches, columns),
+        r.normed_cols[...].reshape(n * mpn * patches, features), ((0,), (0,)),
+    )
+    if features != feature:
+        cut = features // feature
+        got = sum(jnp.where(i % cut == e, got[:, e * feature : (e + 1) * feature], 0.0) for e in range(cut))
+    r.in_grad[...] = got
     r.out_grad[...] = sum(r.out_w_recv[s].astype(f32) for s in range(mpn))
     small = sum(r.small_recv[s] for s in range(mpn))
 
     def chosen(values, size):
         whole = values.shape[1]
         at = lax.broadcasted_iota(jnp.int32, (whole, size), 0)
-        want = lax.broadcasted_iota(jnp.int32, (whole, size), 1) + i * size
+        want = lax.broadcasted_iota(jnp.int32, (whole, size), 1) + i * size % whole
         return dot(values, (at == want).astype(f32), precision=highest)
 
     conv = chosen(small, CONV_CH // n)
@@ -1468,13 +1660,13 @@
     r.block_out[...] = r.block_all[...]
 
 
-def finish(a):
+def finish(a, line):
     n, mpn, patches, dim = a.plane.shape
     positions = a.patch_weight.shape[0]
     feature = dim // n
     columns = a.in_weight.shape[0]
     names = (
-        "plane", "bytes_part", "patch_weight", "local_all", "g_recv", "ao_all", "in_w_recv", "out_w_recv",
+        "plane", "bytes_part", "patch_weight", "local_all", "g_recv", "ao_all", "proj_all", "normed_cols", "out_w_recv",
         "small_recv", "gains_all", "qkv_sum", "block_all",
     )
     row = lambda size: ((1, size), f32, VMEM)
@@ -1498,7 +1690,7 @@
         block_out=(a.block_all.shape, bf16, VMEM),
     )
     ins = {name: (getattr(a, name), VMEM) for name in names}
-    return launch("finish", finish_kernel, ins, outs, {}, plain_params())
+    return launch("finish", partial(finish_kernel, line), ins, outs, {}, plain_params())
 
 
 def body(
@@ -1544,13 +1736,14 @@
         out_grad=out_grad,
     )
     dim, hidden = ffn_gain.shape[0], ffn_weight.shape[2]
-    if n * out_grad.shape[1] * dim * 2 <= SPILL_BYTES and 2 * hidden <= dim:
+    fits = n * out_grad.shape[1] * dim * 2 <= SPILL_BYTES and 2 * hidden <= dim
+    if fits:
         a.__dict__.update(layer(n, mpn, a).__dict__)
     else:
         a.__dict__.update(forward(n, mpn, a).__dict__)
         a.down_part, a.in_part, a.w_grad = ffn(a.ffn_rows, a.grad_rows, a.w_all)
         a.__dict__.update(backward(n, mpn, a).__dict__)
-    f = finish(a)
+    f = finish(a, fits and mpn == 4)
     return (
         f.block_out,
         f.input_grad,

time: 271 us -> 227 us (0.84)
  Pallas kernels: 264 us -> 222 us
    pallas_call x2, Pallas kernels: 264 us -> 222 us  [launch(): pl.pallas_call(run, out_shape=tuple((jax.ShapeDtypeStruct(shape, dtype) f...]
where the time goes in v4:
time: 227 us; the launch traced here: 224 us
  Pallas kernels  222 us (98%)
    pallas_call x2, Pallas kernels, launch(): pl.pallas_call(run, out_shape=tuple((jax.ShapeDtypeStruct(shape, dtype) f...  222 us

profile of v4, /device:TPU:2, one launch (start us, length us, event | category | flops | bytes accessed | tf_op | source)
XLA Modules:
  0.0 223.9 jit_solution(4589179810326974672)
XLA Ops:
  0.7 0.7 broadcast_in_dim.12
  1.4 0.7 reshape_reshape.3.refs_14_
  2.0 213.0 %layer.1 = (bf16[8,2,4,16,128]{4,3,2,1,0:T(8,128)(2,1)}, bf16[4,8,16,128]{3,2,1,0:T(8,128)(2,1)}, bf16[4,3,256,512]{3,2,1,0:T(8,128)(2,1)}, bf16[8,4,16,1024]{3,...) custom-call(s32[4,3]{1,0:T(4,128)} %refs_0_.1, ...), custom_call_target="tpu_custom_call" | custom-call | tf_op jit(solution)/shard_map/layer/pallas_call | solution.py:95
  215.0 8.7 %finish.1 = (f32[2,128,1024]{2,1,0:T(8,128)}, f32[4,16,2048]{2,1,0:T(8,128)}, f32[3,256,512]{2,1,0:T(8,128)}, f32[256,128]{1,0:T(8,128)}, f32[1288,128]{1,0:T(8,...) custom-call(bf16[8,4,16,1024]{3,2,1,0:T(8,128)(2,1)} %get-tuple-elem, ...), custom_call_target="tpu_custom_call" | custom-call | tf_op jit(solution)/shard_map/finish/pallas_call | solution.py:95

commit v5 on v4

--- a/solution.py
+++ b/solution.py
@@ -33,9 +33,11 @@
 SPILL_BYTES = 4 * 2**20
 FFN_COLS = 256
 WEIGHT_CUTS = 2
-PACE = (1, 1, 1, 0, 1, 3, 6)
+PACE = (1, 1, 1, 1, 1, 2, 6, 0)
 PACE_FFN = 6
-PACE_BACK = (0, 2, 2, 1, 1)
+RELAY_WEIGHTS = ((2, 8), (3, 10))
+RELAY_GRADS = (3, 6)
+PACE_BACK = (0, 3, 3, 0, 0)
 
 
 def dot(a, b, dims=((1,), (0,)), precision=None):
@@ -284,6 +286,7 @@
         self.exchanges, self.begun, self.before, self.relayed = exchanges, 0, 0, 0
 
     def relay(self, last):
+        last = min(last, self.begun)
         for exchange in self.exchanges[self.relayed : last]:
             exchange.relay()
         self.relayed = max(last, self.relayed)
@@ -569,6 +572,11 @@
     return probs / jnp.sum(probs, axis=1, keepdims=True)
 
 
+def skip_columns(r):
+    head = lax.broadcasted_iota(jnp.int32, (1, GROUP_WIDTH), 1) // HEAD_DIM
+    return sum(jnp.where(head == h, r.skip[:, h : h + 1], 0.0) for h in range(GROUP_HEADS))
+
+
 def mixer_fwd(r, lengths, normed):
     projected = dot(normed, r.in_v[...], ((1,), (1,)))
     r.projected[...] = projected
@@ -590,7 +598,7 @@
             weights = head_decay(mask, running, running_t, h) * inner * step_t[h : h + 1, :]
             got.append(dot(weights, values))
         pieces.append(jnp.where(lane < HEAD_DIM, got[0], got[1]))
-    y = jnp.concatenate(pieces, axis=1) + r.skip[...] * act[:, :GROUP_WIDTH]
+    y = jnp.concatenate(pieces, axis=1) + skip_columns(r) * act[:, :GROUP_WIDTH]
     r.mixer_y[...] = y
     gate = projected[:, :GROUP_WIDTH]
     gated = y * (gate * jax.nn.sigmoid(gate))
@@ -610,6 +618,7 @@
 
     load_own = load(r.byte_input.at[:, :, pl.ds(pl.multiple_of(j * own_cols, 128), own_cols)], r.own)
     load_pw = [load(r.patch_weight.at[k], r.pw.at[k]) for k in range(positions)]
+    loads_small = load_small(r, load)
     load_grad = load(r.out_grad.at[j], r.grad_raw)
     load_in = load(r.in_weight, r.in_v)
     load_out = load(r.out_weight, r.out_v)
@@ -619,18 +628,6 @@
 
     barrier = pltpu.get_barrier_semaphore()
     count = greet_all(p, barrier)
-    load_own.wait()
-    sums = None
-    for k in range(positions):
-        load_pw[k].wait()
-        term = dot(r.own[:, :, k * dim : (k + 1) * dim].reshape(micro * patches, dim), r.pw[k])
-        sums = term if sums is None else sums + term
-    for t in range(micro):
-        r.part[t] = sums[t * patches : (t + 1) * patches]
-        r.part_low[t] = sums[t * patches : (t + 1) * patches].astype(bf16)
-    pl.semaphore_wait(barrier, count)
-
-    embed = Exchange(p, lambda t: r.part_low.at[t], lambda s: r.recv.at[s], r.ss1, r.rs1).start()
     halves = max(hidden // FFN_COLS, 1)
     cuts = WEIGHT_CUTS if per // WEIGHT_CUTS >= 16 else 1
     step = per // cuts
@@ -648,11 +645,25 @@
                     r.rsw.at[len(pieces)],
                 ))
     bulk = Bulk(pieces)
+    pl.semaphore_wait(barrier, count)
+    bulk.go(PACE[7])
+    load_own.wait()
+    sums = None
+    for k in range(positions):
+        load_pw[k].wait()
+        term = dot(r.own[:, :, k * dim : (k + 1) * dim].reshape(micro * patches, dim), r.pw[k])
+        sums = term if sums is None else sums + term
+    for t in range(micro):
+        r.part[t] = sums[t * patches : (t + 1) * patches]
+        r.part_low[t] = sums[t * patches : (t + 1) * patches].astype(bf16)
+    embed = Exchange(p, lambda t: r.part_low.at[t], lambda s: r.recv.at[s], r.ss1, r.rs1).start()
     bulk.go(PACE[0])
     load_grad.wait()
     perm = perm_matrix(rows, patches, slabs, sum(own_lengths(r, j)) - i * patches)
     r.own_grad[...] = dot(perm, r.grad_raw[...]).astype(bf16)
     r.grad_rows_own(i, r.own_grad[...])
+    for copy in loads_small:
+        copy.wait()
     total = r.part[j]
     for d in range(1, mpn):
         total = total + r.recv[embed.wait(d)].astype(f32)
@@ -822,8 +833,16 @@
         ins[name] = (getattr(a, name), ANY)
     ins["out_proj"] = (a.attn_out_weight, ANY)
     for name in SMALL_PARAMS:
-        ins[name] = (getattr(a, name), VMEM)
+        ins["given_" + name] = (getattr(a, name), ANY)
     return ins
+
+
+def small_scratch(a):
+    return {name: pltpu.VMEM(getattr(a, name).shape, f32) for name in SMALL_PARAMS}
+
+
+def load_small(r, load):
+    return [load(getattr(r, "given_" + name), getattr(r, name)) for name in SMALL_PARAMS]
 
 
 def forward_results(n, mpn, a):
@@ -867,6 +886,7 @@
     pieces = max(a.ffn_weight.shape[2] // FFN_COLS, 1) * 3 * WEIGHT_CUTS
     line, plane = DMA((mpn,)), DMA((half,))
     return dict(
+        **small_scratch(a),
         own=pltpu.VMEM((micro, patches, positions * dim), bf16),
         pw=pltpu.VMEM(a.patch_weight.shape, bf16),
         grad_raw=pltpu.VMEM((rows, dim), bf16),
@@ -884,7 +904,7 @@
         patch_all=pltpu.VMEM((mpn, patches, dim), bf16),
         heads=pltpu.VMEM((micro, rows, width), bf16),
         ffn_own=pltpu.VMEM((rows, dim), bf16),
-        sem_load=DMA((32,)),
+        sem_load=DMA((48,)),
         ss1=line, rs1=line, ss2=DMA((n,)), rs2=DMA((n,)), ssc=plane, ss3=line, rs3=line, sso=line, rso=line, ss4=line, rs4=line, ss5=line, rs5=line,
         ssg=plane, rsg=DMA((n,)), ssgr=plane, ssf=plane, rsf=DMA((n,)), ssfr=plane,
         ssb=DMA((n, positions)), rsb=DMA((n, positions)),
@@ -995,7 +1015,7 @@
             weights = decay * inner * step_row
             got.append(dot(weights, mine, ((0,), (0,))))
         value_pieces.append(got[0] + got[1])
-    values_grad = jnp.concatenate(value_pieces, axis=1) + r.skip[...] * y_grad
+    values_grad = jnp.concatenate(value_pieces, axis=1) + skip_columns(r) * y_grad
     inputs_grad = dot(inner_grad, outputs, ((0,), (0,)))
     outputs_grad = dot(inner_grad, inputs)
     col_grad = jnp.concatenate(col_sums, axis=0).T
@@ -1087,6 +1107,7 @@
         if d < mpn:
             up_line.copy(t).start()
     r.up_recv[j] = r.up[j]
+    bulk.relay(RELAY_GRADS[1])
     bulk.go(PACE_BACK[0])
     sum_down.spread()
     ready("qkv")
@@ -1215,11 +1236,11 @@
     to_owner.pass_on()
     bulk.go(PACE_BACK[4])
     each_bundle(lambda copy: copy.start())
-    r.out_w_recv[p.m] = r.out_w_part[i]
-    r.small_recv[p.m] = r.small_part[...]
+    keeps = [load(r.out_w_part.at[i], r.out_w_recv.at[p.m]), load(r.small_part, r.small_recv.at[p.m])]
     back, gain_rows = rms_back(r.global_in[...], r.norm_in_gain[...], to_owner.total())
     r.line[j] = (r.global_grad[...] + back).astype(bf16)
     line = Exchange(p, lambda t: r.line.at[j], lambda s: r.line.at[s], r.bs5, r.br5).start()
+    bulk.go(len(bulk.exchanges))
     r.gains[0:1, :] = jnp.sum(gain_rows, axis=0, keepdims=True)
     others = [(p.mine + d) % p.half for d in range(1, p.half)]
 
@@ -1231,20 +1252,21 @@
     r.gains_plane[p.mine] = r.gains[...]
     local_line.start()
     block_line.start()
-    r.local_all[j] = r.local[j]
-    r.block_all[j] = r.block[j]
+    keeps += [load(r.local.at[j], r.local_all.at[j]), load(r.block.at[j], r.block_all.at[j])]
     line.wait_all()
     slot = lambda s: r.plane.at[s]
     plane = PlaneGather(p, r.line, slot, r.bsp, r.brp, r.bspr).start()
     keep_line = load(r.line, r.plane.at[i])
+    bulk.relay(bulk.before)
     proj_plane.relay()
-    r.qkv_sum[...] = sum_qkv.finish()
+    r.qkv_total[...] = sum_qkv.finish()
+    keeps.append(load(r.qkv_total, r.qkv_sum))
     ao = sum_ao.finish().astype(bf16)
     for t in range(mpn):
         r.ao[t] = ao[:, t * width : (t + 1) * width]
     ao_line = Exchange(p, lambda t: r.ao.at[t], lambda s: r.ao_all.at[s], r.bs8, r.br8).start()
-    r.ao_all[j] = r.ao[j]
-    bulk.go(len(bulk.exchanges))
+    keeps.append(load(r.ao.at[j], r.ao_all.at[j]))
+    bulk.relay(len(bulk.exchanges))
     for q in others:
         rcopy(r.gains, r.gains_plane.at[q], r.bsh.at[q], r.brh.at[q], q * 2 + p.c, j).wait_recv()
     r.gains_pair[0] = sum(r.gains_plane[s] for s in range(p.half))
@@ -1253,10 +1275,10 @@
     plane.relay()
     pair_copy.wait()
     r.gains_pair[0] = r.gains_pair[0] + r.gains_pair[1]
-    width_i = r.gains_all.shape[1]
+    width_i = r.gains_mine.shape[1]
     first = i * feature // width_i * width_i
-    r.gains_all[...] = r.gains_pair[0, :, pl.ds(pl.multiple_of(first, 128), width_i)]
-    gains_line = Exchange(p, lambda t: r.gains_all, lambda s: r.gains_line.at[s], r.bsg, r.brg).start()
+    r.gains_mine[...] = r.gains_pair[0, :, pl.ds(pl.multiple_of(first, 128), width_i)]
+    gains_line = Exchange(p, lambda t: r.gains_mine, lambda s: r.gains_line.at[s], r.bsg, r.brg).start()
     plane.finish()
     local_line.wait_all()
     block_line.wait_all()
@@ -1268,12 +1290,15 @@
                 rcopy(src(0), dst.at[s], ss.at[0], rs.at[s], s * p.reps + p.h, j).wait_recv()
     proj_plane.finish()
     gains_line.wait_all()
-    r.gains_line[j] = r.gains_all[...]
+    r.gains_line[j] = r.gains_mine[...]
     gains_line.sent()
-    r.gains_all[...] = sum(r.gains_line[s] for s in range(mpn))
+    r.gains_mine[...] = sum(r.gains_line[s] for s in range(mpn))
+    keeps.append(load(r.gains_mine, r.gains_all))
     bulk.wait(0, len(bulk.exchanges))
     keep_line.wait()
     keep_proj.wait()
+    for copy in keeps:
+        copy.wait()
     for thing in (
         sum_in, sum_down, sum_ao, sum_qkv, bulk, up_line, att_line, cast, to_owner, line, local_line,
         block_line, plane, proj_plane, ao_line,
@@ -1306,6 +1331,7 @@
         copy.wait()
 
     per = r.w_grad.shape[1] // mpn
+    loads_small = load_small(r, load)
     keep_w = load(r.w_grad.at[:, pl.ds(pl.multiple_of(p.j * per, per), per)], r.g_recv.at[p.j])
     loads = dict(
         bytes=[load(r.byte_input.at[p.j], r.own_bytes)],
@@ -1319,6 +1345,8 @@
 
     barrier = pltpu.get_barrier_semaphore()
     pl.semaphore_wait(barrier, greet_all(p, barrier))
+    for copy in loads_small:
+        copy.wait()
     bulk = grad_pieces(p, r, 1, lambda w, at, cols: r.w_grad.at[w, at, cols], *r.w_grad.shape[1:])
     sum_in, sum_down = ffn_sums(p, r, read, write)
     sum_in.start()
@@ -1340,14 +1368,14 @@
     return dict(
         g_recv=((mpn, 3, dim // mpn, hidden), bf16, ANY),
         plane=((n, mpn, patches, dim), bf16, ANY),
-        qkv_sum=((3, feature, width), f32, VMEM),
-        ao_all=((mpn, feature, width), bf16, VMEM),
+        qkv_sum=((3, feature, width), f32, ANY),
+        ao_all=((mpn, feature, width), bf16, ANY),
         proj_all=((n, n * patches // (n // mpn), a.in_weight.shape[0]), bf16, ANY),
-        out_w_recv=((mpn, GROUP_WIDTH // n, dim), bf16, VMEM),
-        small_recv=((mpn, 16, CONV_CH), f32, VMEM),
-        gains_all=((8, max(feature, 128)), f32, VMEM),
-        local_all=((mpn, rows // mpn, dim), bf16, VMEM),
-        block_all=((mpn, rows, width), bf16, VMEM),
+        out_w_recv=((mpn, GROUP_WIDTH // n, dim), bf16, ANY),
+        small_recv=((mpn, 16, CONV_CH), f32, ANY),
+        gains_all=((8, max(feature, 128)), f32, ANY),
+        local_all=((mpn, rows // mpn, dim), bf16, ANY),
+        block_all=((mpn, rows, width), bf16, ANY),
     )
 
 
@@ -1389,11 +1417,13 @@
         proj_grad=pltpu.VMEM((n * patches, a.in_weight.shape[0]), bf16),
         out_w_part=pltpu.VMEM((n, GROUP_WIDTH // n, dim), bf16),
         small_part=pltpu.VMEM((16, CONV_CH), f32),
+        qkv_total=pltpu.VMEM((3, feature, width), f32),
         gains=pltpu.VMEM((8, dim), f32),
+        gains_mine=pltpu.VMEM((8, max(feature, 128)), f32),
         gains_line=pltpu.VMEM((mpn, 8, max(feature, 128)), f32),
         gains_plane=pltpu.VMEM((half, 8, dim), f32),
         gains_pair=pltpu.VMEM((2, 8, dim), f32),
-        b_load=DMA((16,)),
+        b_load=DMA((40,)),
         bs_in=DMA((4, half)), bs_down=DMA((4, half)), bs_ao=DMA((4, half)), bs_qkv=DMA((4, half)),
         bs1=line, br1=line, bs2=line, br2=line, bs3=DMA((n,)), br3=DMA((n,)), bsc=plane, bs4=line, br4=line, bs9=line, br9=line,
         bs5=line, br5=line, bs6=line, br6=line, bs7=line, br7=line, bs8=line, br8=line,
@@ -1418,13 +1448,16 @@
         ins[name] = (getattr(a, name), ANY)
     for name in ("in_part", "down_part"):
         ins[name] = (getattr(a, name), ANY if spill else VMEM)
-    for name in SMALL_PARAMS + (
+    for name in SMALL_PARAMS:
+        ins["given_" + name] = (getattr(a, name), ANY)
+    for name in (
         "after", "own_grad", "heads_own", "qkv", "attn_in", "ao_sorted", "global_in", "global_own", "normed",
         "projected", "mixer_y", "mixer_low",
     ):
         ins[name] = (getattr(a, name), VMEM)
     outs = backward_results(n, mpn, a)
     scratch = backward_scratch(n, mpn, a)
+    scratch.update(small_scratch(a))
     scratch.update(
         own_bytes=pltpu.VMEM(a.byte_input.shape[1:], bf16),
         in_v=pltpu.VMEM(a.in_weight.shape, bf16),
@@ -1490,6 +1523,10 @@
 
         def first_pass(d, _):
             q = (p.mine + half - d) % half
+            for turn, upto in RELAY_WEIGHTS:
+                @pl.when(d == turn)
+                def _():
+                    st.bulk.relay(upto)
 
             @pl.when(d > 0)
             def _():
@@ -1521,7 +1558,9 @@
         grad_of(2, everything, at)[...] = dot(grads_all(), r.hidden_low[hh], ((0,), (0,))).astype(bf16)
         mine = pl.ds(pl.multiple_of(p.j * per, per), per)
         kept += [load(grad_of(w, mine, at), r.g_recv.at[p.j, w, :, at]) for w in range(3)]
-        if not last:
+        if last:
+            bulk.relay(RELAY_GRADS[0])
+        else:
             bulk.go(PACE_FFN)
     return kept
 
@@ -1601,39 +1640,56 @@
     features = r.bytes_part.shape[-1]
     positions = r.patch_weight.shape[0]
     feature = dim // n
-    everyone = r.plane[...].reshape(n * mpn * patches, dim)
-    own = r.plane[i].reshape(mpn * patches, dim)
+    columns = r.in_grad.shape[0]
+    load = Loads(r.sems)
+    writes = []
+    into = lambda name: load(getattr(r, name), getattr(r, name + "_v"))
+    load_g = [load(r.g_recv.at[:, w], r.g_recv_v.at[w]) for w in range(3)]
+    load_patch = [into("plane"), into("bytes_part")]
+    load_in = [into("proj_all"), into("normed_cols")]
+    load_rest = [into(name) for name in ("out_w_recv", "ao_all", "small_recv", "gains_all")]
+    load_copied = [into("qkv_sum"), into("block_all")]
+    load_input = [into("local_all")] + [load(r.patch_weight.at[k], r.patch_weight_v.at[k]) for k in range(positions)]
+
+    def wait(copies):
+        for copy in copies:
+            copy.wait()
+
+    def out(name, value, at=None):
+        src, dst = getattr(r, name + "_v"), getattr(r, name)
+        if at is not None:
+            src, dst = src.at[at], dst.at[at]
+        src[...] = value
+        writes.append(load(src, dst))
+
+    cut = features // feature
+    for w in range(3):
+        load_g[w].wait()
+        out("ffn_grad", sum(
+            jnp.where(absent(line, j, s), 0.0, r.g_recv_v[w, s].astype(f32)) for s in range(mpn)
+        ), w)
+    wait(load_patch)
+    everyone = r.plane_v[...].reshape(n * mpn * patches, dim)
     for k in range(positions):
-        mine = r.bytes_part[:, k].reshape(n * mpn * patches, features)
+        mine = r.bytes_part_v[:, k].reshape(n * mpn * patches, features)
         got = dot(mine, everyone, ((0,), (0,)))
-        if features != feature:
-            cut = features // feature
-            got = sum(
-                jnp.where(i % cut == e, got[e * feature : (e + 1) * feature], 0.0) for e in range(cut)
-            )
-        r.patch_grad[k] = got
-        piece = dot(own, r.patch_weight[k], ((1,), (1,)))
-        for m in range(mpn):
-            r.input_grad[m, :, k * dim : (k + 1) * dim] = (
-                piece[m * patches : (m + 1) * patches]
-                + r.local_all[m, k * patches : (k + 1) * patches, :].astype(f32)
-            )
-    for w in range(3):
-        r.ffn_grad[w] = sum(
-            jnp.where(absent(line, j, s), 0.0, r.g_recv[s, w].astype(f32)) for s in range(mpn)
-        )
-    r.ao_grad[...] = sum(r.ao_all[s].astype(f32) for s in range(mpn)).T
-    columns = r.in_grad.shape[0]
+        if cut > 1:
+            got = sum(jnp.where(i % cut == e, got[e * feature : (e + 1) * feature], 0.0) for e in range(cut))
+        out("patch_grad", got, k)
+    wait(load_in)
     got = dot(
-        r.proj_all[...].reshape(n * mpn * patches, columns),
-        r.normed_cols[...].reshape(n * mpn * patches, features), ((0,), (0,)),
-    )
-    if features != feature:
-        cut = features // feature
+        r.proj_all_v[...].reshape(n * mpn * patches, columns),
+        r.normed_cols_v[...].reshape(n * mpn * patches, features), ((0,), (0,)),
+    )
+    if cut > 1:
         got = sum(jnp.where(i % cut == e, got[:, e * feature : (e + 1) * feature], 0.0) for e in range(cut))
-    r.in_grad[...] = got
-    r.out_grad[...] = sum(r.out_w_recv[s].astype(f32) for s in range(mpn))
-    small = sum(r.small_recv[s] for s in range(mpn))
+    out("in_grad", got)
+    wait(load_copied)
+    writes += [load(r.qkv_sum_v, r.qkv_grad), load(r.block_all_v, r.block_out)]
+    wait(load_rest)
+    out("out_grad", sum(r.out_w_recv_v[s].astype(f32) for s in range(mpn)))
+    out("ao_grad", sum(r.ao_all_v[s].astype(f32) for s in range(mpn)).T)
+    small = sum(r.small_recv_v[s] for s in range(mpn))
 
     def chosen(values, size):
         whole = values.shape[1]
@@ -1642,22 +1698,29 @@
         return dot(values, (at == want).astype(f32), precision=highest)
 
     conv = chosen(small, CONV_CH // n)
-    r.conv_w_grad[...] = conv[:CONV]
-    r.conv_b_grad[...] = conv[CONV : CONV + 1]
-    group = chosen(small[:, :GROUP_WIDTH], GROUP_WIDTH // n)
-    r.group_grad[...] = group[CONV + 1 : CONV + 2]
+    out("conv_w_grad", conv[:CONV])
+    out("conv_b_grad", conv[CONV : CONV + 1])
+    out("group_grad", chosen(small[:, :GROUP_WIDTH], GROUP_WIDTH // n)[CONV + 1 : CONV + 2])
     heads = lax.broadcasted_iota(jnp.int32, (GROUP_WIDTH, GROUP_HEADS), 0) // HEAD_DIM
     pick = heads == lax.broadcasted_iota(jnp.int32, (GROUP_WIDTH, GROUP_HEADS), 1)
-    skip = dot(small[:, :GROUP_WIDTH], pick.astype(f32), precision=highest)
-    r.skip_grad[...] = skip[CONV + 2 : CONV + 3]
-    r.step_grad[...] = small[CONV + 3 : CONV + 4, :GROUP_HEADS]
-    r.decay_grad[...] = small[CONV + 4 : CONV + 5, :GROUP_HEADS]
-    gains = chosen(r.gains_all[...], feature)
-    r.norm_in_grad[...] = gains[0:1]
-    r.attn_gain_grad[...] = gains[1:2]
-    r.ffn_gain_grad[...] = gains[2:3]
-    r.qkv_grad[...] = r.qkv_sum[...]
-    r.block_out[...] = r.block_all[...]
+    out("skip_grad", dot(small[:, :GROUP_WIDTH], pick.astype(f32), precision=highest)[CONV + 2 : CONV + 3])
+    out("step_grad", small[CONV + 3 : CONV + 4, :GROUP_HEADS])
+    out("decay_grad", small[CONV + 4 : CONV + 5, :GROUP_HEADS])
+    gains = chosen(r.gains_all_v[...], feature)
+    out("norm_in_grad", gains[0:1])
+    out("attn_gain_grad", gains[1:2])
+    out("ffn_gain_grad", gains[2:3])
+    wait(load_input)
+    own = r.plane_v[i].reshape(mpn * patches, dim)
+    for k in range(positions):
+        piece = dot(own, r.patch_weight_v[k], ((1,), (1,)))
+        for m in range(mpn):
+            r.input_grad_v[m, :, k * dim : (k + 1) * dim] = (
+                piece[m * patches : (m + 1) * patches]
+                + r.local_all_v[m, k * patches : (k + 1) * patches, :].astype(f32)
+            )
+    writes.append(load(r.input_grad_v, r.input_grad))
+    wait(writes)
 
 
 def finish(a, line):
@@ -1669,15 +1732,17 @@
         "plane", "bytes_part", "patch_weight", "local_all", "g_recv", "ao_all", "proj_all", "normed_cols", "out_w_recv",
         "small_recv", "gains_all", "qkv_sum", "block_all",
     )
-    row = lambda size: ((1, size), f32, VMEM)
-    outs = dict(
-        patch_grad=((positions, feature, dim), f32, VMEM),
-        input_grad=((mpn, patches, positions * dim), f32, VMEM),
-        ffn_grad=(a.g_recv.shape[1:], f32, VMEM),
-        ao_grad=(a.ao_all.shape[:0:-1], f32, VMEM),
-        in_grad=((columns, feature), f32, VMEM),
-        out_grad=(a.out_w_recv.shape[1:], f32, VMEM),
-        conv_w_grad=((CONV, CONV_CH // n), f32, VMEM),
+    large = dict(
+        patch_grad=((positions, feature, dim), f32),
+        input_grad=((mpn, patches, positions * dim), f32),
+        ffn_grad=(a.g_recv.shape[1:], f32),
+        ao_grad=(a.ao_all.shape[:0:-1], f32),
+        in_grad=((columns, feature), f32),
+        out_grad=(a.out_w_recv.shape[1:], f32),
+    )
+    row = lambda size: ((1, size), f32)
+    large.update(
+        conv_w_grad=((CONV, CONV_CH // n), f32),
         conv_b_grad=row(CONV_CH // n),
         group_grad=row(GROUP_WIDTH // n),
         skip_grad=row(GROUP_HEADS),
@@ -1686,11 +1751,15 @@
         norm_in_grad=row(feature),
         attn_gain_grad=row(feature),
         ffn_gain_grad=row(feature),
-        qkv_grad=(a.qkv_sum.shape, f32, VMEM),
-        block_out=(a.block_all.shape, bf16, VMEM),
-    )
-    ins = {name: (getattr(a, name), VMEM) for name in names}
-    return launch("finish", partial(finish_kernel, line), ins, outs, {}, plain_params())
+    )
+    outs = {name: value + (ANY,) for name, value in large.items()}
+    outs.update(qkv_grad=(a.qkv_sum.shape, f32, ANY), block_out=(a.block_all.shape, bf16, ANY))
+    scratch = {name + "_v": pltpu.VMEM(getattr(a, name).shape, getattr(a, name).dtype) for name in names}
+    scratch["g_recv_v"] = pltpu.VMEM((3, mpn) + a.g_recv.shape[2:], bf16)
+    scratch.update({name + "_v": pltpu.VMEM(*value) for name, value in large.items()})
+    scratch["sems"] = DMA((48,))
+    ins = {name: (getattr(a, name), ANY) for name in names}
+    return launch("finish", partial(finish_kernel, line), ins, outs, scratch, plain_params(60))
 
 
 def body(
@@ -1725,7 +1794,7 @@
         conv_bias=conv_bias,
         step_bias=step_bias,
         log_decay=log_decay,
-        skip=row(jnp.repeat(skip_gain[0], HEAD_DIM)),
+        skip=skip_gain,
         group_gain=group_gain,
         out_weight=out_weight[0],
         attn_gain=row(attn_gain),

time: 227 us -> 211 us (0.930); the launches traced: 224 us -> 211 us
  Pallas kernels: 222 us -> 210 us
    pallas_call x2, Pallas kernels: 222 us -> 210 us  [launch(): pl.pallas_call(run, out_shape=tuple((jax.ShapeDtypeStruct(shape, dtype) f...]
where the time goes in v5:
time: 211 us
  Pallas kernels  210 us (100%)
    pallas_call x2, Pallas kernels, launch(): pl.pallas_call(run, out_shape=tuple((jax.ShapeDtypeStruct(shape, dtype) f...  210 us

profile of v5, /device:TPU:2, one launch (start us, length us, event | category | flops | bytes accessed | tf_op | source)
XLA Modules:
  0.0 211.0 jit_solution(14980678432711271649)
XLA Ops:
  0.7 201.5 %layer.1 = (bf16[8,2,4,16,128]{4,3,2,1,0:T(8,128)(2,1)}, bf16[4,8,16,128]{3,2,1,0:T(8,128)(2,1)}, bf16[4,3,256,512]{3,2,1,0:T(8,128)(2,1)}, bf16[8,4,16,1024]{3,...) custom-call(s32[4,3]{1,0:T(4,128)} %refs_0_.1, ...), custom_call_target="tpu_custom_call" | custom-call | tf_op jit(solution)/shard_map/layer/pallas_call | solution.py:97
  202.2 8.6 %finish.1 = (f32[2,128,1024]{2,1,0:T(8,128)}, f32[4,16,2048]{2,1,0:T(8,128)}, f32[3,256,512]{2,1,0:T(8,128)}, f32[256,128]{1,0:T(8,128)}, f32[1288,128]{1,0:T(8,...) custom-call(bf16[8,4,16,1024]{3,2,1,0:T(8,128)(2,1)} %get-tuple-elem, ...), custom_call_target="tpu_custom_call" | custom-call | tf_op jit(solution)/shard_map/finish/pallas_call | solution.py:97

commit v6 on v5

--- a/solution.py
+++ b/solution.py
@@ -36,8 +36,8 @@
 PACE = (1, 1, 1, 1, 1, 2, 6, 0)
 PACE_FFN = 6
 RELAY_WEIGHTS = ((2, 8), (3, 10))
-RELAY_GRADS = (3, 6)
-PACE_BACK = (0, 3, 3, 0, 0)
+RELAY_GRADS = (4, 6, 6, 6, 9, 10, 11, 12)
+PACE_BACK = (0, 5, 0, 0, 1)
 
 
 def dot(a, b, dims=((1,), (0,)), precision=None):
@@ -291,9 +291,9 @@
             exchange.relay()
         self.relayed = max(last, self.relayed)
 
-    def go(self, count):
+    def go(self, count, relay=None):
         count = min(count, len(self.exchanges) - self.begun)
-        self.relay(self.before)
+        self.relay(self.before if relay is None else relay)
         self.before = self.begun
         for exchange in self.exchanges[self.begun : self.begun + count]:
             exchange.begin()
@@ -801,7 +801,7 @@
                     r.normed_cols.at[s], r.normed_cols.at[s], r.ssn.at[0], r.rsn.at[s], s * p.reps + p.h, j
                 ).wait_recv()
         each_normed(lambda q: normed_copy(q).wait_send(), lambda: keep_normed().wait())
-        for thing in (embed, grads, bulk, cast, ao_line, to_owner, ao_plane, patch_line, heads_line, rows_gather):
+        for thing in (embed, bulk, cast, ao_line, to_owner, ao_plane, patch_line, heads_line):
             thing.sent()
         for d in range(1, n):
             for k in range(positions):
@@ -823,6 +823,8 @@
     st.bulk.go(len(st.bulk.exchanges))
     st.bulk.wait(0, len(st.bulk.exchanges))
     st.settle()
+    st.rows.sent()
+    st.grads.sent()
     for copy in kept + st.kept:
         copy.wait()
 
@@ -1072,7 +1074,7 @@
     )
 
 
-def backward_steps(p, r, load, own_slab, ready, sum_in, sum_down, bulk):
+def backward_steps(p, r, load, own_slab, ready, sum_in, sum_down, bulk, pieces_of=None):
     n, mpn, i, j = p.n, p.mpn, p.i, p.j
     micro, rows, dim = r.attn_in.shape
     patches = r.global_own.shape[0]
@@ -1107,8 +1109,7 @@
         if d < mpn:
             up_line.copy(t).start()
     r.up_recv[j] = r.up[j]
-    bulk.relay(RELAY_GRADS[1])
-    bulk.go(PACE_BACK[0])
+    bulk.go(PACE_BACK[0], RELAY_GRADS[1])
     sum_down.spread()
     ready("qkv")
 
@@ -1190,7 +1191,7 @@
     cast = Cast(p, r.b_low, r.mixer, r.bs3, r.br3, r.bsc)
     cast.start()
     sum_ao.spread()
-    bulk.go(PACE_BACK[1])
+    bulk.go(PACE_BACK[1], RELAY_GRADS[2])
     r.gains[1:2, :] = jnp.sum(gain_rows, axis=0, keepdims=True)
     share_rows = rows // mpn
     for t in range(mpn):
@@ -1199,7 +1200,7 @@
     block_line = Exchange(p, lambda t: r.block.at[t], lambda s: r.block_all.at[s], r.bs7, r.br7)
     ready("mixer")
     cast.wait()
-    bulk.go(PACE_BACK[2])
+    bulk.go(PACE_BACK[2], RELAY_GRADS[3])
 
     upstream = r.mixer[...].reshape(n * patches, dim)
     proj_grad = mixer_bwd(r, p, own_lengths(r, p.m), upstream)
@@ -1208,7 +1209,7 @@
         r.b_part[b] = part[b * patches : (b + 1) * patches].astype(bf16)
     to_owner = ToOwner(p, r.b_part, r.b_mid, r.b_recv, r.bs4, r.br4, r.bs9, r.br9)
     to_owner.start()
-    bulk.go(PACE_BACK[3])
+    bulk.go(PACE_BACK[3], RELAY_GRADS[4])
 
     r.proj_grad[...] = proj_grad
     size = n * patches // p.reps
@@ -1234,13 +1235,13 @@
                     act(rcopy(src(t), dst.at[p.m], ss.at[q], rs.at[p.m], t, j))
 
     to_owner.pass_on()
-    bulk.go(PACE_BACK[4])
+    bulk.go(PACE_BACK[4], RELAY_GRADS[5])
     each_bundle(lambda copy: copy.start())
     keeps = [load(r.out_w_part.at[i], r.out_w_recv.at[p.m]), load(r.small_part, r.small_recv.at[p.m])]
     back, gain_rows = rms_back(r.global_in[...], r.norm_in_gain[...], to_owner.total())
     r.line[j] = (r.global_grad[...] + back).astype(bf16)
     line = Exchange(p, lambda t: r.line.at[j], lambda s: r.line.at[s], r.bs5, r.br5).start()
-    bulk.go(len(bulk.exchanges))
+    bulk.go(len(bulk.exchanges), RELAY_GRADS[6])
     r.gains[0:1, :] = jnp.sum(gain_rows, axis=0, keepdims=True)
     others = [(p.mine + d) % p.half for d in range(1, p.half)]
 
@@ -1257,7 +1258,7 @@
     slot = lambda s: r.plane.at[s]
     plane = PlaneGather(p, r.line, slot, r.bsp, r.brp, r.bspr).start()
     keep_line = load(r.line, r.plane.at[i])
-    bulk.relay(bulk.before)
+    bulk.relay(RELAY_GRADS[7])
     proj_plane.relay()
     r.qkv_total[...] = sum_qkv.finish()
     keeps.append(load(r.qkv_total, r.qkv_sum))
@@ -1267,6 +1268,8 @@
     ao_line = Exchange(p, lambda t: r.ao.at[t], lambda s: r.ao_all.at[s], r.bs8, r.br8).start()
     keeps.append(load(r.ao.at[j], r.ao_all.at[j]))
     bulk.relay(len(bulk.exchanges))
+    if pieces_of is not None:
+        keeps.append(pieces_of())
     for q in others:
         rcopy(r.gains, r.gains_plane.at[q], r.bsh.at[q], r.brh.at[q], q * 2 + p.c, j).wait_recv()
     r.gains_pair[0] = sum(r.gains_plane[s] for s in range(p.half))
@@ -1423,7 +1426,7 @@
         gains_line=pltpu.VMEM((mpn, 8, max(feature, 128)), f32),
         gains_plane=pltpu.VMEM((half, 8, dim), f32),
         gains_pair=pltpu.VMEM((2, 8, dim), f32),
-        b_load=DMA((40,)),
+        b_load=DMA((64,)),
         bs_in=DMA((4, half)), bs_down=DMA((4, half)), bs_ao=DMA((4, half)), bs_qkv=DMA((4, half)),
         bs1=line, br1=line, bs2=line, br2=line, bs3=DMA((n,)), br3=DMA((n,)), bsc=plane, bs4=line, br4=line, bs9=line, br9=line,
         bs5=line, br5=line, bs6=line, br6=line, bs7=line, br7=line, bs8=line, br8=line,
@@ -1597,7 +1600,27 @@
     load = Loads(r.b_load)
     kept = ffn_steps(p, r, st, load, sum_in, sum_down, bulk, grad_of)
     own_slab = lambda k: r.bytes_v[p.j, :, k * dim : (k + 1) * dim]
-    backward_steps(p, r, load, own_slab, lambda what: None, sum_in, sum_down, bulk)
+    st.rows.sent()
+    st.grads.sent()
+    rows = r.own_grad.shape[0]
+    positions = r.patch_weight.shape[0]
+    places = (r.ffn_rows, r.grad_rows)
+    again = [
+        load(r.patch_weight.at[k, s * rows : (s + 1) * rows], places[k].at[s])
+        for k in range(positions) for s in range(dim // rows)
+    ]
+
+    def pieces_of():
+        for copy in again:
+            copy.wait()
+        own = r.line[...].reshape(-1, dim)
+        for k in range(positions):
+            r.piece_v[:, k * dim : (k + 1) * dim] = dot(
+                own, places[k][: dim // rows].reshape(dim, dim), ((1,), (1,))
+            )
+        return load(r.piece_v, r.piece)
+
+    backward_steps(p, r, load, own_slab, lambda what: None, sum_in, sum_down, bulk, pieces_of)
     st.settle()
     for copy in kept:
         copy.wait()
@@ -1611,9 +1634,13 @@
     rows = small["own_grad"][0][0]
     outs = {name: large.pop(name) + (ANY,) for name in ("bytes_part", "normed_cols")}
     outs.update(backward_results(n, mpn, a))
+    patches, cols = a.byte_input.shape[1:]
+    piece = ((mpn * patches, a.patch_weight.shape[0] * dim), f32)
+    outs.update(piece=piece + (ANY,))
     large.pop("w_all")
     scratch = forward_scratch(n, mpn, a)
     scratch.update(backward_scratch(n, mpn, a))
+    scratch.update(piece_v=pltpu.VMEM(*piece))
     for name, (shape, dtype) in (*large.items(), *small.items()):
         scratch[name] = pltpu.VMEM(shape, dtype)
     scratch.update(sum_buffers(n, a, lambda shape: pltpu.VMEM(shape, bf16)))
@@ -1638,7 +1665,7 @@
     mpn, patches, dim = r.plane.shape[1:]
     n = r.plane.shape[0]
     features = r.bytes_part.shape[-1]
-    positions = r.patch_weight.shape[0]
+    positions = r.bytes_part.shape[1]
     feature = dim // n
     columns = r.in_grad.shape[0]
     load = Loads(r.sems)
@@ -1649,7 +1676,8 @@
     load_in = [into("proj_all"), into("normed_cols")]
     load_rest = [into(name) for name in ("out_w_recv", "ao_all", "small_recv", "gains_all")]
     load_copied = [into("qkv_sum"), into("block_all")]
-    load_input = [into("local_all")] + [load(r.patch_weight.at[k], r.patch_weight_v.at[k]) for k in range(positions)]
+    given = hasattr(r, "piece")
+    load_input = [into("local_all"), into("piece" if given else "patch_weight")]
 
     def wait(copies):
         for copy in copies:
@@ -1713,7 +1741,10 @@
     wait(load_input)
     own = r.plane_v[i].reshape(mpn * patches, dim)
     for k in range(positions):
-        piece = dot(own, r.patch_weight_v[k], ((1,), (1,)))
+        if given:
+            piece = r.piece_v[:, k * dim : (k + 1) * dim]
+        else:
+            piece = dot(own, r.patch_weight_v[k], ((1,), (1,)))
         for m in range(mpn):
             r.input_grad_v[m, :, k * dim : (k + 1) * dim] = (
                 piece[m * patches : (m + 1) * patches]
@@ -1729,7 +1760,7 @@
     feature = dim // n
     columns = a.in_weight.shape[0]
     names = (
-        "plane", "bytes_part", "patch_weight", "local_all", "g_recv", "ao_all", "proj_all", "normed_cols", "out_w_recv",
+        "plane", "bytes_part", "piece" if hasattr(a, "piece") else "patch_weight", "local_all", "g_recv", "ao_all", "proj_all", "normed_cols", "out_w_recv",
         "small_recv", "gains_all", "qkv_sum", "block_all",
     )
     large = dict(
@@ -1805,7 +1836,9 @@
         out_grad=out_grad,
     )
     dim, hidden = ffn_gain.shape[0], ffn_weight.shape[2]
-    fits = n * out_grad.shape[1] * dim * 2 <= SPILL_BYTES and 2 * hidden <= dim
+    rows = out_grad.shape[1]
+    fits = n * rows * dim * 2 <= SPILL_BYTES and 2 * hidden <= dim
+    fits = fits and dim % rows == 0 and dim // rows <= n and patch_weight.shape[0] <= 2
     if fits:
         a.__dict__.update(layer(n, mpn, a).__dict__)
     else:

time: 211 us -> 206 us (0.976); the launches traced: 211 us -> 204 us
  Pallas kernels: 210 us -> 203 us
    pallas_call x2, Pallas kernels: 210 us -> 203 us  [launch(): pl.pallas_call(run, out_shape=tuple((jax.ShapeDtypeStruct(shape, dtype) f...]
where the time goes in v6:
time: 206 us; the launch traced here: 204 us
  Pallas kernels  203 us (99%)
    pallas_call x2, Pallas kernels, launch(): pl.pallas_call(run, out_shape=tuple((jax.ShapeDtypeStruct(shape, dtype) f...  203 us

profile of v6, /device:TPU:2, one launch (start us, length us, event | category | flops | bytes accessed | tf_op | source)
XLA Modules:
  0.0 203.5 jit_solution(3005746934940609884)
XLA Ops:
  0.7 196.2 %layer.1 = (bf16[8,2,4,16,128]{4,3,2,1,0:T(8,128)(2,1)}, bf16[4,8,16,128]{3,2,1,0:T(8,128)(2,1)}, bf16[4,3,256,512]{3,2,1,0:T(8,128)(2,1)}, bf16[8,4,16,1024]{3,...) custom-call(s32[4,3]{1,0:T(4,128)} %refs_0_.1, ...), custom_call_target="tpu_custom_call" | custom-call | tf_op jit(solution)/shard_map/layer/pallas_call | solution.py:97
  196.9 6.5 %finish.1 = (f32[2,128,1024]{2,1,0:T(8,128)}, f32[4,16,2048]{2,1,0:T(8,128)}, f32[3,256,512]{2,1,0:T(8,128)}, f32[256,128]{1,0:T(8,128)}, f32[1288,128]{1,0:T(8,...) custom-call(bf16[8,4,16,1024]{3,2,1,0:T(8,128)(2,1)} %get-tuple-elem, ...), custom_call_target="tpu_custom_call" | custom-call | tf_op jit(solution)/shard_map/finish/pallas_call | solution.py:97

commit v7 on v6

--- a/solution.py
+++ b/solution.py
@@ -36,8 +36,8 @@
 PACE = (1, 1, 1, 1, 1, 2, 6, 0)
 PACE_FFN = 6
 RELAY_WEIGHTS = ((2, 8), (3, 10))
-RELAY_GRADS = (4, 6, 6, 6, 9, 10, 11, 12)
-PACE_BACK = (0, 5, 0, 0, 1)
+RELAY_GRADS = (4, 6, 6, 7, 9, 10, 11, 12)
+PACE_BACK = (0, 6, 0, 0, 0)
 
 
 def dot(a, b, dims=((1,), (0,)), precision=None):
@@ -773,7 +773,6 @@
     r.heads_own[j] = r.heads[j]
     ao_plane.relay()
     ao_plane.finish()
-    grads.relay()
     for k in range(slabs):
         here = r.bytes_v[j, :, k * dim : (k + 1) * dim].astype(f32) + r.global_own[...]
         r.after[k * patches : (k + 1) * patches, :] = here
@@ -787,6 +786,7 @@
     r.ffn_own[...] = (after * inv_rms(after) * r.ffn_gain[...]).astype(bf16)
     rows_gather = PlaneGather(p, r.ffn_own, lambda s: r.ffn_rows.at[s], r.ssf, r.rsf, r.ssfr).start()
     r.ffn_rows_own(i, r.ffn_own[...])
+    grads.relay()
     bulk.go(PACE[6])
 
     def settle():

time: 206 us -> 206 us (level)
  no operation moved by 1% of the time
where the time goes in v7:
time: 206 us; the launch traced here: 204 us
  Pallas kernels  203 us (99%)
    pallas_call x2, Pallas kernels, launch(): pl.pallas_call(run, out_shape=tuple((jax.ShapeDtypeStruct(shape, dtype) f...  203 us

profile of v7, /device:TPU:2, one launch (start us, length us, event | category | flops | bytes accessed | tf_op | source)
XLA Modules:
  0.0 203.9 jit_solution(2104278805305676781)
XLA Ops:
  0.7 196.6 %layer.1 = (bf16[8,2,4,16,128]{4,3,2,1,0:T(8,128)(2,1)}, bf16[4,8,16,128]{3,2,1,0:T(8,128)(2,1)}, bf16[4,3,256,512]{3,2,1,0:T(8,128)(2,1)}, bf16[8,4,16,1024]{3,...) custom-call(s32[4,3]{1,0:T(4,128)} %refs_0_.1, ...), custom_call_target="tpu_custom_call" | custom-call | tf_op jit(solution)/shard_map/layer/pallas_call | solution.py:97
  197.3 6.5 %finish.1 = (f32[2,128,1024]{2,1,0:T(8,128)}, f32[4,16,2048]{2,1,0:T(8,128)}, f32[3,256,512]{2,1,0:T(8,128)}, f32[256,128]{1,0:T(8,128)}, f32[1288,128]{1,0:T(8,...) custom-call(bf16[8,4,16,1024]{3,2,1,0:T(8,128)(2,1)} %get-tuple-elem, ...), custom_call_target="tpu_custom_call" | custom-call | tf_op jit(solution)/shard_map/finish/pallas_call | solution.py:97
